TPU v7x, 32 devices: a whole 2x2x4 slice. The times are simulated.
32 devices in a mesh: seq: 4 (over y, core), exp: 8 (over z, x).
Axes of the slice: x: 2, y: 2, z: 4, core: 2. Of those that a mesh axis runs over, the one named last changes fastest.
Arguments:
- moe_input: bfloat16 [512, 4096], P('seq', 'exp'), may hold values from -6 to 6
- out_grad: bfloat16 [512, 4096], P('seq', 'exp'), may hold values from -6 to 6
- expert_ids: int32 [512, 2], P('seq'), may hold values from 0 to 3, all different within a row; in each aligned block of 128 rows (0 to 127, 128 to 255, ...) at most 96 rows name the same one
- expert_route_weights: float32 [512, 2], P('seq'), may hold values from 0.1 to 1
- gate_weight: bfloat16 [8, 4096, 4096], P('exp', None, 'seq'), may hold values from -0.09375 to 0.09375
- up_weight: bfloat16 [8, 4096, 4096], P('exp', None, 'seq'), may hold values from -0.09375 to 0.09375
- down_weight: bfloat16 [8, 4096, 4096], P('exp', 'seq'), may hold values from -0.0625 to 0.0625
- out_weight: bfloat16 [8192, 4096], P(None, 'exp'), may hold values from -0.09375 to 0.09375
- scan_input: bfloat16 [8192, 512], P('exp', 'seq'), may hold values from -6 to 6
- delta_raw: bfloat16 [8192, 512], P('exp', 'seq'), may hold values from -1 to 512
- mixer_gate_branch: bfloat16 [8192, 512], P('exp', 'seq'), may hold values from -6 to 6
- state_input: float32 [16, 512], P(None, 'seq'), may hold values from -0.25 to 0.25
- state_output: float32 [16, 512], P(None, 'seq'), may hold values from -1.5 to 1.5
- log_rates: float32 [16, 8192], P(None, 'exp'), may hold values from -9 to -3
- skip_gain: float32 [8192], P('exp'), may hold values from 0.5 to 1.5
- block_states: float32 [4, 16, 8192], P('seq', None, 'exp'), may hold values from -6 to 6
Outputs:
- resid_grad: bfloat16 [512, 4096], P('seq', 'exp')
- probs_grad: float32 [512, 2], P('seq')
- input_grad: bfloat16 [8192, 512], P('exp', 'seq')
- delta_grad: bfloat16 [8192, 512], P('exp', 'seq')
- gate_grad: bfloat16 [8192, 512], P('exp', 'seq')
- rates_grad: float32 [16, 8192], P(None, 'exp')
- skip_grad: float32 [8192], P('exp')
Inputs may be any that keep to these rules, and one draw needn't show every extreme that they name: `expert_ids`: within each aligned block of 128 rows (one sequence shard) no expert is named by more than 96 rows, and in every draw some expert is named by exactly 96 rows of some block.
All inputs are finite; a program needn't handle non-finite values.
Results may differ from a plain program's by a relative error of at most 0.0052.
Values may be sent and summed in bfloat16 or wider, within the bound.
No kernel may reach another device: no remote copies, remote signals or barrier semaphores. Data moves between devices by JAX's collectives and lax.ppermute only.
A program may use at most 192 MiB of HBM per device.

v0:
```python
import math

import jax
import jax.numpy as jnp
from jax import lax
from jax.experimental import pallas as pl
from jax.experimental.pallas import tpu as pltpu
from jax.sharding import PartitionSpec as P

LN2 = math.log(2.0)
LANES = 128
VMEM_LIMIT = 48 * 1024 * 1024


def to_rows(rows_ref, block, group, groups):
    rows_ref[pl.ds(group, block.shape[0], stride=groups), :] = block


def forward_kernel(
    signal_ref, delta_ref, gate_ref, inmap_ref, outmap_ref, rates_ref, skip_ref, start_ref,
    kept_ref, step_rows, signal_rows, act_ref, slope_ref, weigh_ref, total_ref,
    rate_rows, state_rows, out_rows,
):
    channels, tokens = signal_ref.shape
    count = rates_ref.shape[0]
    groups = channels // LANES
    for g in range(groups):
        part = slice(g * LANES, (g + 1) * LANES)
        to_rows(signal_rows, signal_ref[part, :].astype(jnp.float32).T, g, groups)
        to_rows(step_rows, jax.nn.softplus(delta_ref[part, :].astype(jnp.float32)).T, g, groups)
        to_rows(rate_rows, jnp.exp(rates_ref[:, part]) * (-1.0 / LN2), g, groups)
        to_rows(state_rows, start_ref[:, part], g, groups)
    skip = skip_ref[...]

    def row(ref, index):
        return ref[pl.ds(pl.multiple_of(index * groups, groups), groups), :]

    def advance(t, carry):
        states, weighed, total = carry
        step = row(step_rows, t)
        signal = row(signal_rows, t)
        drive = step * signal
        out = skip * signal
        new_states, new_weighed = [], []
        for n in range(count):
            decay = jnp.exp2(step * rate_rows[n * groups : (n + 1) * groups, :])
            kept = decay * states[n]
            kept_ref[t, n] = kept
            state = kept + inmap_ref[n, t] * drive
            out = out + outmap_ref[n, t] * state
            new_weighed.append(decay * weighed[n] + step * kept)
            new_states.append(state)
        out_rows[pl.ds(pl.multiple_of(t * groups, groups), groups), :] = out
        return (tuple(new_states), tuple(new_weighed), total + step)

    zero = jnp.zeros((groups, LANES), jnp.float32)
    first = tuple(state_rows[n * groups : (n + 1) * groups, :] for n in range(count))
    unused, weighed, total = lax.fori_loop(0, tokens, advance, (first, (zero,) * count, zero))
    for n in range(count):
        weigh_ref[n] = weighed[n]
        total_ref[n] = jnp.exp2(total * rate_rows[n * groups : (n + 1) * groups, :])
    for g in range(groups):
        part = slice(g * LANES, (g + 1) * LANES)
        scan_out = out_rows[pl.ds(g, tokens, stride=groups), :].T
        gate = gate_ref[part, :].astype(jnp.float32)
        sig = jax.nn.sigmoid(gate)
        act_ref[part, :] = gate * sig
        slope_ref[part, :] = scan_out * sig * (1.0 + gate * (1.0 - sig))


def forward_call(scan_input, delta_raw, gate_branch, state_input, state_output, log_rates, skip, start):
    channels, tokens = scan_input.shape
    count = log_rates.shape[0]
    groups = channels // LANES
    f32 = jnp.float32
    vmem = pl.BlockSpec(memory_space=pltpu.VMEM)
    smem = pl.BlockSpec(memory_space=pltpu.SMEM)
    return pl.pallas_call(
        forward_kernel,
        out_shape=(
            jax.ShapeDtypeStruct((tokens, count, groups, LANES), f32),
            jax.ShapeDtypeStruct((tokens * groups, LANES), f32),
            jax.ShapeDtypeStruct((tokens * groups, LANES), f32),
            jax.ShapeDtypeStruct((channels, tokens), f32),
            jax.ShapeDtypeStruct((channels, tokens), f32),
            jax.ShapeDtypeStruct((count, groups, LANES), f32),
            jax.ShapeDtypeStruct((count, groups, LANES), f32),
        ),
        in_specs=[vmem, vmem, vmem, smem, smem, vmem, vmem, vmem],
        out_specs=(vmem,) * 7,
        scratch_shapes=[
            pltpu.VMEM((count * groups, LANES), f32),
            pltpu.VMEM((count * groups, LANES), f32),
            pltpu.VMEM((tokens * groups, LANES), f32),
        ],
        compiler_params=pltpu.CompilerParams(vmem_limit_bytes=VMEM_LIMIT),
        cost_estimate=pl.CostEstimate(
            flops=10 * channels * tokens * count,
            bytes_accessed=6 * channels * tokens * count,
            transcendentals=channels * tokens * count,
        ),
        name="scan_forward",
    )(scan_input, delta_raw, gate_branch, state_input, state_output, log_rates, skip, start)


def local_kernel(
    inner_ref, act_ref, slope_ref, step_rows, signal_rows, kept_ref, outmap_ref, rates_ref,
    gate_out, y_rows, term_ref, moment_ref, skip_out,
    rate_rows,
):
    channels, tokens = inner_ref.shape
    count = rates_ref.shape[0]
    groups = channels // LANES
    for g in range(groups):
        part = slice(g * LANES, (g + 1) * LANES)
        inner = inner_ref[part, :]
        gate_out[part, :] = (inner * slope_ref[part, :]).astype(gate_out.dtype)
        to_rows(y_rows, (inner * act_ref[part, :]).T, g, groups)
        to_rows(rate_rows, jnp.exp(rates_ref[:, part]) * (-1.0 / LN2), g, groups)

    def row(ref, index):
        return ref[pl.ds(pl.multiple_of(index * groups, groups), groups), :]

    def advance(turn, carry):
        terms, moments, skips = carry
        t = tokens - 1 - turn
        step = row(step_rows, t)
        y_grad = row(y_rows, t)
        new_terms, new_moments = [], []
        for n in range(count):
            adjoint = outmap_ref[n, t] * y_grad + terms[n]
            new_moments.append(moments[n] + adjoint * kept_ref[t, n] * step)
            new_terms.append(
                jnp.exp2(step * rate_rows[n * groups : (n + 1) * groups, :]) * adjoint
            )
        return (tuple(new_terms), tuple(new_moments), skips + y_grad * row(signal_rows, t))

    zero = jnp.zeros((groups, LANES), jnp.float32)
    terms, moments, skips = lax.fori_loop(
        0, tokens, advance, ((zero,) * count, (zero,) * count, zero)
    )
    for n in range(count):
        term_ref[n] = terms[n]
        moment_ref[n] = moments[n]
    skip_out[...] = skips


def local_call(inner, act, slope, steps, signals, kept, state_output, log_rates):
    channels, tokens = inner.shape
    count = log_rates.shape[0]
    groups = channels // LANES
    f32 = jnp.float32
    vmem = pl.BlockSpec(memory_space=pltpu.VMEM)
    smem = pl.BlockSpec(memory_space=pltpu.SMEM)
    return pl.pallas_call(
        local_kernel,
        out_shape=(
            jax.ShapeDtypeStruct((channels, tokens), jnp.bfloat16),
            jax.ShapeDtypeStruct((tokens * groups, LANES), f32),
            jax.ShapeDtypeStruct((count, groups, LANES), f32),
            jax.ShapeDtypeStruct((count, groups, LANES), f32),
            jax.ShapeDtypeStruct((groups, LANES), f32),
        ),
        in_specs=[vmem] * 6 + [smem, vmem],
        out_specs=(vmem,) * 5,
        scratch_shapes=[pltpu.VMEM((count * groups, LANES), f32)],
        compiler_params=pltpu.CompilerParams(vmem_limit_bytes=VMEM_LIMIT),
        cost_estimate=pl.CostEstimate(
            flops=8 * channels * tokens * count,
            bytes_accessed=5 * channels * tokens * count,
            transcendentals=channels * tokens * count,
        ),
        name="scan_local",
    )(inner, act, slope, steps, signals, kept, state_output, log_rates)


def adjoint_kernel(
    incoming_ref, y_rows, step_rows, signal_rows, kept_ref, delta_ref, inmap_ref, outmap_ref,
    rates_ref, skip_ref,
    input_out, delta_out,
    rate_rows, in_rows, slope_rows,
):
    channels, tokens = delta_ref.shape
    count = rates_ref.shape[0]
    groups = channels // LANES
    for g in range(groups):
        part = slice(g * LANES, (g + 1) * LANES)
        to_rows(rate_rows, jnp.exp(rates_ref[:, part]) * (-1.0 / LN2), g, groups)
    skip = skip_ref[...]

    def row(ref, index):
        return ref[pl.ds(pl.multiple_of(index * groups, groups), groups), :]

    def advance(turn, later):
        t = tokens - 1 - turn
        step = row(step_rows, t)
        y_grad = row(y_rows, t)
        pulled = jnp.zeros((groups, LANES), jnp.float32)
        decayed = jnp.zeros((groups, LANES), jnp.float32)
        new_later = []
        for n in range(count):
            rate = rate_rows[n * groups : (n + 1) * groups, :]
            adjoint = outmap_ref[n, t] * y_grad + later[n]
            pulled = pulled + inmap_ref[n, t] * adjoint
            decayed = decayed + adjoint * kept_ref[t, n] * rate
            new_later.append(jnp.exp2(step * rate) * adjoint)
        here = pl.ds(pl.multiple_of(t * groups, groups), groups)
        in_rows[here, :] = pulled * step + skip * y_grad
        slope_rows[here, :] = pulled * row(signal_rows, t) + decayed * LN2
        return tuple(new_later)

    lax.fori_loop(0, tokens, advance, tuple(incoming_ref[n] for n in range(count)))
    for g in range(groups):
        part = slice(g * LANES, (g + 1) * LANES)
        input_out[part, :] = in_rows[pl.ds(g, tokens, stride=groups), :].T.astype(input_out.dtype)
        sig = jax.nn.sigmoid(delta_ref[part, :].astype(jnp.float32))
        slope = slope_rows[pl.ds(g, tokens, stride=groups), :].T
        delta_out[part, :] = (slope * sig).astype(delta_out.dtype)


def adjoint_call(incoming, y_grads, steps, signals, kept, delta_raw, state_input, state_output, log_rates, skip):
    channels, tokens = delta_raw.shape
    count = log_rates.shape[0]
    groups = channels // LANES
    f32 = jnp.float32
    vmem = pl.BlockSpec(memory_space=pltpu.VMEM)
    smem = pl.BlockSpec(memory_space=pltpu.SMEM)
    return pl.pallas_call(
        adjoint_kernel,
        out_shape=(
            jax.ShapeDtypeStruct((channels, tokens), jnp.bfloat16),
            jax.ShapeDtypeStruct((channels, tokens), jnp.bfloat16),
        ),
        in_specs=[vmem] * 6 + [smem, smem, vmem, vmem],
        out_specs=(vmem,) * 2,
        scratch_shapes=[
            pltpu.VMEM((count * groups, LANES), f32),
            pltpu.VMEM((tokens * groups, LANES), f32),
            pltpu.VMEM((tokens * groups, LANES), f32),
        ],
        compiler_params=pltpu.CompilerParams(vmem_limit_bytes=VMEM_LIMIT),
        cost_estimate=pl.CostEstimate(
            flops=11 * channels * tokens * count,
            bytes_accessed=5 * channels * tokens * count,
            transcendentals=channels * tokens * count,
        ),
        name="scan_adjoint",
    )(incoming, y_grads, steps, signals, kept, delta_raw, state_input, state_output, log_rates, skip)


def later_term(term, block_decay):
    count = lax.axis_size("seq")
    ahead = []
    for distance in range(1, count):
        pairs = [(source, source - distance) for source in range(distance, count)]
        ahead.append(
            (lax.ppermute(term, "seq", pairs), lax.ppermute(block_decay, "seq", pairs))
        )
    incoming = jnp.zeros_like(term)
    for far_term, far_decay in reversed(ahead):
        incoming = far_term + far_decay * incoming
    return incoming


def expert_backward(rows_in, rows_grad, gate_slice, up_slice, down_slice):
    contract = (((1,), (1,)), ((), ()))
    gate_pre = jnp.dot(rows_in, gate_slice, preferred_element_type=jnp.float32)
    up_pre = jnp.dot(rows_in, up_slice, preferred_element_type=jnp.float32)
    hidden_grad = lax.dot_general(
        rows_grad, down_slice, contract, preferred_element_type=jnp.float32
    )
    gate_sig = jax.nn.sigmoid(gate_pre)
    silu_gate = gate_pre * gate_sig
    probes = jnp.sum(silu_gate * up_pre * hidden_grad, axis=1)
    grad_up = (hidden_grad * silu_gate).astype(jnp.bfloat16)
    grad_gate = (hidden_grad * up_pre * gate_sig * (1.0 + gate_pre * (1.0 - gate_sig))).astype(
        jnp.bfloat16
    )
    partial_rows = lax.dot_general(
        grad_gate, gate_slice, contract, preferred_element_type=jnp.float32
    )
    partial_rows = partial_rows + lax.dot_general(
        grad_up, up_slice, contract, preferred_element_type=jnp.float32
    )
    return (partial_rows, probes)


def local(
    moe_input,
    out_grad,
    expert_ids,
    expert_route_weights,
    gate_weight,
    up_weight,
    down_weight,
    out_weight,
    scan_input,
    delta_raw,
    mixer_gate_branch,
    state_input,
    state_output,
    log_rates,
    skip_gain,
    block_states,
):
    seq_count = lax.axis_size("seq")
    exp_count = lax.axis_size("exp")
    row_count, feat_cols = moe_input.shape
    top_count = expert_ids.shape[1]
    experts = exp_count // 2
    capacity = 3 * top_count * row_count // (2 * experts)
    channels = scan_input.shape[0]
    groups = channels // LANES
    states = log_rates.shape[0]
    skip_rows = skip_gain.reshape(groups, LANES)
    kept, steps, signals, act, slope, weighed, block_decay = forward_call(
        scan_input, delta_raw, mixer_gate_branch, state_input, state_output, log_rates, skip_rows,
        block_states[0],
    )
    flat_ids = expert_ids.reshape(row_count * top_count)
    matches = (flat_ids[:, None] == jnp.arange(experts, dtype=jnp.int32)[None, :]).astype(jnp.int32)
    slot_ids = jnp.sum((jnp.cumsum(matches, axis=0) - matches) * matches, axis=1)
    owners = jnp.arange(row_count * top_count, dtype=jnp.int32) // top_count
    slot_table = jnp.zeros((capacity, experts), jnp.int32).at[slot_ids, flat_ids].set(owners)
    send_in = moe_input[slot_table]
    send_grad = out_grad[slot_table]

    def widen_pair(block):
        wide = jnp.broadcast_to(block[:, :, None, :], (capacity, experts, 2, feat_cols))
        return wide.reshape(capacity, exp_count, feat_cols)

    got_in, got_grad = (
        lax.all_to_all(widen_pair(send_in), "exp", split_axis=1, concat_axis=1, tiled=True),
        lax.all_to_all(widen_pair(send_grad), "exp", split_axis=1, concat_axis=1, tiled=True),
    )
    rows_in, rows_grad = (
        lax.all_gather(got_in.reshape(capacity, exp_count * feat_cols), "seq", axis=0, tiled=True),
        lax.all_gather(
            got_grad.reshape(capacity, exp_count * feat_cols), "seq", axis=0, tiled=True
        ),
    )
    partial_rows, probes = expert_backward(
        rows_in, rows_grad, gate_weight[0], up_weight[0], down_weight[0]
    )
    sum_part, sum_probe = (
        lax.psum_scatter(partial_rows, "seq", scatter_dimension=0, tiled=True),
        lax.psum_scatter(probes, "seq", scatter_dimension=0, tiled=True),
    )
    probe_wide = jnp.broadcast_to(sum_probe[:, None, None], (capacity, exp_count, 1))
    back_part, back_probe = (
        lax.all_to_all(
            sum_part.reshape(capacity, exp_count, feat_cols),
            "exp",
            split_axis=1,
            concat_axis=1,
            tiled=True,
        ),
        lax.all_to_all(probe_wide, "exp", split_axis=1, concat_axis=1, tiled=True),
    )
    route_sum = jnp.sum(back_part.reshape(capacity, experts, 2, feat_cols), axis=2)
    probe_sum = jnp.sum(back_probe.reshape(capacity, experts, 2), axis=2)
    route_grad = route_sum[slot_ids, flat_ids].reshape(row_count, top_count, feat_cols)
    probs_grad = probe_sum[slot_ids, flat_ids].reshape(row_count, top_count)
    mixture = jnp.sum(expert_route_weights[:, :, None] * route_grad, axis=1)
    resid_grad = (out_grad.astype(jnp.float32) + mixture).astype(jnp.bfloat16)
    block = out_weight
    inner_grad = lax.psum_scatter(
        lax.dot_general(
            block, resid_grad, (((1,), (1,)), ((), ())), preferred_element_type=jnp.float32
        ),
        "exp",
        scatter_dimension=0,
        tiled=True,
    )
    gate_grad, y_grads, term, moment, skip_part = local_call(
        inner_grad, act, slope, steps, signals, kept, state_output, log_rates
    )
    incoming = later_term(term, block_decay)
    input_grad, delta_grad = adjoint_call(
        incoming, y_grads, steps, signals, kept, delta_raw, state_input, state_output, log_rates,
        skip_rows,
    )
    moment = moment + weighed * incoming
    rate_part = -jnp.exp(log_rates) * moment.reshape(states, channels)
    rates_grad, skip_grad = lax.psum((rate_part, skip_part.reshape(channels)), "seq")
    return (resid_grad, probs_grad, input_grad, delta_grad, gate_grad, rates_grad, skip_grad)


def solution(mesh):
    in_specs = (
        P("seq", "exp"),
        P("seq", "exp"),
        P("seq", None),
        P("seq", None),
        P("exp", None, "seq"),
        P("exp", None, "seq"),
        P("exp", "seq", None),
        P(None, "exp"),
        P("exp", "seq"),
        P("exp", "seq"),
        P("exp", "seq"),
        P(None, "seq"),
        P(None, "seq"),
        P(None, "exp"),
        P("exp"),
        P("seq", None, "exp"),
    )
    out_specs = (
        P("seq", "exp"),
        P("seq", None),
        P("exp", "seq"),
        P("exp", "seq"),
        P("exp", "seq"),
        P(None, "exp"),
        P("exp"),
    )
    return jax.shard_map(local, mesh=mesh, in_specs=in_specs, out_specs=out_specs, check_vma=False)
```

profile of v0, /device:TPU:0, one launch (start us, length us, event | category | flops | bytes accessed | tf_op | source)
XLA Modules:
  0.0 394.9 jit_solution(2999127977745404477)
XLA Ops:
  10.2 11.1 %scatter_fusion = s32[96,4]{0,1:T(4,128)S(1)} fusion(s32[96,4]{0,1:T(4,128)S(1)} %broadcast.74, s32[256]{0:T(256)S(1)} %bitcast.72, s32[256]{0:T(256)S(1)} %and_select_fusion), kind=kCustom, calls=%fused_computation.4 | custom fusion | bytes 5120 | tf_op jit(solution)/shard_map/scatter | solution.py:324
  21.5 2.1 gather_fusion.1
  23.8 27.2 %all_to_all.20 = bf16[96,8,512]{2,0,1:T(8,128)(2,1)S(1)} all-to-all(bf16[96,8,512]{2,0,1:T(8,128)(2,1)S(1)} %bitcast.75), channel_id=1, replica_groups=mesh['seq'=4,'exp'=8] {'exp'}, dimensions={1} | all-to-all | bytes 1572864 | tf_op jit(solution)/shard_map/all_to_all | solution.py:333
  52.1 2.1 gather_fusion
  54.4 23.2 %all_to_all.21 = bf16[96,8,512]{2,0,1:T(8,128)(2,1)S(1)} all-to-all(bf16[96,8,512]{2,0,1:T(8,128)(2,1)S(1)} %bitcast.77), channel_id=1, replica_groups=mesh['seq'=4,'exp'=8] {'exp'}, dimensions={1} | all-to-all | bytes 1572864 | tf_op jit(solution)/shard_map/all_to_all | solution.py:334
  79.8 7.8 %fusion.2 = f32[384,1024]{1,0:T(8,128)S(1)} fusion(bf16[384,4096]{1,0:T(8,128)(2,1)} %all-gather.5.cloned.1.call-done, bf16[1,4096,1024]{2,1,0:T(8,128)(2,1)} %param.20), kind=kOutput, calls=%fused_computation.8 | convolution fusion | flops 3221225472 | bytes 13107200 | tf_op jit(solution)/shard_map/dot_general | solution.py:267
  87.6 6.3 %fusion.6 = f32[384,1024]{1,0:T(8,128)S(1)} fusion(bf16[384,4096]{1,0:T(8,128)(2,1)S(1)} %copy-done.14, bf16[1,4096,1024]{2,1,0:T(8,128)(2,1)} %param.21), kind=kOutput, calls=%fused_computation.12 | convolution fusion | flops 3221225472 | bytes 13107200 | tf_op jit(solution)/shard_map/dot_general | solution.py:268
  93.9 16.0 %all-gather.3.cloned.1.call-done = bf16[384,4096]{1,0:T(8,128)(2,1)} async-done(((bf16[96,4096]{1,0:T(8,128)(2,1)}), bf16[384,4096]{1,0:T(8,128)(2,1)}) %all-gather.3.cloned.1.call-update) | async-done | bytes 3145744 | tf_op jit(solution)/shard_map/all_gather | solution.py:338
  109.9 7.2 %multiply_reduce_fusion = (f32[384]{0:T(512)S(1)}, f32[384,1024]{1,0:T(8,128)S(1)}) fusion(f32[384,1024]{1,0:T(8,128)S(1)} %fusion.6, f32[384,1024]{1,0:T(8,128)S(1)} %fusion.2, bf16[384,4096]{1,0:T(8,128)(2,1)} %all-gather.3.cloned.1.call-done, bf16[1,1024,4096]{2,1,0:T(8,128)(2,1)} %param.22), kind=kOutput, calls=%fused_computation.19 | convolution fusion | flops 3223977472 | bytes 16254464 | tf_op jit(solution)/shard_map/dot_general | solution.py:269
  117.0 6.8 %fusion = f32[384,4096]{1,0:T(8,128)S(1)} fusion(bf16[1,4096,1024]{2,1,0:T(8,128)(2,1)} %param.20, f32[384,1024]{1,0:T(8,128)S(1)} %fusion.2, f32[384,1024]{1,0:T(8,128)S(1)} %get-tuple-element.70, f32[384,1024]{1,0:T(8,128)S(1)} %fusion.6), kind=kOutput, calls=%fused_computation.6 | convolution fusion | flops 3225157632 | bytes 19398656 | tf_op jit(solution)/shard_map/dot_general | solution.py:279
  123.9 11.0 %fusion.10 = f32[384,4096]{1,0:T(8,128)} fusion(f32[384,4096]{1,0:T(8,128)S(1)} %fusion, bf16[1,4096,1024]{2,1,0:T(8,128)(2,1)} %param.21, f32[384,1024]{1,0:T(8,128)S(1)} %get-tuple-element.70, f32[384,1024]{1,0:T(8,128)S(1)} %fusion.2), kind=kOutput, calls=%fused_computation.16 | convolution fusion | flops 3225157632 | bytes 24117248 | tf_op jit(solution)/shard_map/dot_general | solution.py:282
  134.9 58.5 %reduce-scatter.3.cloned.1.call-done = f32[96,4096]{1,0:T(8,128)} async-done(((f32[384,4096]{1,0:T(8,128)}), f32[96,4096]{1,0:T(8,128)}) %reduce-scatter.3.cloned.1.call-update) | async-done | bytes 1572880 | tf_op jit(solution)/shard_map/reduce_scatter | solution.py:346
  193.5 2.7 copy.87
  196.2 5.6 %all-to-all-start.2 = ((f32[96,8,512]{2,0,1:T(8,128)}), f32[96,8,512]{2,0,1:T(8,128)S(1)}, u32[]{:S(2)}, u32[]{:S(2)}) async-start(f32[96,8,512]{2,0,1:T(8,128)} %bitcast.65), calls=%async_computation.3 | async-start | bytes 3145728 | tf_op jit(solution)/shard_map/all_to_all | solution.py:351
  202.0 36.8 %all-to-all-done.2 = f32[96,8,512]{2,0,1:T(8,128)S(1)} async-done(((f32[96,8,512]{2,0,1:T(8,128)}), f32[96,8,512]{2,0,1:T(8,128)S(1)}, u32[]{:S(2)}, u32[]{:S(2)}) %all-to-all-start.2) | async-done | bytes 1572896 | tf_op jit(solution)/shard_map/all_to_all | solution.py:351
  239.5 1.9 gather_fusion.2
  242.5 7.7 %convolution_bitcast_fusion = f32[8192,128]{1,0:T(8,128)} fusion(bf16[128,512]{1,0:T(8,128)(2,1)S(1)} %add_convert_fusion, bf16[8192,512]{1,0:T(8,128)(2,1)} %param.23), kind=kOutput, calls=%fused_computation.5 | convolution fusion | flops 1073741824 | bytes 12713984 | tf_op jit(solution)/shard_map/dot_general | solution.py:368
  251.4 9.6 %scan_forward.1 = (f32[128,16,8,128]{3,2,1,0:T(8,128)}, f32[1024,128]{1,0:T(8,128)S(1)}, f32[1024,128]{1,0:T(8,128)S(1)}, f32[1024,128]{1,0:T(8,128)S(1)}, f32[1...) custom-call(bf16[1024,128]{1,0:T(8,128)(2,1)S(1)} %copy-done.8, ...), custom_call_target="tpu_custom_call" | custom-call | flops 20971520 | bytes 12582912 | tf_op jit(solution)/shard_map/scan_forward/pallas_call | solution.py:78
  261.0 1.3 collective-permute-start.1
  262.3 1.3 collective-permute-start.3
  263.6 1.3 collective-permute-start.5
  264.9 71.7 %reduce-scatter.5.cloned.1.call-done.inner_ref = f32[1024,128]{1,0:T(8,128)} async-done(((f32[8192,128]{1,0:T(8,128)}), f32[1024,128]{1,0:T(8,128)}) %reduce-scatter.5.cloned.1.call-update) | async-done | bytes 524304 | tf_op jit(solution)/shard_map/reduce_scatter | solution.py:367
  337.7 8.7 %scan_local.1 = (bf16[1024,128]{1,0:T(8,128)(2,1)}, f32[1024,128]{1,0:T(8,128)S(1)}, f32[16,8,128]{2,1,0:T(8,128)S(1)}, f32[16,8,128]{2,1,0:T(8,128)S(1)}, f32[8,128]{1,0:T(8,128)S(1)}) custom-call(f32[1024,128]{1,0:T(8,128)S(1)} %copy-done.3, f32[1024,128]{1,0:T(8,128)S(1)} %get-tuple-element.21.act_ref, f32[1024,128]{1,0:T(8,128)S(1)} %get-tuple-element.22.slope_ref, ...), custom_call_target="tpu_custom_call" | custom-call | flops 16777216 | bytes 10485760 | tf_op jit(solution)/shard_map/scan_local/pallas_call | solution.py:155
  346.4 1.3 collective-permute-start
  347.7 1.3 collective-permute-start.2
  349.0 1.3 collective-permute-start.4
  350.3 4.1 %collective-permute-done.2 = f32[16,8,128]{2,1,0:T(8,128)S(1)} collective-permute-done((f32[16,8,128]{2,1,0:T(8,128)S(1)}, f32[16,8,128]{2,1,0:T(8,128)S(1)}, u32[]{:S(2)}, u32[]{:S(2)}) %collective-permute-start.2) | collective-permute-done | bytes 65568 | tf_op jit(solution)/shard_map/ppermute | solution.py:257
  357.3 6.4 %all-reduce.1 = (f32[384]{0:T(512)S(1)}, f32[1024]{0:T(1024)}) all-reduce(f32[384]{0:T(512)S(1)} %get-tuple-element.69, f32[1024]{0:T(1024)S(1)} %bitcast.68), channel_id=3, replica_groups=mesh['seq'=4,'exp'=8] {'seq'}, use_global_device_ids=true, to_apply=%region_8.9.clone | all-reduce | flops 1408 | bytes 11264
  363.8 10.7 %all_to_all.22 = f32[96,8,1]{0,2,1:T(1,128)S(1)} all-to-all(f32[96,8,1]{0,2,1:T(1,128)S(1)} %broadcast_in_dim.13), channel_id=1, replica_groups=mesh['seq'=4,'exp'=8] {'exp'}, dimensions={1} | all-to-all | bytes 6144 | tf_op jit(solution)/shard_map/all_to_all | solution.py:358
  374.5 2.4 gather_fusion.3
  377.7 9.2 %scan_adjoint.1 = (bf16[1024,128]{1,0:T(8,128)(2,1)}, bf16[1024,128]{1,0:T(8,128)(2,1)}) custom-call(f32[16,8,128]{2,1,0:T(8,128)S(1)} %get-tuple-element.66.incoming_ref, f32[1024,128]{1,0:T(8,128)S(1)} %get-tuple-element.28.y_rows, f32[1024,128]{1,0:T(8,128)S(1)} %get-tuple-element.23.step_rows, f32[1024,128]{1,0:T(8,128)S(1)} %get-tuple-element.24.signal_rows, ...), custom_call_target="tpu_custom_call" | custom-call | flops 23068672 | bytes 10485760 | tf_op jit(solution)/shard_map/scan_adjoint/pallas_call | solution.py:228
  386.9 1.5 copy.90
  (91 shorter events, 14.0 us)
Async XLA Ops:
  7.2 14.3 %copy-start = (bf16[128,512]{1,0:T(8,128)(2,1)S(1)}, bf16[128,512]{1,0:T(8,128)(2,1)}, u32[]{:S(2)}) copy-start(bf16[128,512]{1,0:T(8,128)(2,1)} %param.16) | copy-start | bytes 393220
  7.2 72.6 %all-gather.5.cloned.1.call-start = ((), (), s32[]{:S(2)}) async-start(), calls=%async_computation.7 | async-start | bytes 3932160 | tf_op jit(solution)/shard_map/all_gather | solution.py:337
  51.0 1.1 copy-start.11
  52.0 57.9 %all-gather.3.cloned.1.call-start = ((), (), s32[]{:S(2)}) async-start(), calls=%async_computation.6 | async-start | bytes 3932160 | tf_op jit(solution)/shard_map/all_gather | solution.py:338
  78.6 114.9 %reduce-scatter.3.cloned.1.call-start = ((), (), s32[]{:S(2)}) async-start(), calls=%async_computation.8 | async-start | bytes 7864320 | tf_op jit(solution)/shard_map/reduce_scatter | solution.py:346
  79.7 7.8 %copy-start.14 = (bf16[384,4096]{1,0:T(8,128)(2,1)S(1)}, bf16[384,4096]{1,0:T(8,128)(2,1)}, u32[]{:S(2)}) copy-start(bf16[384,4096]{1,0:T(8,128)(2,1)} %all-gather.5.cloned.1.call-done) | copy-start | bytes 9437188
  196.2 5.7 %copy-start.13 = (f32[128,2]{0,1:T(2,128)S(1)}, f32[128,2]{0,1:T(2,128)}, u32[]{:S(2)}) copy-start(f32[128,2]{0,1:T(2,128)} %param.19) | copy-start | bytes 3076
  196.2 42.6 %all-to-all-start.2 = ((f32[96,8,512]{2,0,1:T(8,128)}), f32[96,8,512]{2,0,1:T(8,128)S(1)}, u32[]{:S(2)}, u32[]{:S(2)}) async-start(f32[96,8,512]{2,0,1:T(8,128)} %bitcast.65), calls=%async_computation.3 | async-start | bytes 3145728 | tf_op jit(solution)/shard_map/all_to_all | solution.py:351
  201.8 134.8 %reduce-scatter.5.cloned.1.call-start = ((), (), s32[]{:S(2)}) async-start(), calls=%async_computation.9 | async-start | bytes 4718592 | tf_op jit(solution)/shard_map/reduce_scatter | solution.py:367
  242.5 7.8 %copy-start.12 = (bf16[128,512]{1,0:T(8,128)(2,1)}, bf16[128,512]{1,0:T(8,128)(2,1)S(1)}, u32[]{:S(2)}) copy-start(bf16[128,512]{1,0:T(8,128)(2,1)S(1)} %add_convert_fusion) | copy-start | bytes 393220
  250.2 0.8 copy-start.2
  250.2 1.0 copy-start.4
  250.2 1.0 copy-start.5
  250.2 1.0 copy-start.6
  250.2 1.0 copy-start.7
  250.2 1.1 copy-start.8
  250.3 1.1 copy-start.9
  250.3 1.1 copy-start.10
  250.3 136.6 %all-reduce.4.cloned.1.call-start = ((), (), s32[]{:S(2)}) async-start(), calls=%async_computation.10 | async-start | bytes 131072 | tf_op jit(solution)/shard_map/psum | solution.py:385
  261.0 88.0 %collective-permute-start.1 = (f32[16,8,128]{2,1,0:T(8,128)S(1)}, f32[16,8,128]{2,1,0:T(8,128)S(1)}, u32[]{:S(2)}, u32[]{:S(2)}) collective-permute-start(f32[16,8,128]{2,1,0:T(8,128)S(1)} %get-tuple-element.27), channel_id=1, source_target_pairs={{8,0},{16,8},{24,16},{9,1},{17,9},{25,17},{10,2},{18,10},{26,18},{... | collective-permute-start | bytes 196616 | tf_op jit(solution)/shard_map/ppermute | solution.py:257
  262.3 88.0 %collective-permute-start.3 = (f32[16,8,128]{2,1,0:T(8,128)S(1)}, f32[16,8,128]{2,1,0:T(8,128)S(1)}, u32[]{:S(2)}, u32[]{:S(2)}) collective-permute-start(f32[16,8,128]{2,1,0:T(8,128)S(1)} %get-tuple-element.27), channel_id=1, source_target_pairs={{16,0},{24,8},{17,1},{25,9},{18,2},{26,10},{19,3},{27,11},{20,4},{... | collective-permute-start | bytes 196616 | tf_op jit(solution)/shard_map/ppermute | solution.py:257
  263.6 86.7 %collective-permute-start.5 = (f32[16,8,128]{2,1,0:T(8,128)S(1)}, f32[16,8,128]{2,1,0:T(8,128)S(1)}, u32[]{:S(2)}, u32[]{:S(2)}) collective-permute-start(f32[16,8,128]{2,1,0:T(8,128)S(1)} %get-tuple-element.27), channel_id=1, source_target_pairs={{24,0},{25,1},{26,2},{27,3},{28,4},{29,5},{30,6},{31,7}} | collective-permute-start | bytes 196616 | tf_op jit(solution)/shard_map/ppermute | solution.py:257
  336.7 1.0 copy-start.3
  337.7 18.3 %copy-start.15 = (u32[32]{0:T(128)S(1)}, u32[32]{0:T(128)}, u32[]{:S(2)}) copy-start(u32[32]{0:T(128)} %constant.82) | copy-start | bytes 388
  346.4 3.9 collective-permute-start
  347.7 6.7 %collective-permute-start.2 = (f32[16,8,128]{2,1,0:T(8,128)S(1)}, f32[16,8,128]{2,1,0:T(8,128)S(1)}, u32[]{:S(2)}, u32[]{:S(2)}) collective-permute-start(f32[16,8,128]{2,1,0:T(8,128)S(1)} %get-tuple-element.26), channel_id=1, source_target_pairs={{16,0},{24,8},{17,1},{25,9},{18,2},{26,10},{19,3},{27,11},{20,4},{... | collective-permute-start | bytes 196616 | tf_op jit(solution)/shard_map/ppermute | solution.py:257
  349.0 6.3 %collective-permute-start.4 = (f32[16,8,128]{2,1,0:T(8,128)S(1)}, f32[16,8,128]{2,1,0:T(8,128)S(1)}, u32[]{:S(2)}, u32[]{:S(2)}) collective-permute-start(f32[16,8,128]{2,1,0:T(8,128)S(1)} %get-tuple-element.26), channel_id=1, source_target_pairs={{24,0},{25,1},{26,2},{27,3},{28,4},{29,5},{30,6},{31,7}} | collective-permute-start | bytes 196616 | tf_op jit(solution)/shard_map/ppermute | solution.py:257
  377.7 10.7 %copy-start.1 = (bf16[128,512]{1,0:T(8,128)(2,1)S(1)}, bf16[128,512]{1,0:T(8,128)(2,1)}, u32[]{:S(2)}) copy-start(bf16[128,512]{1,0:T(8,128)(2,1)} %param.16) | copy-start | bytes 393220
Sparse Core Ops, SparseCore 0:
  52.1 27.5 all-gather.4
  81.3 28.5 all-gather.2
  135.0 58.3 reduce-scatter.2
  250.4 86.1 reduce-scatter.4
  356.2 29.9 all-reduce.3
where the time goes:
time: 396 us; the launch traced here: 395 us
  waiting for transfers between devices  189 us (48%)
  blocking collectives  67.5 us (17%)
  matrix products  46.8 us (12%)
  local copies, waits for them, and re-layouts  32.3 us (8%)
  Pallas kernels  27.5 us (7%)
  between operations  14.9 us (4%)
  starting transfers between devices  13.6 us (3%)
    reduce_scatter x1, waiting for transfers between devices, local(): lax.psum_scatter(lax.dot_general(block, resid_grad, (((1,), (1,)), ((), (...  71.7 us
    reduce_scatter x1, waiting for transfers between devices, local(): lax.psum_scatter(partial_rows, 'seq', scatter_dimension=0, tiled=True)  58.5 us
    all_to_all x1, waiting for transfers between devices, local(): lax.all_to_all(sum_part.reshape(capacity, exp_count, feat_cols), 'exp', s...  36.8 us
    all_to_all x1, blocking collectives, local(): lax.all_to_all(widen_pair(send_in), 'exp', split_axis=1, concat_axis=1, t...  27.2 us
    all_to_all x1, blocking collectives, local(): lax.all_to_all(widen_pair(send_grad), 'exp', split_axis=1, concat_axis=1,...  23.2 us
    all_gather x1, waiting for transfers between devices, local(): lax.all_gather(got_grad.reshape(capacity, exp_count * feat_cols), 'seq',...  16 us
    scatter x1, local copies, waits for them, and re-layouts, local(): jnp.zeros((capacity, experts), jnp.int32).at[slot_ids, flat_ids].set(owners)  11.1 us
    dot_general x1, matrix products, expert_backward(): lax.dot_general(grad_up, up_slice, contract, preferred_element_type=jnp.f...  11 us
  transfers between devices with their start and end apart: 12, of which 7 were waited for; matrix products, arithmetic and copies ran while one was open for 5% of the time, Pallas kernels for 7%

commit v1 on v0

v1 whole, which is shorter than its diff:
```python
import functools
import math

import jax
import jax.numpy as jnp
import numpy as np
from jax import lax
from jax.experimental import pallas as pl
from jax.experimental.pallas import tpu as pltpu
from jax.sharding import Mesh, PartitionSpec as P

ORDER = (0, 1, 3, 2)
PLAN = ((3, 4),)
GROUPS = ((2, 4), (0, 2))
LAG = 1
LN2 = math.log(2.0)
LANES = 128
ROOM = 40 * 1024 * 1024


CHUNKS = 8


def whole(array):
    zeros = (0,) * len(array.shape)
    return pl.BlockSpec(array.shape, lambda *unused: zeros)


def busy(microseconds):
    return pl.CostEstimate(
        flops=int(microseconds * 1.1e9 * 3.0), bytes_accessed=0, transcendentals=0
    )


def staged_call(kernel, operands, kinds, outs, scratch, cost, name, room):
    fetched = [place for place, kind in enumerate(kinds) if kind == "in"]
    given, total = len(operands), len(outs)
    held = {"in": pltpu.HBM, "hbm": pltpu.HBM, "smem": pltpu.SMEM}

    def body(*refs):
        ins, rest = list(refs[:given]), refs[given:]
        made, rest = rest[:total], rest[total:]
        buffers, arrived = rest[: len(fetched)], rest[len(fetched)]
        copies = []
        for index, place in enumerate(fetched):
            copies.append(
                pltpu.make_async_copy(ins[place], buffers[index], arrived.at[index])
            )
            copies[-1].start()
            ins[place] = buffers[index]
        for copy in copies:
            copy.wait()
        kernel(*ins, *made, *rest[len(fetched) + 1 :])

    return pl.pallas_call(
        body,
        grid=(1,),
        out_shape=tuple(out for out, kind in outs),
        in_specs=[pl.BlockSpec(memory_space=held[kind]) for kind in kinds],
        out_specs=tuple(
            whole(out) if kind == "out" else pl.BlockSpec(memory_space=pltpu.HBM)
            for out, kind in outs
        ),
        scratch_shapes=[pltpu.VMEM(operands[place].shape, operands[place].dtype) for place in fetched]
        + [pltpu.SemaphoreType.DMA((len(fetched),))]
        + list(scratch),
        compiler_params=pltpu.CompilerParams(vmem_limit_bytes=room * 1024 * 1024),
        cost_estimate=busy(cost),
        name=name,
    )(*operands)


def to_rows(rows_ref, block, group, groups):
    rows_ref[pl.ds(group, block.shape[0], stride=groups), :] = block


def forward_kernel(
    signal_ref, delta_ref, gate_ref, inmap_ref, outmap_ref, rates_ref, skip_ref, start_ref,
    kept_ref, step_rows, signal_rows, act_ref, slope_ref, maps_ref,
    rate_rows, state_rows, out_rows, kept_rows, copied,
):
    channels, tokens = signal_ref.shape
    count = rates_ref.shape[0]
    groups = channels // LANES
    span = tokens // CHUNKS
    for g in range(groups):
        part = slice(g * LANES, (g + 1) * LANES)
        to_rows(signal_rows, signal_ref[part, :].astype(jnp.float32).T, g, groups)
        to_rows(step_rows, jax.nn.softplus(delta_ref[part, :].astype(jnp.float32)).T, g, groups)
        to_rows(rate_rows, jnp.exp(rates_ref[:, part]) * (-1.0 / LN2), g, groups)
        to_rows(state_rows, start_ref[:, part], g, groups)
    skip = skip_ref[...]

    def row(ref, index):
        return ref[pl.ds(pl.multiple_of(index * groups, groups), groups), :]

    def advance(t, carry):
        states, weighed, total = carry
        step = row(step_rows, t)
        signal = row(signal_rows, t)
        drive = step * signal
        out = skip * signal
        new_states, new_weighed = [], []
        for n in range(count):
            decay = jnp.exp2(step * rate_rows[n * groups : (n + 1) * groups, :])
            kept = decay * states[n]
            kept_rows[t, n] = kept
            state = kept + inmap_ref[n, t] * drive
            out = out + outmap_ref[n, t] * state
            new_weighed.append(decay * weighed[n] + step * kept)
            new_states.append(state)
        out_rows[pl.ds(pl.multiple_of(t * groups, groups), groups), :] = out
        return (tuple(new_states), tuple(new_weighed), total + step)

    zero = jnp.zeros((groups, LANES), jnp.float32)
    first = tuple(state_rows[n * groups : (n + 1) * groups, :] for n in range(count))
    carry = (first, (zero,) * count, zero)
    copies = []
    for chunk in range(CHUNKS):
        low = chunk * span
        carry = lax.fori_loop(low, low + span, advance, carry, unroll=4)
        part = pl.ds(low, span)
        copies.append(
            pltpu.make_async_copy(kept_rows.at[part], kept_ref.at[part], copied.at[chunk])
        )
        copies[-1].start()
    unused, weighed, total = carry
    for n in range(count):
        maps_ref[n] = jnp.exp2(total * rate_rows[n * groups : (n + 1) * groups, :])
        maps_ref[count + n] = weighed[n]
    for g in range(groups):
        part = slice(g * LANES, (g + 1) * LANES)
        scan_out = out_rows[pl.ds(g, tokens, stride=groups), :].T
        gate = gate_ref[part, :].astype(jnp.float32)
        sig = jax.nn.sigmoid(gate)
        act_ref[part, :] = gate * sig
        slope_ref[part, :] = scan_out * sig * (1.0 + gate * (1.0 - sig))
    for copy in copies:
        copy.wait()


def forward_call(scan_input, delta_raw, gate_branch, state_input, state_output, log_rates, skip, start):
    channels, tokens = scan_input.shape
    count = log_rates.shape[0]
    groups = channels // LANES
    f32 = jnp.float32
    kept = pltpu.HBM((tokens, count, groups, LANES), f32)
    rows = jax.ShapeDtypeStruct((tokens * groups, LANES), f32)
    column = jax.ShapeDtypeStruct((channels, tokens), f32)
    maps = jax.ShapeDtypeStruct((2 * count, groups, LANES), f32)
    return staged_call(
        forward_kernel,
        (scan_input, delta_raw, gate_branch, state_input, state_output, log_rates, skip, start),
        ("in", "in", "in", "smem", "smem", "in", "in", "in"),
        ((kept, "hbm"),) + tuple((out, "out") for out in (rows, rows, column, column, maps)),
        [
            pltpu.VMEM((count * groups, LANES), f32),
            pltpu.VMEM((count * groups, LANES), f32),
            pltpu.VMEM((tokens * groups, LANES), f32),
            pltpu.VMEM(kept.shape, f32),
            pltpu.SemaphoreType.DMA((CHUNKS,)),
        ],
        7,
        "scan_forward",
        50,
    )


def fetch_back(kept_ref, kept_rows, copied, span):
    copies = []
    for chunk in reversed(range(CHUNKS)):
        part = pl.ds(chunk * span, span)
        copies.append(
            pltpu.make_async_copy(kept_ref.at[part], kept_rows.at[part], copied.at[chunk])
        )
        copies[-1].start()
    return copies


def local_kernel(
    extra, act_ref, slope_ref, step_rows, signal_rows, kept_ref, outmap_ref, rates_ref, *refs
):
    *inner_refs, gate_out, y_rows, sums_ref, rate_rows, kept_rows, copied = refs[extra:]
    channels, tokens = act_ref.shape
    count = rates_ref.shape[0]
    groups = channels // LANES
    span = tokens // CHUNKS
    copies = fetch_back(kept_ref, kept_rows, copied, span)
    for g in range(groups):
        part = slice(g * LANES, (g + 1) * LANES)
        inner = sum(ref[part, :].astype(jnp.float32) for ref in inner_refs)
        gate_out[part, :] = (inner * slope_ref[part, :]).astype(gate_out.dtype)
        to_rows(y_rows, (inner * act_ref[part, :]).T, g, groups)
        to_rows(rate_rows, jnp.exp(rates_ref[:, part]) * (-1.0 / LN2), g, groups)

    def row(ref, index):
        return ref[pl.ds(pl.multiple_of(index * groups, groups), groups), :]

    def advance(turn, carry):
        terms, moments, skips = carry
        t = tokens - 1 - turn
        step = row(step_rows, t)
        y_grad = row(y_rows, t)
        new_terms, new_moments = [], []
        for n in range(count):
            adjoint = outmap_ref[n, t] * y_grad + terms[n]
            new_moments.append(moments[n] + adjoint * kept_rows[t, n] * step)
            new_terms.append(
                jnp.exp2(step * rate_rows[n * groups : (n + 1) * groups, :]) * adjoint
            )
        return (tuple(new_terms), tuple(new_moments), skips + y_grad * row(signal_rows, t))

    zero = jnp.zeros((groups, LANES), jnp.float32)
    carry = ((zero,) * count, (zero,) * count, zero)
    for turn, copy in enumerate(copies):
        copy.wait()
        carry = lax.fori_loop(turn * span, (turn + 1) * span, advance, carry, unroll=4)
    terms, moments, skips = carry
    for n in range(count):
        sums_ref[n] = terms[n]
        sums_ref[count + n] = moments[n]
    sums_ref[2 * count] = skips


def local_call(inner, joined, act, slope, steps, signals, kept, state_output, log_rates):
    channels, tokens = act.shape
    count = log_rates.shape[0]
    groups = channels // LANES
    f32 = jnp.float32
    outs = (
        jax.ShapeDtypeStruct((channels, tokens), jnp.bfloat16),
        jax.ShapeDtypeStruct((tokens * groups, LANES), f32),
        jax.ShapeDtypeStruct((2 * count + 1, groups, LANES), f32),
    )
    return staged_call(
        functools.partial(local_kernel, len(joined)),
        (act, slope, steps, signals, kept, state_output, log_rates) + tuple(joined) + tuple(inner),
        ("in", "in", "in", "in", "hbm", "smem", "in")
        + ("hbm",) * len(joined)
        + ("in",) * len(inner),
        tuple((out, "out") for out in outs),
        [
            pltpu.VMEM((count * groups, LANES), f32),
            pltpu.VMEM(kept.shape, f32),
            pltpu.SemaphoreType.DMA((CHUNKS,)),
        ],
        6,
        "scan_local",
        50,
    )


def adjoint_kernel(
    incoming_ref, y_rows, step_rows, signal_rows, kept_ref, delta_ref, inmap_ref, outmap_ref,
    rates_ref, skip_ref,
    input_out, delta_out,
    rate_rows, in_rows, slope_rows, kept_rows, copied,
):
    channels, tokens = delta_ref.shape
    count = rates_ref.shape[0]
    groups = channels // LANES
    span = tokens // CHUNKS
    copies = fetch_back(kept_ref, kept_rows, copied, span)
    for g in range(groups):
        part = slice(g * LANES, (g + 1) * LANES)
        to_rows(rate_rows, jnp.exp(rates_ref[:, part]) * (-1.0 / LN2), g, groups)
    skip = skip_ref[...]

    def row(ref, index):
        return ref[pl.ds(pl.multiple_of(index * groups, groups), groups), :]

    def advance(turn, later):
        t = tokens - 1 - turn
        step = row(step_rows, t)
        y_grad = row(y_rows, t)
        pulled = jnp.zeros((groups, LANES), jnp.float32)
        decayed = jnp.zeros((groups, LANES), jnp.float32)
        new_later = []
        for n in range(count):
            rate = rate_rows[n * groups : (n + 1) * groups, :]
            adjoint = outmap_ref[n, t] * y_grad + later[n]
            pulled = pulled + inmap_ref[n, t] * adjoint
            decayed = decayed + adjoint * kept_rows[t, n] * rate
            new_later.append(jnp.exp2(step * rate) * adjoint)
        here = pl.ds(pl.multiple_of(t * groups, groups), groups)
        in_rows[here, :] = pulled * step + skip * y_grad
        slope_rows[here, :] = pulled * row(signal_rows, t) + decayed * LN2
        return tuple(new_later)

    later = tuple(incoming_ref[n] for n in range(count))
    for turn, copy in enumerate(copies):
        copy.wait()
        later = lax.fori_loop(turn * span, (turn + 1) * span, advance, later, unroll=4)
    for g in range(groups):
        part = slice(g * LANES, (g + 1) * LANES)
        input_out[part, :] = in_rows[pl.ds(g, tokens, stride=groups), :].T.astype(input_out.dtype)
        sig = jax.nn.sigmoid(delta_ref[part, :].astype(jnp.float32))
        slope = slope_rows[pl.ds(g, tokens, stride=groups), :].T
        delta_out[part, :] = (slope * sig).astype(delta_out.dtype)


def adjoint_call(incoming, y_grads, steps, signals, kept, delta_raw, state_input, state_output, log_rates, skip):
    channels, tokens = delta_raw.shape
    count = log_rates.shape[0]
    groups = channels // LANES
    f32 = jnp.float32
    out = jax.ShapeDtypeStruct((channels, tokens), jnp.bfloat16)
    return staged_call(
        adjoint_kernel,
        (incoming, y_grads, steps, signals, kept, delta_raw, state_input, state_output, log_rates, skip),
        ("in", "in", "in", "in", "hbm", "in", "smem", "smem", "in", "in"),
        ((out, "out"), (out, "out")),
        [
            pltpu.VMEM((count * groups, LANES), f32),
            pltpu.VMEM((tokens * groups, LANES), f32),
            pltpu.VMEM((tokens * groups, LANES), f32),
            pltpu.VMEM(kept.shape, f32),
            pltpu.SemaphoreType.DMA((CHUNKS,)),
        ],
        7,
        "scan_adjoint",
        50,
    )


def swap(value, axis, distance=1):
    count = lax.axis_size(axis)
    return lax.ppermute(value, axis, [(place, place ^ distance) for place in range(count)])


def full_spec(shape):
    return pl.BlockSpec(shape, lambda *unused: (0,) * len(shape))


def marks_rows(experts):
    return -(-(2 * experts + 2) // 8) * 8


def route_kernel(places_ref, ids_ref, gains_ref, input_ref, grad_ref, *refs):
    *outs, marks_ref, mark_rows = refs
    tokens = input_ref.shape[0]
    capacity = outs[0].shape[1]
    experts = len(outs)
    place = places_ref[3 * experts]
    wanted = lax.broadcasted_iota(jnp.int32, (experts, tokens), 0) ^ place
    first, second = ids_ref[0:1, :] == wanted, ids_ref[1:2, :] == wanted
    hits = first | second
    before = lax.broadcasted_iota(jnp.int32, (tokens, tokens), 0) < lax.broadcasted_iota(
        jnp.int32, (tokens, tokens), 1
    )
    slots = jnp.dot(
        hits.astype(jnp.float32).astype(jnp.bfloat16),
        before.astype(jnp.float32).astype(jnp.bfloat16),
        preferred_element_type=jnp.float32,
    )
    slots = jnp.where(hits, slots, -1.0)
    lines = lax.broadcasted_iota(jnp.int32, (capacity, tokens), 0).astype(jnp.float32)
    for d in range(experts):
        chosen = jnp.where(slots[d : d + 1, :] == lines, 1.0, 0.0).astype(jnp.bfloat16)
        for index, source in enumerate((input_ref, grad_ref)):
            outs[d][index] = jnp.dot(
                chosen, source[...], preferred_element_type=jnp.float32
            ).astype(jnp.bfloat16)
    mark_rows[...] = jnp.zeros_like(mark_rows)
    mark_rows[0:experts, :] = slots
    mark_rows[experts : 2 * experts, :] = jnp.where(
        first, gains_ref[0:1, :], jnp.where(second, gains_ref[1:2, :], 0.0)
    )
    mark_rows[2 * experts : 2 * experts + 2, :] = ids_ref[...].astype(jnp.float32)
    marks_ref[...] = mark_rows[...].T


def route_call(places, ids, gains, moe_input, out_grad, experts, capacity):
    tokens, feats = moe_input.shape
    out = jax.ShapeDtypeStruct((2, capacity, feats), jnp.bfloat16)
    lines = marks_rows(experts)
    marks = jax.ShapeDtypeStruct((tokens, lines), jnp.float32)
    made = staged_call(
        route_kernel,
        (places, ids.T, gains.T, moe_input, out_grad),
        ("smem", "in", "in", "in", "in"),
        ((out, "out"),) * experts + ((marks, "out"),),
        [pltpu.VMEM((lines, tokens), jnp.float32)],
        1,
        "route_rows",
        63,
    )
    return made[:-1], made[-1]


def follow(value, *after):
    anywhere = pl.BlockSpec(memory_space=pl.ANY)
    return pl.pallas_call(
        lambda *refs: None,
        out_shape=jax.ShapeDtypeStruct(value.shape, value.dtype),
        in_specs=[anywhere] * (1 + len(after)),
        out_specs=anywhere,
        input_output_aliases={0: 0},
        name="follow",
    )(value, *after)


def spread_plane(rows, crosswise):
    row_count = lax.axis_size("row")
    across = swap(rows, "half")
    beside = [swap(rows, "row", r) for r in range(1, row_count)]
    if crosswise:
        corner = [swap(across, "row", r) for r in range(1, row_count)]
    else:
        corner = [swap(part, "half") for part in beside]
    mine = [rows, across] + beside + corner
    near = swap(jnp.stack(mine[: 1 + row_count]), "core")
    return mine + [near] + [swap(part, "core") for part in corner]


def piece_of(refs, row_count, core, row, half):
    if core == 0:
        return refs[half if row == 0 else half * (row_count - 1) + 1 + row]
    if row and half:
        return refs[2 * row_count + row]
    return refs[2 * row_count].at[half if row == 0 else 1 + row]


def gather_kernel(groups, blocks, first, last, places_ref, after_ref, *refs):
    row_count = blocks // 2
    per = 3 * row_count
    pieces = refs[: groups * per]
    refs = refs[groups * per :]
    weights = refs[: groups * 3]
    refs = refs[groups * 3 :]
    if not first:
        held, refs = refs[:3], refs[3:]
    outs, (rows_ref,) = refs[:-1], refs[-1:]
    unused, capacity, feats = pieces[0].shape

    @pl.when(pl.program_id(0) == 0)
    def assemble():
        half = places_ref[places_ref.shape[0] - 1]
        for q in range(groups):
            for h in range(2):
                columns = pl.ds(pl.multiple_of((half ^ h) * feats, feats), feats)
                for b in range(blocks):
                    part = piece_of(
                        pieces[q * per : (q + 1) * per], row_count, b // row_count, b % row_count, h
                    )
                    for kind in range(2):
                        rows_ref[q, kind, b * capacity : (b + 1) * capacity, columns] = part[kind]

    if first:
        gate_pre = up_pre = hidden = 0.0
    else:
        gate_pre, up_pre, hidden = (ref[...] for ref in held)
    for q in range(groups):
        gate_ref, up_ref, down_ref = weights[q * 3 : q * 3 + 3]
        rows_in, rows_grad = rows_ref[q, 0], rows_ref[q, 1]
        gate_pre += jnp.dot(rows_in, gate_ref[...], preferred_element_type=jnp.float32)
        up_pre += jnp.dot(rows_in, up_ref[...], preferred_element_type=jnp.float32)
        hidden += lax.dot_general(
            rows_grad, down_ref[...], (((1,), (1,)), ((), ())),
            preferred_element_type=jnp.float32,
        )
    if not last:
        for ref, value in zip(outs, (gate_pre, up_pre, hidden)):
            ref[...] = value
        return
    gate_out, up_out, probe_out = outs
    sig = jax.nn.sigmoid(gate_pre)
    silu = gate_pre * sig
    up_out[...] = (hidden * silu).astype(jnp.bfloat16)
    weighted = hidden * up_pre
    gate_out[...] = (weighted * sig * (1.0 + gate_pre * (1.0 - sig))).astype(jnp.bfloat16)
    probe = weighted * silu
    folded = sum(
        probe[:, at : at + LANES] for at in range(0, probe.shape[1], LANES)
    )

    @pl.when(pl.program_id(0) == 0)
    def begin():
        probe_out[...] = folded

    @pl.when(pl.program_id(0) != 0)
    def add():
        probe_out[...] += folded


def gather_call(places, distances, after, pieces, gate_weight, up_weight, down_weight, held, last):
    groups, blocks = len(pieces), 2 * lax.axis_size("row")
    unused, capacity, feats = pieces[0][0].shape
    hidden = gate_weight.shape[2]
    width = min(256, hidden)
    rows = blocks * capacity
    first = held is None
    flat = [part for q in pieces for part in q]
    in_specs = [pl.BlockSpec(memory_space=pl.ANY)]
    in_specs += [full_spec(part.shape) for part in flat]
    weights = []
    for q in distances:
        in_specs += [
            pl.BlockSpec((None, 2 * feats, width), lambda j, at, q=q: (0, at[q], j)),
            pl.BlockSpec((None, 2 * feats, width), lambda j, at, q=q: (0, at[q], j)),
            pl.BlockSpec((None, width, 2 * feats), lambda j, at, q=q: (0, j, at[q])),
        ]
        weights += [gate_weight, up_weight, down_weight]
    column = pl.BlockSpec((rows, width), lambda j, at: (0, j))
    operands = [places, after] + flat + weights
    aliases = {}
    if not first:
        if not last:
            aliases = {len(operands) + i: i for i in range(3)}
        operands += list(held)
        in_specs += [column] * 3
    if last:
        out_shape = (
            jax.ShapeDtypeStruct((rows, hidden), jnp.bfloat16),
            jax.ShapeDtypeStruct((rows, hidden), jnp.bfloat16),
            jax.ShapeDtypeStruct((rows, LANES), jnp.float32),
        )
        out_specs = (column, column, full_spec((rows, LANES)))
    else:
        out_shape = (jax.ShapeDtypeStruct((rows, hidden), jnp.float32),) * 3
        out_specs = (column,) * 3
    return pl.pallas_call(
        functools.partial(gather_kernel, groups, blocks, first, last),
        out_shape=out_shape,
        grid_spec=pltpu.PrefetchScalarGridSpec(
            num_scalar_prefetch=1,
            grid=(hidden // width,),
            in_specs=in_specs,
            out_specs=out_specs,
            scratch_shapes=[pltpu.VMEM((groups, 2, rows, 2 * feats), jnp.bfloat16)],
        ),
        input_output_aliases=aliases,
        compiler_params=pltpu.CompilerParams(vmem_limit_bytes=ROOM),
        cost_estimate=busy(4 * groups),
        name="hidden_rows",
    )(*operands)


def return_kernel(
    blocks, places_ref, gate_ref, up_ref, gate_weight, up_weight, after_ref, keep_ref, send_ref
):
    contract = (((1,), (1,)), ((), ()))
    value = lax.dot_general(
        gate_ref[...], gate_weight[...], contract, preferred_element_type=jnp.float32
    ) + lax.dot_general(up_ref[...], up_weight[...], contract, preferred_element_type=jnp.float32)
    capacity = keep_ref.shape[1]
    for b in range(blocks):
        keep_ref[b] = value[b * capacity : (b + 1) * capacity]
        at = (blocks + b) * capacity
        send_ref[b] = value[at : at + capacity].astype(jnp.bfloat16)


def return_call(places, low, high, grad_gate, grad_up, gate_weight, up_weight, after, feats, row_count):
    rows, hidden = grad_gate.shape
    count, experts = high - low, lax.axis_size("expert")
    capacity = rows // (2 * row_count)
    every = pl.BlockSpec((rows, hidden), lambda q, h, at: (0, 0))
    weight = pl.BlockSpec((None, feats, hidden), lambda q, h, at: (0, at[experts * (1 + h) + low + q], 0))
    out = pl.BlockSpec((row_count, None, None, capacity, feats), lambda q, h, at: (0, h, q, 0, 0))
    shape = (row_count, 2, count, capacity, feats)
    return pl.pallas_call(
        functools.partial(return_kernel, row_count),
        out_shape=(
            jax.ShapeDtypeStruct(shape, jnp.float32),
            jax.ShapeDtypeStruct(shape, jnp.bfloat16),
        ),
        grid_spec=pltpu.PrefetchScalarGridSpec(
            num_scalar_prefetch=1,
            grid=(count, 2),
            in_specs=[every, every, weight, weight, pl.BlockSpec(memory_space=pl.ANY)],
            out_specs=(out, out),
        ),
        compiler_params=pltpu.CompilerParams(vmem_limit_bytes=ROOM),
        cost_estimate=busy(4 * count),
        name="route_grads",
    )(places, grad_gate, grad_up, gate_weight, up_weight, after)


def corner_swap(value, distance):
    rows = lax.axis_size("row")
    pairs = [
        (row * 2 + half, (row ^ distance) * 2 + (half ^ 1))
        for row in range(rows)
        for half in range(2)
    ]
    return lax.ppermute(value, ("row", "half"), pairs)


def sum_plane(keep, send):
    row_count = keep.shape[0]
    wide, narrow = jnp.float32, jnp.bfloat16
    paired = keep + swap(send, "core").astype(wide)
    small = paired.astype(narrow)
    parts = [swap(small[0, 1], "half")]
    for r in range(1, row_count):
        parts += [corner_swap(small[r, 1], r), swap(small[r, 0], "row", r)]
    total = paired[0, 0] + sum(part.astype(wide) for part in parts)
    return small, total.astype(narrow)


def resid_kernel(marks_ref, grad_ref, *refs):
    *parts, out_ref = refs
    tokens = grad_ref.shape[0]
    experts, capacity = len(parts), parts[0].shape[0]
    lines = lax.broadcasted_iota(jnp.int32, (tokens, capacity), 1).astype(jnp.float32)
    total = grad_ref[...].astype(jnp.float32)
    for d, part in enumerate(parts):
        chosen = jnp.where(marks_ref[:, d : d + 1] == lines, 1.0, 0.0).astype(jnp.bfloat16)
        gain = marks_ref[:, experts + d : experts + d + 1]
        total += gain * jnp.dot(chosen, part[...], preferred_element_type=jnp.float32)
    out_ref[...] = total.astype(out_ref.dtype)


def resid_call(marks, out_grad, parts):
    out = jax.ShapeDtypeStruct(out_grad.shape, jnp.bfloat16)
    return staged_call(
        resid_kernel,
        (marks, out_grad) + tuple(parts),
        ("in", "in") + ("in",) * len(parts),
        ((out, "out"),),
        [],
        2,
        "resid_rows",
        63,
    )[0]


def probe_lines_kernel(probes_ref, after_ref, out_ref):
    blocks, capacity = out_ref.shape
    for b in range(blocks):
        part = probes_ref[b * capacity : (b + 1) * capacity, :].T
        out_ref[b : b + 1, :] = jnp.sum(part, axis=0, keepdims=True)


def probe_lines_call(probes, after, blocks):
    out = jax.ShapeDtypeStruct((blocks, probes.shape[0] // blocks), jnp.float32)
    return staged_call(
        probe_lines_kernel, (probes, after), ("in", "hbm"), ((out, "out"),), [], 1, "probe_lines", 16
    )[0]


def probe_kernel(places_ref, marks_ref, table_ref, out_ref):
    experts, capacity = table_ref.shape
    tokens = marks_ref.shape[0]
    place = places_ref[3 * experts]
    lines = lax.broadcasted_iota(jnp.int32, (tokens, capacity), 1).astype(jnp.float32)
    columns = lax.broadcasted_iota(jnp.int32, (tokens, 2), 1)
    named = marks_ref[:, 2 * experts : 2 * experts + 2]
    total = jnp.zeros(columns.shape, jnp.float32)
    for d in range(experts):
        taken = jnp.where(marks_ref[:, d : d + 1] == lines, table_ref[d : d + 1, :], 0.0)
        value = jnp.sum(taken, axis=1, keepdims=True)
        total += jnp.where(named == (place ^ d).astype(jnp.float32), value, 0.0)
    out_ref[...] = total


def probe_call(places, marks, table):
    out = jax.ShapeDtypeStruct((marks.shape[0], 2), jnp.float32)
    return staged_call(
        probe_kernel, (places, marks, table), ("smem", "in", "in"), ((out, "out"),), [], 1,
        "probe_rows",
        16,
    )[0]


def project_kernel(places_ref, far_weight, own_weight, resid_ref, after_ref, far_ref, own_ref):
    for weight_ref, out_ref in ((far_weight, far_ref), (own_weight, own_ref)):
        value = lax.dot_general(
            weight_ref[...], resid_ref[...], (((1,), (1,)), ((), ())),
            preferred_element_type=jnp.float32,
        )
        out_ref[...] = value.astype(out_ref.dtype)


def project_call(places, distance, out_weight, resid, after, channels):
    tokens, feats = resid.shape
    shape = (channels, tokens)
    experts = lax.axis_size("expert")
    return pl.pallas_call(
        project_kernel,
        out_shape=(
            jax.ShapeDtypeStruct(shape, jnp.bfloat16),
            jax.ShapeDtypeStruct(shape, jnp.float32),
        ),
        grid_spec=pltpu.PrefetchScalarGridSpec(
            num_scalar_prefetch=1,
            grid=(1,),
            in_specs=[
                pl.BlockSpec((channels, feats), lambda i, at: (at[2 * experts + distance], 0)),
                pl.BlockSpec((channels, feats), lambda i, at: (at[experts + distance], 0)),
                full_spec((tokens, feats)),
                pl.BlockSpec(memory_space=pl.ANY),
            ],
            out_specs=(full_spec(shape),) * 2,
        ),
        compiler_params=pltpu.CompilerParams(vmem_limit_bytes=ROOM),
        cost_estimate=busy(2),
        name="inner_parts",
    )(places, out_weight, out_weight, resid, after)


def probe_table(lines):
    experts, rows = lax.axis_size("expert"), lax.axis_size("row")
    lines = lines.reshape(2, rows, lines.shape[1])
    lines = lines[0] + swap(lines[1], "core")
    lines = lines[0] + sum(swap(lines[r], "row", r) for r in range(1, rows))
    lines = lines + swap(lines, "half")
    return jnp.stack([lines] + [swap(lines, "expert", d) for d in range(1, experts)])


def in_order(own, other):
    first = lax.axis_index("core") == 0
    return jnp.where(first, own, other), jnp.where(first, other, own)


def join_maps(maps):
    count = maps.shape[0] // 2
    former, latter = in_order(maps, swap(maps, "core"))
    decay = former[:count] * latter[:count]
    weight = latter[count:] + former[count:] * latter[:count]
    joined = jnp.concatenate([decay, weight], axis=0)
    rows = lax.axis_size("row")
    return former, latter, [joined] + [swap(joined, "row", r) for r in range(1, rows)]


def join_sums(sums, former, latter, joined):
    count = joined[0].shape[0] // 2
    rows, row = lax.axis_size("row"), lax.axis_index("row")
    ahead, behind = in_order(sums, swap(sums, "core"))
    own_term = behind[:count]
    both = ahead + behind
    pair = jnp.concatenate(
        [
            ahead[:count] + former[:count] * own_term,
            both[count : 2 * count] + former[count:] * own_term,
            both[2 * count :],
        ],
        axis=0,
    )
    pairs = [pair] + [swap(pair, "row", r) for r in range(1, rows)]
    carried = jnp.zeros_like(own_term)
    incoming = jnp.zeros_like(own_term)
    moment = jnp.zeros_like(own_term)
    for place in reversed(range(rows)):
        maps_here, pair_here = joined[0], pair
        for r in range(1, rows):
            there = (row ^ r) == place
            maps_here = jnp.where(there, joined[r], maps_here)
            pair_here = jnp.where(there, pairs[r], pair_here)
        incoming = jnp.where(row == place, carried, incoming)
        moment = moment + pair_here[count : 2 * count] + maps_here[count:] * carried
        carried = pair_here[:count] + maps_here[:count] * carried
    skips = sum(part[2 * count] for part in pairs)
    into_first = own_term + latter[:count] * incoming
    return jnp.where(lax.axis_index("core") == 0, into_first, incoming), moment, skips


def local(
    moe_input,
    out_grad,
    expert_ids,
    expert_route_weights,
    gate_weight,
    up_weight,
    down_weight,
    out_weight,
    scan_input,
    delta_raw,
    mixer_gate_branch,
    state_input,
    state_output,
    log_rates,
    skip_gain,
    block_states,
):
    experts = lax.axis_size("expert")
    row_count = lax.axis_size("row")
    tokens, feats = moe_input.shape
    capacity = 3 * expert_ids.shape[1] * tokens // (2 * experts)
    channels = scan_input.shape[0]
    groups = channels // LANES
    states = log_rates.shape[0]
    skip_rows = skip_gain.reshape(groups, LANES)
    apart = np.arange(experts) ^ np.arange(experts)[:, None]
    table = np.zeros((experts, 2, 3 * experts + 2), np.int32)
    for half in range(2):
        table[:, half, :experts] = apart
        table[:, half, experts : 2 * experts] = 2 * apart + half
        table[:, half, 2 * experts : 3 * experts] = 2 * apart + 1 - half
        table[:, half, 3 * experts] = np.arange(experts)
        table[:, half, 3 * experts + 1] = half
    places = lax.dynamic_index_in_dim(
        jnp.asarray(table.reshape(2 * experts, -1)),
        2 * lax.axis_index("expert") + lax.axis_index("half"),
        keepdims=False,
    )

    kept, steps, signals, act, slope, maps = forward_call(
        scan_input, delta_raw, mixer_gate_branch, state_input, state_output, log_rates, skip_rows,
        block_states[0],
    )
    sent, marks = route_call(
        places, expert_ids, expert_route_weights, moe_input, out_grad, experts, capacity
    )
    got = {}
    for d in ORDER:
        got[d] = sent[d] if d == 0 else swap(sent[d], "expert", d)
        if d == 1:
            got[d] = follow(got[d], maps)
    held = None
    queue = []
    step = 0
    for index, d in enumerate(ORDER):
        queue.append((d, spread_plane(got[d], d % 2 == 0)))
        while step < len(PLAN) and PLAN[step][0] == index:
            took = PLAN[step][1]
            group, queue = queue[:took], queue[took:]
            step += 1
            held = gather_call(
                places,
                [q for q, unused in group],
                maps,
                [pieces for unused, pieces in group],
                gate_weight, up_weight, down_weight, held, step == len(PLAN),
            )
    grad_gate, grad_up, probes = held

    parts = [None] * experts
    after = [probes] * LAG
    for low, high in GROUPS:
        low, high = low * experts // 4, high * experts // 4
        keep, send = return_call(
            places, low, high, grad_gate, grad_up, gate_weight, up_weight, after[-LAG], feats,
            row_count,
        )
        small, summed = sum_plane(keep, send)
        after.append(small)
        for d in reversed(range(low, high)):
            parts[d] = summed[d - low] if d == 0 else swap(summed[d - low], "expert", d)
    resid_grad = resid_call(marks, out_grad, parts)
    lines = probe_lines_call(probes, resid_grad, 2 * row_count)
    probs_grad = probe_call(places, marks, probe_table(lines))

    inner = [None] * experts
    after = [resid_grad] * 2
    for d in reversed(range(experts)):
        far_part, own_part = project_call(
            places, d, out_weight, resid_grad, after[-2], channels
        )
        far_part = swap(far_part, "half")
        after.append(far_part)
        total = own_part + far_part.astype(jnp.float32)
        inner[d] = total if d == 0 else swap(total.astype(jnp.bfloat16), "expert", d)

    former, latter, joined = join_maps(maps)
    gate_grad, y_grads, sums = local_call(
        inner, joined, act, slope, steps, signals, kept, state_output, log_rates
    )
    incoming, moment, skips = join_sums(sums, former, latter, joined)
    input_grad, delta_grad = adjoint_call(
        incoming, y_grads, steps, signals, kept, delta_raw, state_input, state_output, log_rates,
        skip_rows,
    )
    rates_grad = -jnp.exp(log_rates) * moment.reshape(states, channels)
    skip_grad = skips.reshape(channels)
    return (resid_grad, probs_grad, input_grad, delta_grad, gate_grad, rates_grad, skip_grad)


def solution(mesh):
    seq_count, exp_count = mesh.shape["seq"], mesh.shape["exp"]
    split = Mesh(
        mesh.devices.reshape(seq_count // 2, 2, exp_count // 2, 2),
        ("row", "core", "expert", "half"),
    )
    seq, exp = ("row", "core"), ("expert", "half")
    in_specs = (
        P(seq, exp),
        P(seq, exp),
        P(seq, None),
        P(seq, None),
        P(exp, None, seq),
        P(exp, None, seq),
        P(exp, seq, None),
        P(None, exp),
        P(exp, seq),
        P(exp, seq),
        P(exp, seq),
        P(None, seq),
        P(None, seq),
        P(None, exp),
        P(exp),
        P(seq, None, exp),
    )
    out_specs = (
        P(seq, exp),
        P(seq, None),
        P(exp, seq),
        P(exp, seq),
        P(exp, seq),
        P(None, exp),
        P(exp),
    )
    return jax.shard_map(local, mesh=split, in_specs=in_specs, out_specs=out_specs, check_vma=False)
```

time: 396 us -> 196 us (0.49)
  waiting for transfers between devices: 189 us -> 63.3 us
  blocking collectives: 67.5 us -> 0 us
  matrix products: 46.8 us -> 0 us
  starting transfers between devices: 13.6 us -> 49 us
  Pallas kernels: 27.5 us -> 60.6 us
  local copies, waits for them, and re-layouts: 32.3 us -> 12.2 us
  between operations: 14.9 us -> 1.33 us
  other arithmetic: 2.97 us -> 8.85 us
    reduce_scatter x2 -> x0, waiting for transfers between devices: 130 us -> none  [the longest x1 71.7 us: local(): lax.psum_scatter(lax.dot_general(block, resid_grad, (((1,), (1,)), ((), (...]
    all_to_all x3 -> x0, blocking collectives: 61.1 us -> none  [the longest x1 27.2 us: local(): lax.all_to_all(widen_pair(send_in), 'exp', split_axis=1, concat_axis=1, t...]
    ppermute x6 -> x51, waiting for transfers between devices: 5 us -> 63.3 us  [the longest x49 63.3 us: swap(): lax.ppermute(value, axis, [(place, place ^ distance) for place in range(c...]
    dot_general x6 -> x0, matrix products: 46.8 us -> none  [the longest x1 11 us: expert_backward(): lax.dot_general(grad_up, up_slice, contract, preferred_element_type=jnp.f...]
    ppermute x6 -> x51, starting transfers between devices: 7.73 us -> 49 us  [the longest x49 44.4 us: swap(): lax.ppermute(value, axis, [(place, place ^ distance) for place in range(c...]
    all_to_all x1 -> x0, waiting for transfers between devices: 36.8 us -> none  [local(): lax.all_to_all(sum_part.reshape(capacity, exp_count, feat_cols), 'exp', s...]
    pallas_call x3 -> x15, Pallas kernels: 27.5 us -> 60.6 us  [the longest x7 27.7 us: staged_call(): pl.pallas_call(body, grid=(1,), out_shape=tuple((out for out, kind in out...]
    all_gather x2 -> x0, waiting for transfers between devices: 17.1 us -> none  [the longest x1 16 us: local(): lax.all_gather(got_grad.reshape(capacity, exp_count * feat_cols), 'seq',...]
  transfers between devices with their start and end apart: 12 -> 51, of which waited for: 7 -> 23; matrix products, arithmetic and copies ran while one was open for 5% -> 3% of each run, Pallas kernels for 7% -> 10%
where the time goes in v1:
time: 196 us; the launch traced here: 195 us
  waiting for transfers between devices  63.3 us (32%)
  Pallas kernels  60.6 us (31%)
  starting transfers between devices  49 us (25%)
  local copies, waits for them, and re-layouts  12.2 us (6%)
  other arithmetic  8.85 us (5%)
    ppermute x49, waiting for transfers between devices, swap(): lax.ppermute(value, axis, [(place, place ^ distance) for place in range(c...  63.3 us
    ppermute x49, starting transfers between devices, swap(): lax.ppermute(value, axis, [(place, place ^ distance) for place in range(c...  44.4 us
    pallas_call x7, Pallas kernels, staged_call(): pl.pallas_call(body, grid=(1,), out_shape=tuple((out for out, kind in out...  27.7 us
    pallas_call x1, Pallas kernels, gather_call(): pl.pallas_call(functools.partial(gather_kernel, groups, blocks, first, la...  15.5 us
    pallas_call x2, Pallas kernels, return_call(): pl.pallas_call(functools.partial(return_kernel, row_count), out_shape=(ja...  12.5 us
    unnamed x75, local copies, waits for them, and re-layouts  10.3 us
    pallas_call x4, Pallas kernels, project_call(): pl.pallas_call(project_kernel, out_shape=(jax.ShapeDtypeStruct(shape, jnp...  4.96 us
    ppermute x2, starting transfers between devices, corner_swap(): return lax.ppermute(value, ('row', 'half'), pairs)  4.61 us
  transfers between devices with their start and end apart: 51, of which 23 were waited for; matrix products, arithmetic and copies ran while one was open for 3% of the time, Pallas kernels for 10%

profile of v1, /device:TPU:0, one launch (start us, length us, event | category | flops | bytes accessed | tf_op | source)
XLA Modules:
  0.0 195.3 jit_solution(7713085428008447252)
XLA Ops:
  1.9 3.0 %route_rows.1 = (bf16[2,96,512]{2,1,0:T(8,128)(2,1)}, bf16[2,96,512]{2,1,0:T(8,128)(2,1)}, bf16[2,96,512]{2,1,0:T(8,128)(2,1)}, bf16[2,96,512]{2,1,0:T(8,128)(2,1)}, f32[128,16]{1,0:T(8,128)}) custom-call(s32[14]{0:T(128)} %dynamic-slice_bitcast_fusion.refs_0_.places_ref, s32[2,128]{1,0:T(2,128)} %bitcast.85, f32[2,128]{1,0:T(2,128)} %bitcast.86, ...), custom_call_target="tpu_custom_call" | custom-call | flops 3300000000 | tf_op jit(solution)/shard_map/route_rows/pallas_call | solution.py:55
  5.0 3.0 %collective-permute-start = (bf16[2,96,512]{2,1,0:T(8,128)(2,1)}, bf16[2,96,512]{2,1,0:T(8,128)(2,1)S(1)}, u32[]{:S(2)}, u32[]{:S(2)}) collective-permute-start(bf16[2,96,512]{2,1,0:T(8,128)(2,1)} %get-tuple-element.40.refs_0_), channel_id=1, source_target_pairs={{0,1},{1,0},{2,3},{3,2},{4,5},{5,4},{6,7},{7,6},{8,9},{9,8},{10,11... | collective-permute-start | bytes 589832 | tf_op jit(solution)/shard_map/ppermute | solution.py:328
  11.1 2.5 %collective-permute-start.11 = (bf16[2,96,512]{2,1,0:T(8,128)(2,1)}, bf16[2,96,512]{2,1,0:T(8,128)(2,1)S(1)}, u32[]{:S(2)}, u32[]{:S(2)}) collective-permute-start(bf16[2,96,512]{2,1,0:T(8,128)(2,1)} %get-tuple-element.42), channel_id=1, source_target_pairs={{0,6},{2,4},{4,2},{6,0},{1,7},{3,5},{5,3},{7,1},{8,14},{10,12},{12... | collective-permute-start | bytes 589832 | tf_op jit(solution)/shard_map/ppermute | solution.py:328
  13.7 6.4 %scan_forward.1 = (f32[128,16,8,128]{3,2,1,0:T(8,128)}, f32[1024,128]{1,0:T(8,128)S(1)}, f32[1024,128]{1,0:T(8,128)S(1)}, f32[1024,128]{1,0:T(8,128)S(1)}, f32[1...) custom-call(bf16[1024,128]{1,0:T(8,128)(2,1)S(1)} %copy-done.7, bf16[1024,128]{1,0:T(8,128)(2,1)S(1)} %copy-done.9, ...), custom_call_target="tpu_custom_call" | custom-call | flops 23100000256 | tf_op jit(solution)/shard_map/scan_forward/pallas_call | solution.py:55
  28.8 1.8 collective-permute-done.17.refs_18_
  31.1 1.7 collective-permute-done.6.refs_7_
  35.0 6.3 %collective-permute-done.2.refs_3_ = bf16[2,96,512]{2,1,0:T(8,128)(2,1)S(1)} collective-permute-done((bf16[2,96,512]{2,1,0:T(8,128)(2,1)S(1)}, bf16[2,96,512]{2,1,0:T(8,128)(2,1)S(1)}, u32[]{:S(2)}, u32[]{:S(2)}) %collective-permute-start.2) | collective-permute-done | bytes 196640 | tf_op jit(solution)/shard_map/ppermute | solution.py:328
  44.5 4.5 %collective-permute-done.8.refs_9_ = bf16[2,96,512]{2,1,0:T(8,128)(2,1)S(1)} collective-permute-done((bf16[2,96,512]{2,1,0:T(8,128)(2,1)S(1)}, bf16[2,96,512]{2,1,0:T(8,128)(2,1)S(1)}, u32[]{:S(2)}, u32[]{:S(2)}) %collective-permute-start.8) | collective-permute-done | bytes 196640 | tf_op jit(solution)/shard_map/ppermute | solution.py:328
  48.9 3.8 %collective-permute-done.14.refs_15_ = bf16[2,96,512]{2,1,0:T(8,128)(2,1)S(1)} collective-permute-done((bf16[2,96,512]{2,1,0:T(8,128)(2,1)S(1)}, bf16[2,96,512]{2,1,0:T(8,128)(2,1)S(1)}, u32[]{:S(2)}, u32[]{:S(2)}) %collective-permute-start.14) | collective-permute-done | bytes 196640 | tf_op jit(solution)/shard_map/ppermute | solution.py:328
  53.4 1.7 collective-permute-done.10.refs_11_
  56.5 15.5 %hidden_rows.1 = (bf16[384,1024]{1,0:T(8,128)(2,1)S(1)}, bf16[384,1024]{1,0:T(8,128)(2,1)S(1)}, f32[384,128]{1,0:T(8,128)S(1)}) custom-call(s32[14]{0:T(128)S(1)} %copy-done.16, f32[32,8,128]{2,1,0:T(8,128)S(1)} %copy-done.3, bf16[2,96,512]{2,1,0:T(8,128)(2,1)S(1)} %copy-done.4, bf16[2,96,512]{2,1,0:T(8,128)(2,1)S(1)} %collective-permute-done.refs_1_, ...), custom_call_target="tpu_custom_call" | custom-call | flops 52800000000 | tf_op jit(solution)/shard_map/hidden_rows/pallas_call | solution.py:522
  72.1 6.2 %route_grads.2 = (f32[2,2,2,96,512]{4,3,2,1,0:T(8,128)S(1)}, bf16[2,2,2,96,512]{4,3,2,1,0:T(8,128)(2,1)S(1)}) custom-call(s32[14]{0:T(128)S(1)} %copy-done.16, bf16[384,1024]{1,0:T(8,128)(2,1)S(1)} %get-tuple-element.44.gate_ref, bf16[384,1024]{1,0:T(8,128)(2,1)S(1)} %get-tuple-element.45.up_ref, bf16[1,4096,1024]{2,1,0:T(8,128)(2,1)S(1)} %bitcast.76, ...), custom_call_target="tpu_custom_call" | custom-call | flops 26400000000 | tf_op jit(solution)/shard_map/route_grads/pallas_call | solution.py:561
  78.6 2.1 %collective-permute-done.23 = bf16[2,2,2,96,512]{4,3,2,1,0:T(8,128)(2,1)S(1)} collective-permute-done((bf16[2,2,2,96,512]{4,3,2,1,0:T(8,128)(2,1)S(1)}, bf16[2,2,2,96,512]{4,3,2,1,0:T(8,128)(2,1)S(1)}, u32[]{:S(2)}, u32[]{:S(2)}) %collective-permute-start.23) | collective-permute-done | bytes 786464 | tf_op jit(solution)/shard_map/ppermute | solution.py:328
  82.2 6.2 %route_grads.3 = (f32[2,2,2,96,512]{4,3,2,1,0:T(8,128)S(1)}, bf16[2,2,2,96,512]{4,3,2,1,0:T(8,128)(2,1)S(1)}) custom-call(s32[14]{0:T(128)S(1)} %copy-done.16, bf16[384,1024]{1,0:T(8,128)(2,1)S(1)} %get-tuple-element.44.gate_ref, bf16[384,1024]{1,0:T(8,128)(2,1)S(1)} %get-tuple-element.45.up_ref, bf16[1,4096,1024]{2,1,0:T(8,128)(2,1)S(1)} %bitcast.76, ...), custom_call_target="tpu_custom_call" | custom-call | flops 26400000000 | tf_op jit(solution)/shard_map/route_grads/pallas_call | solution.py:561
  89.8 2.3 %collective-permute-start.30 = (bf16[2,96,512]{2,1,0:T(8,128)(2,1)S(1)}, bf16[2,96,512]{2,1,0:T(8,128)(2,1)S(1)}, u32[]{:S(2)}, u32[]{:S(2)}) collective-permute-start(bf16[2,96,512]{2,1,0:T(8,128)(2,1)S(1)} %get-tuple-element.85), channel_id=1, source_target_pairs={{0,17},{1,16},{16,1},{17,0},{2,19},{3,18},{18,3},{19,2},{4,21},{5,... | collective-permute-start | bytes 589832 | tf_op jit(solution)/shard_map/ppermute | solution.py:586
  93.6 6.7 %collective-permute-done.31 = bf16[2,96,512]{2,1,0:T(8,128)(2,1)S(1)} collective-permute-done((bf16[2,96,512]{2,1,0:T(8,128)(2,1)S(1)}, bf16[2,96,512]{2,1,0:T(8,128)(2,1)S(1)}, u32[]{:S(2)}, u32[]{:S(2)}) %collective-permute-start.31) | collective-permute-done | bytes 196640 | tf_op jit(solution)/shard_map/ppermute | solution.py:328
  104.9 2.3 %collective-permute-start.26 = (bf16[2,96,512]{2,1,0:T(8,128)(2,1)S(1)}, bf16[2,96,512]{2,1,0:T(8,128)(2,1)S(1)}, u32[]{:S(2)}, u32[]{:S(2)}) collective-permute-start(bf16[2,96,512]{2,1,0:T(8,128)(2,1)S(1)} %get-tuple-element.88), channel_id=1, source_target_pairs={{0,17},{1,16},{16,1},{17,0},{2,19},{3,18},{18,3},{19,2},{4,21},{5,... | collective-permute-start | bytes 589832 | tf_op jit(solution)/shard_map/ppermute | solution.py:586
  107.7 2.6 %collective-permute-start.32 = (bf16[96,512]{1,0:T(8,128)(2,1)S(1)}, bf16[96,512]{1,0:T(8,128)(2,1)S(1)}, u32[]{:S(2)}, u32[]{:S(2)}) collective-permute-start(bf16[96,512]{1,0:T(8,128)(2,1)S(1)} %get-tuple-element.98), channel_id=1, source_target_pairs={{0,4},{2,6},{4,0},{6,2},{1,5},{3,7},{5,1},{7,3},{8,12},{10,14},{12... | collective-permute-start | bytes 294920 | tf_op jit(solution)/shard_map/ppermute | solution.py:328
  111.7 2.6 %collective-permute-done.27 = bf16[2,96,512]{2,1,0:T(8,128)(2,1)S(1)} collective-permute-done((bf16[2,96,512]{2,1,0:T(8,128)(2,1)S(1)}, bf16[2,96,512]{2,1,0:T(8,128)(2,1)S(1)}, u32[]{:S(2)}, u32[]{:S(2)}) %collective-permute-start.27) | collective-permute-done | bytes 196640 | tf_op jit(solution)/shard_map/ppermute | solution.py:328
  117.9 3.1 %collective-permute-done.28.refs_3_ = bf16[96,512]{1,0:T(8,128)(2,1)S(1)} collective-permute-done((bf16[96,512]{1,0:T(8,128)(2,1)S(1)}, bf16[96,512]{1,0:T(8,128)(2,1)S(1)}, u32[]{:S(2)}, u32[]{:S(2)}) %collective-permute-start.28) | collective-permute-done | bytes 98336 | tf_op jit(solution)/shard_map/ppermute | solution.py:328
  121.6 2.2 %resid_rows.1.refs_1_.resid_ref.after_ref = bf16[128,512]{1,0:T(8,128)(2,1)} custom-call(f32[128,16]{1,0:T(8,128)} %get-tuple-element.38.refs_0_.refs_1_, bf16[128,512]{1,0:T(8,128)(2,1)} %refs_1_.3, bf16[96,512]{1,0:T(8,128)(2,1)} %get-tuple-element.100.refs_2_, bf16[96,512]{1,0:T(8,128)(2,1)} %copy-done.34, bf16[96,512]{1,0:T(8,128)(2,1)} %copy-done.32, ...), custom_call_target="tpu_custom_call" | custom-call | flops 6600000000 | tf_op jit(solution)/shard_map/resid_rows/pallas_call | solution.py:55
  125.4 3.4 %copy-done.6 = bf16[8192,512]{1,0:T(8,128)(2,1)S(1)} copy-done((bf16[8192,512]{1,0:T(8,128)(2,1)S(1)}, bf16[8192,512]{1,0:T(8,128)(2,1)}, u32[]{:S(2)}) %copy-start.6) | copy-done | bytes 8388632
  135.7 3.5 %collective-permute-done.42.after_ref = bf16[1024,128]{1,0:T(8,128)(2,1)S(1)} collective-permute-done((bf16[1024,128]{1,0:T(8,128)(2,1)S(1)}, bf16[1024,128]{1,0:T(8,128)(2,1)S(1)}, u32[]{:S(2)}, u32[]{:S(2)}) %collective-permute-start.42) | collective-permute-done | bytes 262176 | tf_op jit(solution)/shard_map/ppermute | solution.py:328
  141.9 2.8 %collective-permute-done.44.after_ref = bf16[1024,128]{1,0:T(8,128)(2,1)S(1)} collective-permute-done((bf16[1024,128]{1,0:T(8,128)(2,1)S(1)}, bf16[1024,128]{1,0:T(8,128)(2,1)S(1)}, u32[]{:S(2)}, u32[]{:S(2)}) %collective-permute-start.44) | collective-permute-done | bytes 262176 | tf_op jit(solution)/shard_map/ppermute | solution.py:328
  147.6 2.6 %collective-permute-start.47 = (bf16[1024,128]{1,0:T(8,128)(2,1)S(1)}, bf16[1024,128]{1,0:T(8,128)(2,1)S(1)}, u32[]{:S(2)}, u32[]{:S(2)}) collective-permute-start(bf16[1024,128]{1,0:T(8,128)(2,1)S(1)} %add_convert_fusion.1), channel_id=1, source_target_pairs={{0,4},{2,6},{4,0},{6,2},{1,5},{3,7},{5,1},{7,3},{8,12},{10,14},{12... | collective-permute-start | bytes 786440 | tf_op jit(solution)/shard_map/ppermute | solution.py:328
  151.7 3.9 %collective-permute-done.45 = bf16[1024,128]{1,0:T(8,128)(2,1)S(1)} collective-permute-done((bf16[1024,128]{1,0:T(8,128)(2,1)S(1)}, bf16[1024,128]{1,0:T(8,128)(2,1)S(1)}, u32[]{:S(2)}, u32[]{:S(2)}) %collective-permute-start.45) | collective-permute-done | bytes 262176 | tf_op jit(solution)/shard_map/ppermute | solution.py:328
  158.0 2.5 %collective-permute-start.39 = (f32[96]{0:T(128)S(1)}, f32[96]{0:T(128)S(1)}, u32[]{:S(2)}, u32[]{:S(2)}) collective-permute-start(f32[96]{0:T(128)S(1)} %add.98), channel_id=1, source_target_pairs={{0,6},{2,4},{4,2},{6,0},{1,7},{3,5},{5,3},{7,1},{8,14},{10,12},{12... | collective-permute-start | bytes 1160 | tf_op jit(solution)/shard_map/ppermute | solution.py:328
  164.0 4.3 %collective-permute-done.47.refs_11_ = bf16[1024,128]{1,0:T(8,128)(2,1)S(1)} collective-permute-done((bf16[1024,128]{1,0:T(8,128)(2,1)S(1)}, bf16[1024,128]{1,0:T(8,128)(2,1)S(1)}, u32[]{:S(2)}, u32[]{:S(2)}) %collective-permute-start.47) | collective-permute-done | bytes 262176 | tf_op jit(solution)/shard_map/ppermute | solution.py:328
  168.2 4.1 %collective-permute-done.46.refs_10_ = bf16[1024,128]{1,0:T(8,128)(2,1)S(1)} collective-permute-done((bf16[1024,128]{1,0:T(8,128)(2,1)S(1)}, bf16[1024,128]{1,0:T(8,128)(2,1)S(1)}, u32[]{:S(2)}, u32[]{:S(2)}) %collective-permute-start.46) | collective-permute-done | bytes 262176 | tf_op jit(solution)/shard_map/ppermute | solution.py:328
  172.4 7.0 %scan_local.1 = (bf16[1024,128]{1,0:T(8,128)(2,1)}, f32[1024,128]{1,0:T(8,128)S(1)}, f32[33,8,128]{2,1,0:T(8,128)S(1)}) custom-call(f32[1024,128]{1,0:T(8,128)S(1)} %copy-done.25, f32[1024,128]{1,0:T(8,128)S(1)} %copy-done.27, f32[1024,128]{1,0:T(8,128)S(1)} %copy-done.21, f32[1024,128]{1,0:T(8,128)S(1)} %copy-done.23, ...), custom_call_target="tpu_custom_call" | custom-call | flops 19800000512 | tf_op jit(solution)/shard_map/scan_local/pallas_call | solution.py:55
  183.3 3.3 %collective-permute-done.50 = f32[33,8,128]{2,1,0:T(8,128)S(1)} collective-permute-done((f32[33,8,128]{2,1,0:T(8,128)S(1)}, f32[33,8,128]{2,1,0:T(8,128)S(1)}, u32[]{:S(2)}, u32[]{:S(2)}) %collective-permute-start.50) | collective-permute-done | bytes 135200 | tf_op jit(solution)/shard_map/ppermute | solution.py:328
  187.3 7.4 %scan_adjoint.1 = (bf16[1024,128]{1,0:T(8,128)(2,1)}, bf16[1024,128]{1,0:T(8,128)(2,1)}) custom-call(f32[16,8,128]{2,1,0:T(8,128)S(1)} %get-tuple-element.90.refs_0_, f32[1024,128]{1,0:T(8,128)S(1)} %get-tuple-element.65.refs_1_, f32[1024,128]{1,0:T(8,128)S(1)} %copy-done.21, f32[1024,128]{1,0:T(8,128)S(1)} %copy-done.23, ...), custom_call_target="tpu_custom_call" | custom-call | flops 23100000256 | tf_op jit(solution)/shard_map/scan_adjoint/pallas_call | solution.py:55
  (196 shorter events, 62.8 us)
Async XLA Ops:
  5.0 20.3 %collective-permute-start = (bf16[2,96,512]{2,1,0:T(8,128)(2,1)}, bf16[2,96,512]{2,1,0:T(8,128)(2,1)S(1)}, u32[]{:S(2)}, u32[]{:S(2)}) collective-permute-start(bf16[2,96,512]{2,1,0:T(8,128)(2,1)} %get-tuple-element.40.refs_0_), channel_id=1, source_target_pairs={{0,1},{1,0},{2,3},{3,2},{4,5},{5,4},{6,7},{7,6},{8,9},{9,8},{10,11... | collective-permute-start | bytes 589832 | tf_op jit(solution)/shard_map/ppermute | solution.py:328
  8.0 19.3 %collective-permute-start.1 = (bf16[2,96,512]{2,1,0:T(8,128)(2,1)}, bf16[2,96,512]{2,1,0:T(8,128)(2,1)S(1)}, u32[]{:S(2)}, u32[]{:S(2)}) collective-permute-start(bf16[2,96,512]{2,1,0:T(8,128)(2,1)} %get-tuple-element.40.refs_0_), channel_id=1, source_target_pairs={{0,16},{16,0},{1,17},{17,1},{2,18},{18,2},{3,19},{19,3},{4,20},{20... | collective-permute-start | bytes 589832 | tf_op jit(solution)/shard_map/ppermute | solution.py:328
  9.5 14.6 %collective-permute-start.5 = (bf16[2,96,512]{2,1,0:T(8,128)(2,1)}, bf16[2,96,512]{2,1,0:T(8,128)(2,1)S(1)}, u32[]{:S(2)}, u32[]{:S(2)}) collective-permute-start(bf16[2,96,512]{2,1,0:T(8,128)(2,1)} %get-tuple-element.41), channel_id=1, source_target_pairs={{0,2},{2,0},{4,6},{6,4},{1,3},{3,1},{5,7},{7,5},{8,10},{10,8},{12,... | collective-permute-start | bytes 589832 | tf_op jit(solution)/shard_map/ppermute | solution.py:328
  11.1 14.7 %collective-permute-start.11 = (bf16[2,96,512]{2,1,0:T(8,128)(2,1)}, bf16[2,96,512]{2,1,0:T(8,128)(2,1)S(1)}, u32[]{:S(2)}, u32[]{:S(2)}) collective-permute-start(bf16[2,96,512]{2,1,0:T(8,128)(2,1)} %get-tuple-element.42), channel_id=1, source_target_pairs={{0,6},{2,4},{4,2},{6,0},{1,7},{3,5},{5,3},{7,1},{8,14},{10,12},{12... | collective-permute-start | bytes 589832 | tf_op jit(solution)/shard_map/ppermute | solution.py:328
  13.5 17.0 %collective-permute-start.17 = (bf16[2,96,512]{2,1,0:T(8,128)(2,1)}, bf16[2,96,512]{2,1,0:T(8,128)(2,1)S(1)}, u32[]{:S(2)}, u32[]{:S(2)}) collective-permute-start(bf16[2,96,512]{2,1,0:T(8,128)(2,1)} %get-tuple-element.43), channel_id=1, source_target_pairs={{0,4},{2,6},{4,0},{6,2},{1,5},{3,7},{5,1},{7,3},{8,12},{10,14},{12... | collective-permute-start | bytes 589832 | tf_op jit(solution)/shard_map/ppermute | solution.py:328
  25.8 15.5 %collective-permute-start.12 = (bf16[2,96,512]{2,1,0:T(8,128)(2,1)S(1)}, bf16[2,96,512]{2,1,0:T(8,128)(2,1)S(1)}, u32[]{:S(2)}, u32[]{:S(2)}) collective-permute-start(bf16[2,96,512]{2,1,0:T(8,128)(2,1)S(1)} %collective-permute-done.11.refs_12_), channel_id=1, source_target_pairs={{0,1},{1,0},{2,3},{3,2},{4,5},{5,4},{6,7},{7,6},{8,9},{9,8},{10,11... | collective-permute-start | bytes 589832 | tf_op jit(solution)/shard_map/ppermute | solution.py:328
  27.3 15.5 %collective-permute-start.13 = (bf16[2,96,512]{2,1,0:T(8,128)(2,1)S(1)}, bf16[2,96,512]{2,1,0:T(8,128)(2,1)S(1)}, u32[]{:S(2)}, u32[]{:S(2)}) collective-permute-start(bf16[2,96,512]{2,1,0:T(8,128)(2,1)S(1)} %collective-permute-done.11.refs_12_), channel_id=1, source_target_pairs={{0,16},{16,0},{1,17},{17,1},{2,18},{18,2},{3,19},{19,3},{4,20},{20... | collective-permute-start | bytes 589832 | tf_op jit(solution)/shard_map/ppermute | solution.py:328
  30.6 10.7 %collective-permute-start.2 = (bf16[2,96,512]{2,1,0:T(8,128)(2,1)S(1)}, bf16[2,96,512]{2,1,0:T(8,128)(2,1)S(1)}, u32[]{:S(2)}, u32[]{:S(2)}) collective-permute-start(bf16[2,96,512]{2,1,0:T(8,128)(2,1)S(1)} %collective-permute-done.refs_1_), channel_id=1, source_target_pairs={{0,16},{16,0},{1,17},{17,1},{2,18},{18,2},{3,19},{19,3},{4,20},{20... | collective-permute-start | bytes 589832 | tf_op jit(solution)/shard_map/ppermute | solution.py:328
  32.8 10.2 %collective-permute-start.18 = (bf16[2,96,512]{2,1,0:T(8,128)(2,1)S(1)}, bf16[2,96,512]{2,1,0:T(8,128)(2,1)S(1)}, u32[]{:S(2)}, u32[]{:S(2)}) collective-permute-start(bf16[2,96,512]{2,1,0:T(8,128)(2,1)S(1)} %collective-permute-done.17.refs_18_), channel_id=1, source_target_pairs={{0,1},{1,0},{2,3},{3,2},{4,5},{5,4},{6,7},{7,6},{8,9},{9,8},{10,11... | collective-permute-start | bytes 589832 | tf_op jit(solution)/shard_map/ppermute | solution.py:328
  33.4 10.2 %collective-permute-start.19 = (bf16[2,96,512]{2,1,0:T(8,128)(2,1)S(1)}, bf16[2,96,512]{2,1,0:T(8,128)(2,1)S(1)}, u32[]{:S(2)}, u32[]{:S(2)}) collective-permute-start(bf16[2,96,512]{2,1,0:T(8,128)(2,1)S(1)} %collective-permute-done.17.refs_18_), channel_id=1, source_target_pairs={{0,16},{16,0},{1,17},{17,1},{2,18},{18,2},{3,19},{19,3},{4,20},{20... | collective-permute-start | bytes 589832 | tf_op jit(solution)/shard_map/ppermute | solution.py:328
  41.2 12.1 %collective-permute-start.3 = (bf16[3,2,96,512]{3,2,1,0:T(8,128)(2,1)S(1)}, bf16[3,2,96,512]{3,2,1,0:T(8,128)(2,1)S(1)}, u32[]{:S(2)}, u32[]{:S(2)}) collective-permute-start(bf16[3,2,96,512]{3,2,1,0:T(8,128)(2,1)S(1)} %pad_maximum_fusion), channel_id=1, source_target_pairs={{0,8},{8,0},{1,9},{9,1},{2,10},{10,2},{3,11},{11,3},{4,12},{12,4},... | collective-permute-start | bytes 1769480 | tf_op jit(solution)/shard_map/ppermute | solution.py:328
  43.0 9.8 %collective-permute-start.14 = (bf16[2,96,512]{2,1,0:T(8,128)(2,1)S(1)}, bf16[2,96,512]{2,1,0:T(8,128)(2,1)S(1)}, u32[]{:S(2)}, u32[]{:S(2)}) collective-permute-start(bf16[2,96,512]{2,1,0:T(8,128)(2,1)S(1)} %collective-permute-done.13.refs_14_), channel_id=1, source_target_pairs={{0,1},{1,0},{2,3},{3,2},{4,5},{5,4},{6,7},{7,6},{8,9},{9,8},{10,11... | collective-permute-start | bytes 589832 | tf_op jit(solution)/shard_map/ppermute | solution.py:328
  43.6 9.2 %collective-permute-start.20 = (bf16[2,96,512]{2,1,0:T(8,128)(2,1)S(1)}, bf16[2,96,512]{2,1,0:T(8,128)(2,1)S(1)}, u32[]{:S(2)}, u32[]{:S(2)}) collective-permute-start(bf16[2,96,512]{2,1,0:T(8,128)(2,1)S(1)} %collective-permute-done.18.refs_19_), channel_id=1, source_target_pairs={{0,16},{16,0},{1,17},{17,1},{2,18},{18,2},{3,19},{19,3},{4,20},{20... | collective-permute-start | bytes 589832 | tf_op jit(solution)/shard_map/ppermute | solution.py:328
  44.4 12.1 %collective-permute-start.9 = (bf16[3,2,96,512]{3,2,1,0:T(8,128)(2,1)S(1)}, bf16[3,2,96,512]{3,2,1,0:T(8,128)(2,1)S(1)}, u32[]{:S(2)}, u32[]{:S(2)}) collective-permute-start(bf16[3,2,96,512]{3,2,1,0:T(8,128)(2,1)S(1)} %pad_maximum_fusion.1), channel_id=1, source_target_pairs={{0,8},{8,0},{1,9},{9,1},{2,10},{10,2},{3,11},{11,3},{4,12},{12,4},... | collective-permute-start | bytes 1769480 | tf_op jit(solution)/shard_map/ppermute | solution.py:328
  88.5 14.2 %collective-permute-start.24 = (bf16[2,2,2,96,512]{4,3,2,1,0:T(8,128)(2,1)S(1)}, bf16[2,2,2,96,512]{4,3,2,1,0:T(8,128)(2,1)}, u32[]{:S(2)}, u32[]{:S(2)}) collective-permute-start(bf16[2,2,2,96,512]{4,3,2,1,0:T(8,128)(2,1)S(1)} %get-tuple-element.50), channel_id=1, source_target_pairs={{0,8},{8,0},{1,9},{9,1},{2,10},{10,2},{3,11},{11,3},{4,12},{12,4},... | collective-permute-start | bytes 2359304 | tf_op jit(solution)/shard_map/ppermute | solution.py:328
  89.1 11.2 %collective-permute-start.31 = (bf16[2,96,512]{2,1,0:T(8,128)(2,1)S(1)}, bf16[2,96,512]{2,1,0:T(8,128)(2,1)S(1)}, u32[]{:S(2)}, u32[]{:S(2)}) collective-permute-start(bf16[2,96,512]{2,1,0:T(8,128)(2,1)S(1)} %get-tuple-element.84), channel_id=1, source_target_pairs={{0,16},{16,0},{1,17},{17,1},{2,18},{18,2},{3,19},{19,3},{4,20},{20... | collective-permute-start | bytes 589832 | tf_op jit(solution)/shard_map/ppermute | solution.py:328
  89.8 10.5 %collective-permute-start.30 = (bf16[2,96,512]{2,1,0:T(8,128)(2,1)S(1)}, bf16[2,96,512]{2,1,0:T(8,128)(2,1)S(1)}, u32[]{:S(2)}, u32[]{:S(2)}) collective-permute-start(bf16[2,96,512]{2,1,0:T(8,128)(2,1)S(1)} %get-tuple-element.85), channel_id=1, source_target_pairs={{0,17},{1,16},{16,1},{17,0},{2,19},{3,18},{18,3},{19,2},{4,21},{5,... | collective-permute-start | bytes 589832 | tf_op jit(solution)/shard_map/ppermute | solution.py:586
  92.1 9.4 %collective-permute-start.29 = (bf16[2,96,512]{2,1,0:T(8,128)(2,1)S(1)}, bf16[2,96,512]{2,1,0:T(8,128)(2,1)S(1)}, u32[]{:S(2)}, u32[]{:S(2)}) collective-permute-start(bf16[2,96,512]{2,1,0:T(8,128)(2,1)S(1)} %get-tuple-element.83), channel_id=1, source_target_pairs={{0,1},{1,0},{2,3},{3,2},{4,5},{5,4},{6,7},{7,6},{8,9},{9,8},{10,11... | collective-permute-start | bytes 589832 | tf_op jit(solution)/shard_map/ppermute | solution.py:328
  104.2 10.1 %collective-permute-start.27 = (bf16[2,96,512]{2,1,0:T(8,128)(2,1)S(1)}, bf16[2,96,512]{2,1,0:T(8,128)(2,1)S(1)}, u32[]{:S(2)}, u32[]{:S(2)}) collective-permute-start(bf16[2,96,512]{2,1,0:T(8,128)(2,1)S(1)} %get-tuple-element.87), channel_id=1, source_target_pairs={{0,16},{16,0},{1,17},{17,1},{2,18},{18,2},{3,19},{19,3},{4,20},{20... | collective-permute-start | bytes 589832 | tf_op jit(solution)/shard_map/ppermute | solution.py:328
  104.9 9.4 %collective-permute-start.26 = (bf16[2,96,512]{2,1,0:T(8,128)(2,1)S(1)}, bf16[2,96,512]{2,1,0:T(8,128)(2,1)S(1)}, u32[]{:S(2)}, u32[]{:S(2)}) collective-permute-start(bf16[2,96,512]{2,1,0:T(8,128)(2,1)S(1)} %get-tuple-element.88), channel_id=1, source_target_pairs={{0,17},{1,16},{16,1},{17,0},{2,19},{3,18},{18,3},{19,2},{4,21},{5,... | collective-permute-start | bytes 589832 | tf_op jit(solution)/shard_map/ppermute | solution.py:586
  107.7 10.1 %collective-permute-start.32 = (bf16[96,512]{1,0:T(8,128)(2,1)S(1)}, bf16[96,512]{1,0:T(8,128)(2,1)S(1)}, u32[]{:S(2)}, u32[]{:S(2)}) collective-permute-start(bf16[96,512]{1,0:T(8,128)(2,1)S(1)} %get-tuple-element.98), channel_id=1, source_target_pairs={{0,4},{2,6},{4,0},{6,2},{1,5},{3,7},{5,1},{7,3},{8,12},{10,14},{12... | collective-permute-start | bytes 294920 | tf_op jit(solution)/shard_map/ppermute | solution.py:328
  130.0 9.2 %collective-permute-start.42 = (bf16[1024,128]{1,0:T(8,128)(2,1)S(1)}, bf16[1024,128]{1,0:T(8,128)(2,1)S(1)}, u32[]{:S(2)}, u32[]{:S(2)}) collective-permute-start(bf16[1024,128]{1,0:T(8,128)(2,1)S(1)} %get-tuple-element.56), channel_id=1, source_target_pairs={{0,1},{1,0},{2,3},{3,2},{4,5},{5,4},{6,7},{7,6},{8,9},{9,8},{10,11... | collective-permute-start | bytes 786440 | tf_op jit(solution)/shard_map/ppermute | solution.py:328
  133.4 11.4 %collective-permute-start.44 = (bf16[1024,128]{1,0:T(8,128)(2,1)S(1)}, bf16[1024,128]{1,0:T(8,128)(2,1)S(1)}, u32[]{:S(2)}, u32[]{:S(2)}) collective-permute-start(bf16[1024,128]{1,0:T(8,128)(2,1)S(1)} %get-tuple-element.59), channel_id=1, source_target_pairs={{0,1},{1,0},{2,3},{3,2},{4,5},{5,4},{6,7},{7,6},{8,9},{9,8},{10,11... | collective-permute-start | bytes 786440 | tf_op jit(solution)/shard_map/ppermute | solution.py:328
  135.2 22.1 %collective-permute-start.36 = (f32[96]{0:T(128)S(1)}, f32[96]{0:T(128)S(1)}, u32[]{:S(2)}, u32[]{:S(2)}) collective-permute-start(f32[96]{0:T(128)S(1)} %bitcast_add_fusion), channel_id=1, source_target_pairs={{0,1},{1,0},{2,3},{3,2},{4,5},{5,4},{6,7},{7,6},{8,9},{9,8},{10,11... | collective-permute-start | bytes 1160 | tf_op jit(solution)/shard_map/ppermute | solution.py:328
  140.4 17.6 %collective-permute-start.43 = (bf16[1024,128]{1,0:T(8,128)(2,1)S(1)}, bf16[1024,128]{1,0:T(8,128)(2,1)S(1)}, u32[]{:S(2)}, u32[]{:S(2)}) collective-permute-start(bf16[1024,128]{1,0:T(8,128)(2,1)S(1)} %get-tuple-element.58), channel_id=1, source_target_pairs={{0,1},{1,0},{2,3},{3,2},{4,5},{5,4},{6,7},{7,6},{8,9},{9,8},{10,11... | collective-permute-start | bytes 786440 | tf_op jit(solution)/shard_map/ppermute | solution.py:328
  146.0 9.6 %collective-permute-start.45 = (bf16[1024,128]{1,0:T(8,128)(2,1)S(1)}, bf16[1024,128]{1,0:T(8,128)(2,1)S(1)}, u32[]{:S(2)}, u32[]{:S(2)}) collective-permute-start(bf16[1024,128]{1,0:T(8,128)(2,1)S(1)} %get-tuple-element.61), channel_id=1, source_target_pairs={{0,1},{1,0},{2,3},{3,2},{4,5},{5,4},{6,7},{7,6},{8,9},{9,8},{10,11... | collective-permute-start | bytes 786440 | tf_op jit(solution)/shard_map/ppermute | solution.py:328
  147.6 20.6 %collective-permute-start.47 = (bf16[1024,128]{1,0:T(8,128)(2,1)S(1)}, bf16[1024,128]{1,0:T(8,128)(2,1)S(1)}, u32[]{:S(2)}, u32[]{:S(2)}) collective-permute-start(bf16[1024,128]{1,0:T(8,128)(2,1)S(1)} %add_convert_fusion.1), channel_id=1, source_target_pairs={{0,4},{2,6},{4,0},{6,2},{1,5},{3,7},{5,1},{7,3},{8,12},{10,14},{12... | collective-permute-start | bytes 786440 | tf_op jit(solution)/shard_map/ppermute | solution.py:328
  150.3 17.9 %collective-permute-start.48 = (bf16[1024,128]{1,0:T(8,128)(2,1)S(1)}, bf16[1024,128]{1,0:T(8,128)(2,1)S(1)}, u32[]{:S(2)}, u32[]{:S(2)}) collective-permute-start(bf16[1024,128]{1,0:T(8,128)(2,1)S(1)} %add_convert_fusion), channel_id=1, source_target_pairs={{0,6},{2,4},{4,2},{6,0},{1,7},{3,5},{5,3},{7,1},{8,14},{10,12},{12... | collective-permute-start | bytes 786440 | tf_op jit(solution)/shard_map/ppermute | solution.py:328
  155.7 16.6 %collective-permute-start.46 = (bf16[1024,128]{1,0:T(8,128)(2,1)S(1)}, bf16[1024,128]{1,0:T(8,128)(2,1)S(1)}, u32[]{:S(2)}, u32[]{:S(2)}) collective-permute-start(bf16[1024,128]{1,0:T(8,128)(2,1)S(1)} %add_convert_fusion.2), channel_id=1, source_target_pairs={{0,2},{2,0},{4,6},{6,4},{1,3},{3,1},{5,7},{7,5},{8,10},{10,8},{12,... | collective-permute-start | bytes 786440 | tf_op jit(solution)/shard_map/ppermute | solution.py:328
  158.0 21.5 %collective-permute-start.39 = (f32[96]{0:T(128)S(1)}, f32[96]{0:T(128)S(1)}, u32[]{:S(2)}, u32[]{:S(2)}) collective-permute-start(f32[96]{0:T(128)S(1)} %add.98), channel_id=1, source_target_pairs={{0,6},{2,4},{4,2},{6,0},{1,7},{3,5},{5,3},{7,1},{8,14},{10,12},{12... | collective-permute-start | bytes 1160 | tf_op jit(solution)/shard_map/ppermute | solution.py:328
  162.3 17.2 %collective-permute-start.38 = (f32[96]{0:T(128)S(1)}, f32[96]{0:T(128)S(1)}, u32[]{:S(2)}, u32[]{:S(2)}) collective-permute-start(f32[96]{0:T(128)S(1)} %add.98), channel_id=1, source_target_pairs={{0,4},{2,6},{4,0},{6,2},{1,5},{3,7},{5,1},{7,3},{8,12},{10,14},{12... | collective-permute-start | bytes 1160 | tf_op jit(solution)/shard_map/ppermute | solution.py:328
  168.2 11.2 %collective-permute-start.37 = (f32[96]{0:T(128)S(1)}, f32[96]{0:T(128)S(1)}, u32[]{:S(2)}, u32[]{:S(2)}) collective-permute-start(f32[96]{0:T(128)S(1)} %add.98), channel_id=1, source_target_pairs={{0,2},{2,0},{4,6},{6,4},{1,3},{3,1},{5,7},{7,5},{8,10},{10,8},{12,... | collective-permute-start | bytes 1160 | tf_op jit(solution)/shard_map/ppermute | solution.py:328
  (56 other events, 512.7 us)

commit v2 on v1

--- a/solution.py
+++ b/solution.py
@@ -15,7 +15,7 @@
 LAG = 1
 LN2 = math.log(2.0)
 LANES = 128
-ROOM = 40 * 1024 * 1024
+ROOM = 44 * 1024 * 1024
 
 
 CHUNKS = 8
@@ -104,10 +104,11 @@
         for n in range(count):
             decay = jnp.exp2(step * rate_rows[n * groups : (n + 1) * groups, :])
             kept = decay * states[n]
-            kept_rows[t, n] = kept
+            paced = step * kept
+            kept_rows[t, n] = paced
             state = kept + inmap_ref[n, t] * drive
             out = out + outmap_ref[n, t] * state
-            new_weighed.append(decay * weighed[n] + step * kept)
+            new_weighed.append(decay * weighed[n] + paced)
             new_states.append(state)
         out_rows[pl.ds(pl.multiple_of(t * groups, groups), groups), :] = out
         return (tuple(new_states), tuple(new_weighed), total + step)
@@ -145,8 +146,8 @@
     groups = channels // LANES
     f32 = jnp.float32
     kept = pltpu.HBM((tokens, count, groups, LANES), f32)
-    rows = jax.ShapeDtypeStruct((tokens * groups, LANES), f32)
-    column = jax.ShapeDtypeStruct((channels, tokens), f32)
+    rows = pltpu.HBM((tokens * groups, LANES), f32)
+    column = pltpu.HBM((channels, tokens), f32)
     maps = jax.ShapeDtypeStruct((2 * count, groups, LANES), f32)
     return staged_call(
         forward_kernel,
@@ -204,7 +205,7 @@
         new_terms, new_moments = [], []
         for n in range(count):
             adjoint = outmap_ref[n, t] * y_grad + terms[n]
-            new_moments.append(moments[n] + adjoint * kept_rows[t, n] * step)
+            new_moments.append(moments[n] + adjoint * kept_rows[t, n])
             new_terms.append(
                 jnp.exp2(step * rate_rows[n * groups : (n + 1) * groups, :]) * adjoint
             )
@@ -284,7 +285,7 @@
             new_later.append(jnp.exp2(step * rate) * adjoint)
         here = pl.ds(pl.multiple_of(t * groups, groups), groups)
         in_rows[here, :] = pulled * step + skip * y_grad
-        slope_rows[here, :] = pulled * row(signal_rows, t) + decayed * LN2
+        slope_rows[here, :] = pulled * row(signal_rows, t) + decayed * (LN2 / step)
         return tuple(new_later)
 
     later = tuple(incoming_ref[n] for n in range(count))
@@ -336,11 +337,11 @@
     return -(-(2 * experts + 2) // 8) * 8
 
 
-def route_kernel(places_ref, ids_ref, gains_ref, input_ref, grad_ref, *refs):
-    *outs, marks_ref, mark_rows = refs
+def route_kernel(low, high, places_ref, ids_ref, gains_ref, input_ref, grad_ref, *refs):
+    outs = refs[: high - low]
     tokens = input_ref.shape[0]
     capacity = outs[0].shape[1]
-    experts = len(outs)
+    experts = (places_ref.shape[0] - 2) // 3
     place = places_ref[3 * experts]
     wanted = lax.broadcasted_iota(jnp.int32, (experts, tokens), 0) ^ place
     first, second = ids_ref[0:1, :] == wanted, ids_ref[1:2, :] == wanted
@@ -355,12 +356,15 @@
     )
     slots = jnp.where(hits, slots, -1.0)
     lines = lax.broadcasted_iota(jnp.int32, (capacity, tokens), 0).astype(jnp.float32)
-    for d in range(experts):
+    for d in range(low, high):
         chosen = jnp.where(slots[d : d + 1, :] == lines, 1.0, 0.0).astype(jnp.bfloat16)
         for index, source in enumerate((input_ref, grad_ref)):
-            outs[d][index] = jnp.dot(
+            outs[d - low][index] = jnp.dot(
                 chosen, source[...], preferred_element_type=jnp.float32
             ).astype(jnp.bfloat16)
+    if low:
+        return
+    marks_ref, mark_rows = refs[-2:]
     mark_rows[...] = jnp.zeros_like(mark_rows)
     mark_rows[0:experts, :] = slots
     mark_rows[experts : 2 * experts, :] = jnp.where(
@@ -375,17 +379,23 @@
     out = jax.ShapeDtypeStruct((2, capacity, feats), jnp.bfloat16)
     lines = marks_rows(experts)
     marks = jax.ShapeDtypeStruct((tokens, lines), jnp.float32)
-    made = staged_call(
-        route_kernel,
-        (places, ids.T, gains.T, moe_input, out_grad),
-        ("smem", "in", "in", "in", "in"),
-        ((out, "out"),) * experts + ((marks, "out"),),
+    given = (places, ids.T, gains.T, moe_input, out_grad)
+    kinds = ("smem", "in", "in", "in", "in")
+    far = staged_call(
+        functools.partial(route_kernel, 1, experts), given, kinds, ((out, "out"),) * (experts - 1),
+        [], 1, "route_rows", 63,
+    )
+    own, marks = staged_call(
+        lambda *refs: route_kernel(0, 1, *refs[:5], *refs[6:]),
+        given + (far[0],),
+        kinds + ("hbm",),
+        ((out, "out"), (marks, "out")),
         [pltpu.VMEM((lines, tokens), jnp.float32)],
         1,
-        "route_rows",
+        "route_own",
         63,
     )
-    return made[:-1], made[-1]
+    return (own,) + tuple(far), marks
 
 
 def follow(value, *after):
@@ -838,18 +848,17 @@
         for d in reversed(range(low, high)):
             parts[d] = summed[d - low] if d == 0 else swap(summed[d - low], "expert", d)
     resid_grad = resid_call(marks, out_grad, parts)
-    lines = probe_lines_call(probes, resid_grad, 2 * row_count)
+    lines = probe_lines_call(probes, grad_up, 2 * row_count)
     probs_grad = probe_call(places, marks, probe_table(lines))
 
     inner = [None] * experts
-    after = [resid_grad] * 2
+    after = resid_grad
     for d in reversed(range(experts)):
         far_part, own_part = project_call(
-            places, d, out_weight, resid_grad, after[-2], channels
+            places, d, out_weight, resid_grad, after, channels
         )
-        far_part = swap(far_part, "half")
-        after.append(far_part)
-        total = own_part + far_part.astype(jnp.float32)
+        after = far_part
+        total = own_part + swap(far_part, "half").astype(jnp.float32)
         inner[d] = total if d == 0 else swap(total.astype(jnp.bfloat16), "expert", d)
 
     former, latter, joined = join_maps(maps)

time: 196 us -> 182 us (0.929)
  waiting for transfers between devices: 63.3 us -> 40.8 us
  starting transfers between devices: 49 us -> 54.5 us
  Pallas kernels: 60.6 us -> 65.8 us
  local copies, waits for them, and re-layouts: 12.2 us -> 10.2 us
    ppermute x49, waiting for transfers between devices: 63.3 us -> 36.7 us  [swap(): lax.ppermute(value, axis, [(place, place ^ distance) for place in range(c...]
    ppermute x49, starting transfers between devices: 44.4 us -> 51.5 us  [swap(): lax.ppermute(value, axis, [(place, place ^ distance) for place in range(c...]
    ppermute x2, waiting for transfers between devices: 0.01 us -> 4.19 us  [corner_swap(): return lax.ppermute(value, ('row', 'half'), pairs)]
    pallas_call x7 -> x8, Pallas kernels: 27.7 us -> 31.1 us  [staged_call(): pl.pallas_call(body, grid=(1,), out_shape=tuple((out for out, kind in out...]
    unnamed x75 -> x77, local copies, waits for them, and re-layouts: 10.3 us -> 8.17 us
  transfers between devices with their start and end apart: 51 -> 51, of which waited for: 23 -> 23; matrix products, arithmetic and copies ran while one was open for 3% -> 4% of each run, Pallas kernels for 10% -> 29%
where the time goes in v2:
time: 182 us; the launch traced here: 181 us
  Pallas kernels  65.8 us (36%)
  starting transfers between devices  54.5 us (30%)
  waiting for transfers between devices  40.8 us (22%)
  local copies, waits for them, and re-layouts  10.2 us (6%)
  other arithmetic  8.4 us (5%)
    ppermute x49, starting transfers between devices, swap(): lax.ppermute(value, axis, [(place, place ^ distance) for place in range(c...  51.5 us
    ppermute x49, waiting for transfers between devices, swap(): lax.ppermute(value, axis, [(place, place ^ distance) for place in range(c...  36.7 us
    pallas_call x8, Pallas kernels, staged_call(): pl.pallas_call(body, grid=(1,), out_shape=tuple((out for out, kind in out...  31.1 us
    pallas_call x1, Pallas kernels, gather_call(): pl.pallas_call(functools.partial(gather_kernel, groups, blocks, first, la...  15.5 us
    pallas_call x2, Pallas kernels, return_call(): pl.pallas_call(functools.partial(return_kernel, row_count), out_shape=(ja...  14.1 us
    unnamed x77, local copies, waits for them, and re-layouts  8.17 us
    pallas_call x4, Pallas kernels, project_call(): pl.pallas_call(project_kernel, out_shape=(jax.ShapeDtypeStruct(shape, jnp...  4.95 us
    ppermute x2, waiting for transfers between devices, corner_swap(): return lax.ppermute(value, ('row', 'half'), pairs)  4.19 us
  transfers between devices with their start and end apart: 51, of which 23 were waited for; matrix products, arithmetic and copies ran while one was open for 4% of the time, Pallas kernels for 29%

profile of v2, /device:TPU:0, one launch (start us, length us, event | category | flops | bytes accessed | tf_op | source)
XLA Modules:
  0.0 181.1 jit_solution(11683692172100256985)
XLA Ops:
  1.8 2.8 %route_rows.1 = (bf16[2,96,512]{2,1,0:T(8,128)(2,1)}, bf16[2,96,512]{2,1,0:T(8,128)(2,1)}, bf16[2,96,512]{2,1,0:T(8,128)(2,1)}) custom-call(s32[14]{0:T(128)} %dynamic-slice_bitcast_fusion.refs_0_.places_ref, s32[2,128]{1,0:T(2,128)} %bitcast.83, f32[2,128]{1,0:T(2,128)} %bitcast.85, bf16[128,512]{1,0:T(8,128)(2,1)} %refs_3_.4, bf16[128,512]{1,0:T(8,128)(2,1)} %refs_1_.3), custom_call_target="tpu_custom_call" | custom-call | flops 3300000000 | tf_op jit(solution)/shard_map/route_rows/pallas_call | solution.py:55
  4.8 2.8 %route_own.1 = (bf16[2,96,512]{2,1,0:T(8,128)(2,1)}, f32[128,16]{1,0:T(8,128)}) custom-call(s32[14]{0:T(128)} %dynamic-slice_bitcast_fusion.refs_0_.places_ref, s32[2,128]{1,0:T(2,128)} %bitcast.84, f32[2,128]{1,0:T(2,128)} %bitcast.86, bf16[128,512]{1,0:T(8,128)(2,1)} %refs_3_.4, bf16[128,512]{1,0:T(8,128)(2,1)} %refs_1_.3, ...), custom_call_target="tpu_custom_call" | custom-call | flops 3300000000 | tf_op jit(solution)/shard_map/route_own/pallas_call | solution.py:55
  7.6 3.0 %collective-permute-start = (bf16[2,96,512]{2,1,0:T(8,128)(2,1)}, bf16[2,96,512]{2,1,0:T(8,128)(2,1)S(1)}, u32[]{:S(2)}, u32[]{:S(2)}) collective-permute-start(bf16[2,96,512]{2,1,0:T(8,128)(2,1)} %get-tuple-element.41.refs_0_), channel_id=1, source_target_pairs={{0,1},{1,0},{2,3},{3,2},{4,5},{5,4},{6,7},{7,6},{8,9},{9,8},{10,11... | collective-permute-start | bytes 589832 | tf_op jit(solution)/shard_map/ppermute | solution.py:329
  13.7 2.5 %collective-permute-start.11 = (bf16[2,96,512]{2,1,0:T(8,128)(2,1)}, bf16[2,96,512]{2,1,0:T(8,128)(2,1)S(1)}, u32[]{:S(2)}, u32[]{:S(2)}) collective-permute-start(bf16[2,96,512]{2,1,0:T(8,128)(2,1)} %get-tuple-element.42), channel_id=1, source_target_pairs={{0,6},{2,4},{4,2},{6,0},{1,7},{3,5},{5,3},{7,1},{8,14},{10,12},{12... | collective-permute-start | bytes 589832 | tf_op jit(solution)/shard_map/ppermute | solution.py:329
  16.4 7.8 %scan_forward.1 = (f32[128,16,8,128]{3,2,1,0:T(8,128)}, f32[1024,128]{1,0:T(8,128)}, f32[1024,128]{1,0:T(8,128)}, f32[1024,128]{1,0:T(8,128)}, f32[1024,128]{1,0:T(8,128)}, /*index=5*/f32[32,8,128]{2,1,0:T(8,128)S(1)}) custom-call(bf16[1024,128]{1,0:T(8,128)(2,1)S(1)} %copy-done.7, bf16[1024,128]{1,0:T(8,128)(2,1)S(1)} %copy-done.9, ...), custom_call_target="tpu_custom_call" | custom-call | flops 23100000256 | tf_op jit(solution)/shard_map/scan_forward/pallas_call | solution.py:55
  29.6 3.6 %collective-permute-done.17.refs_18_ = bf16[2,96,512]{2,1,0:T(8,128)(2,1)S(1)} collective-permute-done((bf16[2,96,512]{2,1,0:T(8,128)(2,1)}, bf16[2,96,512]{2,1,0:T(8,128)(2,1)S(1)}, u32[]{:S(2)}, u32[]{:S(2)}) %collective-permute-start.17) | collective-permute-done | bytes 196640 | tf_op jit(solution)/shard_map/ppermute | solution.py:329
  34.4 1.6 collective-permute-start.19
  38.7 2.9 %collective-permute-done.2.refs_3_ = bf16[2,96,512]{2,1,0:T(8,128)(2,1)S(1)} collective-permute-done((bf16[2,96,512]{2,1,0:T(8,128)(2,1)S(1)}, bf16[2,96,512]{2,1,0:T(8,128)(2,1)S(1)}, u32[]{:S(2)}, u32[]{:S(2)}) %collective-permute-start.2) | collective-permute-done | bytes 196640 | tf_op jit(solution)/shard_map/ppermute | solution.py:329
  45.1 3.9 %collective-permute-done.14.refs_15_ = bf16[2,96,512]{2,1,0:T(8,128)(2,1)S(1)} collective-permute-done((bf16[2,96,512]{2,1,0:T(8,128)(2,1)S(1)}, bf16[2,96,512]{2,1,0:T(8,128)(2,1)S(1)}, u32[]{:S(2)}, u32[]{:S(2)}) %collective-permute-start.14) | collective-permute-done | bytes 196640 | tf_op jit(solution)/shard_map/ppermute | solution.py:329
  52.7 15.5 %hidden_rows.1 = (bf16[384,1024]{1,0:T(8,128)(2,1)S(1)}, bf16[384,1024]{1,0:T(8,128)(2,1)S(1)}, f32[384,128]{1,0:T(8,128)S(1)}) custom-call(s32[14]{0:T(128)S(1)} %copy-done.16, f32[32,8,128]{2,1,0:T(8,128)S(1)} %copy-done.3, bf16[2,96,512]{2,1,0:T(8,128)(2,1)S(1)} %copy-done.4, bf16[2,96,512]{2,1,0:T(8,128)(2,1)S(1)} %collective-permute-done.refs_1_, ...), custom_call_target="tpu_custom_call" | custom-call | flops 52800000000 | tf_op jit(solution)/shard_map/hidden_rows/pallas_call | solution.py:532
  68.3 7.0 %route_grads.2 = (f32[2,2,2,96,512]{4,3,2,1,0:T(8,128)S(1)}, bf16[2,2,2,96,512]{4,3,2,1,0:T(8,128)(2,1)S(1)}) custom-call(s32[14]{0:T(128)S(1)} %copy-done.16, bf16[384,1024]{1,0:T(8,128)(2,1)S(1)} %get-tuple-element.44.gate_ref, bf16[384,1024]{1,0:T(8,128)(2,1)S(1)} %get-tuple-element.45.up_ref.refs_1_, bf16[1,4096,1024]{2,1,0:T(8,128)(2,1)} %gate_weight.3, ...), custom_call_target="tpu_custom_call" | custom-call | flops 26400000000 | tf_op jit(solution)/shard_map/route_grads/pallas_call | solution.py:571
  79.1 1.6 fusion.14
  80.7 7.2 %route_grads.3 = (f32[2,2,2,96,512]{4,3,2,1,0:T(8,128)S(1)}, bf16[2,2,2,96,512]{4,3,2,1,0:T(8,128)(2,1)S(1)}) custom-call(s32[14]{0:T(128)S(1)} %copy-done.16, bf16[384,1024]{1,0:T(8,128)(2,1)S(1)} %copy-done.26, bf16[384,1024]{1,0:T(8,128)(2,1)S(1)} %copy-done.19, bf16[1,4096,1024]{2,1,0:T(8,128)(2,1)} %gate_weight.3, bf16[1,4096,1024]{2,1,0:T(8,128)(2,1)} %up_weight.3, ...), custom_call_target="tpu_custom_call" | custom-call | flops 26400000000 | tf_op jit(solution)/shard_map/route_grads/pallas_call | solution.py:571
  92.6 3.3 %collective-permute-done.29 = bf16[2,96,512]{2,1,0:T(8,128)(2,1)S(1)} collective-permute-done((bf16[2,96,512]{2,1,0:T(8,128)(2,1)S(1)}, bf16[2,96,512]{2,1,0:T(8,128)(2,1)S(1)}, u32[]{:S(2)}, u32[]{:S(2)}) %collective-permute-start.29) | collective-permute-done | bytes 196640 | tf_op jit(solution)/shard_map/ppermute | solution.py:329
  95.9 4.1 %collective-permute-done.30 = bf16[2,96,512]{2,1,0:T(8,128)(2,1)S(1)} collective-permute-done((bf16[2,96,512]{2,1,0:T(8,128)(2,1)S(1)}, bf16[2,96,512]{2,1,0:T(8,128)(2,1)S(1)}, u32[]{:S(2)}, u32[]{:S(2)}) %collective-permute-start.30) | collective-permute-done | bytes 196640 | tf_op jit(solution)/shard_map/ppermute | solution.py:596
  102.8 1.8 collective-permute-start.26
  105.5 2.8 %collective-permute-start.32 = (bf16[96,512]{1,0:T(8,128)(2,1)S(1)}, bf16[96,512]{1,0:T(8,128)(2,1)S(1)}, u32[]{:S(2)}, u32[]{:S(2)}) collective-permute-start(bf16[96,512]{1,0:T(8,128)(2,1)S(1)} %get-tuple-element.98), channel_id=1, source_target_pairs={{0,4},{2,6},{4,0},{6,2},{1,5},{3,7},{5,1},{7,3},{8,12},{10,14},{12... | collective-permute-start | bytes 294920 | tf_op jit(solution)/shard_map/ppermute | solution.py:329
  109.9 2.6 %collective-permute-start.33 = (bf16[96,512]{1,0:T(8,128)(2,1)S(1)}, bf16[96,512]{1,0:T(8,128)(2,1)S(1)}, u32[]{:S(2)}, u32[]{:S(2)}) collective-permute-start(bf16[96,512]{1,0:T(8,128)(2,1)S(1)} %get-tuple-element.97), channel_id=1, source_target_pairs={{0,6},{2,4},{4,2},{6,0},{1,7},{3,5},{5,3},{7,1},{8,14},{10,12},{12... | collective-permute-start | bytes 294920 | tf_op jit(solution)/shard_map/ppermute | solution.py:329
  114.7 1.9 %collective-permute-start.28 = (bf16[96,512]{1,0:T(8,128)(2,1)S(1)}, bf16[96,512]{1,0:T(8,128)(2,1)S(1)}, u32[]{:S(2)}, u32[]{:S(2)}) collective-permute-start(bf16[96,512]{1,0:T(8,128)(2,1)S(1)} %get-tuple-element.99), channel_id=1, source_target_pairs={{0,2},{2,0},{4,6},{6,4},{1,3},{3,1},{5,7},{7,5},{8,10},{10,8},{12,... | collective-permute-start | bytes 294920 | tf_op jit(solution)/shard_map/ppermute | solution.py:329
  117.5 1.8 %collective-permute-done.28.refs_3_ = bf16[96,512]{1,0:T(8,128)(2,1)S(1)} collective-permute-done((bf16[96,512]{1,0:T(8,128)(2,1)S(1)}, bf16[96,512]{1,0:T(8,128)(2,1)S(1)}, u32[]{:S(2)}, u32[]{:S(2)}) %collective-permute-start.28) | collective-permute-done | bytes 98336 | tf_op jit(solution)/shard_map/ppermute | solution.py:329
  120.0 2.2 %resid_rows.1.resid_ref.after_ref = bf16[128,512]{1,0:T(8,128)(2,1)} custom-call(f32[128,16]{1,0:T(8,128)} %get-tuple-element.39.refs_0_.refs_1_, bf16[128,512]{1,0:T(8,128)(2,1)} %refs_1_.3, bf16[96,512]{1,0:T(8,128)(2,1)} %get-tuple-element.100.refs_2_, bf16[96,512]{1,0:T(8,128)(2,1)} %copy-done.37, bf16[96,512]{1,0:T(8,128)(2,1)} %copy-done.35, ...), custom_call_target="tpu_custom_call" | custom-call | flops 6600000000 | tf_op jit(solution)/shard_map/resid_rows/pallas_call | solution.py:55
  122.2 3.4 %copy-done.6 = bf16[8192,512]{1,0:T(8,128)(2,1)S(1)} copy-done((bf16[8192,512]{1,0:T(8,128)(2,1)S(1)}, bf16[8192,512]{1,0:T(8,128)(2,1)}, u32[]{:S(2)}) %copy-start.6) | copy-done | bytes 8388632
  137.1 2.7 %collective-permute-start.48 = (bf16[1024,128]{1,0:T(8,128)(2,1)S(1)}, bf16[1024,128]{1,0:T(8,128)(2,1)S(1)}, u32[]{:S(2)}, u32[]{:S(2)}) collective-permute-start(bf16[1024,128]{1,0:T(8,128)(2,1)S(1)} %add_convert_fusion), channel_id=1, source_target_pairs={{0,6},{2,4},{4,2},{6,0},{1,7},{3,5},{5,3},{7,1},{8,14},{10,12},{12... | collective-permute-start | bytes 786440 | tf_op jit(solution)/shard_map/ppermute | solution.py:329
  139.8 2.8 %collective-permute-done.45 = bf16[1024,128]{1,0:T(8,128)(2,1)S(1)} collective-permute-done((bf16[1024,128]{1,0:T(8,128)(2,1)S(1)}, bf16[1024,128]{1,0:T(8,128)(2,1)S(1)}, u32[]{:S(2)}, u32[]{:S(2)}) %collective-permute-start.45) | collective-permute-done | bytes 262176 | tf_op jit(solution)/shard_map/ppermute | solution.py:329
  142.8 3.2 %collective-permute-start.46 = (bf16[1024,128]{1,0:T(8,128)(2,1)S(1)}, bf16[1024,128]{1,0:T(8,128)(2,1)S(1)}, u32[]{:S(2)}, u32[]{:S(2)}) collective-permute-start(bf16[1024,128]{1,0:T(8,128)(2,1)S(1)} %add_convert_fusion.1), channel_id=1, source_target_pairs={{0,4},{2,6},{4,0},{6,2},{1,5},{3,7},{5,1},{7,3},{8,12},{10,14},{12... | collective-permute-start | bytes 786440 | tf_op jit(solution)/shard_map/ppermute | solution.py:329
  146.1 2.2 %collective-permute-start.44 = (bf16[1024,128]{1,0:T(8,128)(2,1)S(1)}, bf16[1024,128]{1,0:T(8,128)(2,1)S(1)}, u32[]{:S(2)}, u32[]{:S(2)}) collective-permute-start(bf16[1024,128]{1,0:T(8,128)(2,1)S(1)} %add_convert_fusion.2), channel_id=1, source_target_pairs={{0,2},{2,0},{4,6},{6,4},{1,3},{3,1},{5,7},{7,5},{8,10},{10,8},{12,... | collective-permute-start | bytes 786440 | tf_op jit(solution)/shard_map/ppermute | solution.py:329
  148.8 2.2 %collective-permute-start.37 = (f32[96]{0:T(128)S(1)}, f32[96]{0:T(128)S(1)}, u32[]{:S(2)}, u32[]{:S(2)}) collective-permute-start(f32[96]{0:T(128)S(1)} %add.98), channel_id=1, source_target_pairs={{0,2},{2,0},{4,6},{6,4},{1,3},{3,1},{5,7},{7,5},{8,10},{10,8},{12,... | collective-permute-start | bytes 1160 | tf_op jit(solution)/shard_map/ppermute | solution.py:329
  154.1 1.7 collective-permute-start.39
  155.8 1.8 collective-permute-done.46.refs_11_
  157.6 6.7 %scan_local.1 = (bf16[1024,128]{1,0:T(8,128)(2,1)}, f32[1024,128]{1,0:T(8,128)S(1)}, f32[33,8,128]{2,1,0:T(8,128)S(1)}) custom-call(f32[1024,128]{1,0:T(8,128)S(1)} %copy-done.23, f32[1024,128]{1,0:T(8,128)S(1)} %copy-done.24, f32[1024,128]{1,0:T(8,128)S(1)} %copy-done.21, f32[1024,128]{1,0:T(8,128)S(1)} %copy-done.22, ...), custom_call_target="tpu_custom_call" | custom-call | flops 19800000512 | tf_op jit(solution)/shard_map/scan_local/pallas_call | solution.py:55
  168.2 3.3 %collective-permute-done.50 = f32[33,8,128]{2,1,0:T(8,128)S(1)} collective-permute-done((f32[33,8,128]{2,1,0:T(8,128)S(1)}, f32[33,8,128]{2,1,0:T(8,128)S(1)}, u32[]{:S(2)}, u32[]{:S(2)}) %collective-permute-start.50) | collective-permute-done | bytes 135200 | tf_op jit(solution)/shard_map/ppermute | solution.py:329
  173.1 7.3 %scan_adjoint.1 = (bf16[1024,128]{1,0:T(8,128)(2,1)}, bf16[1024,128]{1,0:T(8,128)(2,1)}) custom-call(f32[16,8,128]{2,1,0:T(8,128)S(1)} %get-tuple-element.90.refs_0_, f32[1024,128]{1,0:T(8,128)S(1)} %get-tuple-element.65.refs_1_, f32[1024,128]{1,0:T(8,128)S(1)} %copy-done.21, f32[1024,128]{1,0:T(8,128)S(1)} %copy-done.22, ...), custom_call_target="tpu_custom_call" | custom-call | flops 23100000256 | tf_op jit(solution)/shard_map/scan_adjoint/pallas_call | solution.py:55
  (198 shorter events, 59.5 us)
Async XLA Ops:
  7.6 18.4 %collective-permute-start = (bf16[2,96,512]{2,1,0:T(8,128)(2,1)}, bf16[2,96,512]{2,1,0:T(8,128)(2,1)S(1)}, u32[]{:S(2)}, u32[]{:S(2)}) collective-permute-start(bf16[2,96,512]{2,1,0:T(8,128)(2,1)} %get-tuple-element.41.refs_0_), channel_id=1, source_target_pairs={{0,1},{1,0},{2,3},{3,2},{4,5},{5,4},{6,7},{7,6},{8,9},{9,8},{10,11... | collective-permute-start | bytes 589832 | tf_op jit(solution)/shard_map/ppermute | solution.py:329
  10.6 17.5 %collective-permute-start.1 = (bf16[2,96,512]{2,1,0:T(8,128)(2,1)}, bf16[2,96,512]{2,1,0:T(8,128)(2,1)S(1)}, u32[]{:S(2)}, u32[]{:S(2)}) collective-permute-start(bf16[2,96,512]{2,1,0:T(8,128)(2,1)} %get-tuple-element.41.refs_0_), channel_id=1, source_target_pairs={{0,16},{16,0},{1,17},{17,1},{2,18},{18,2},{3,19},{19,3},{4,20},{20... | collective-permute-start | bytes 589832 | tf_op jit(solution)/shard_map/ppermute | solution.py:329
  12.2 12.7 %collective-permute-start.5 = (bf16[2,96,512]{2,1,0:T(8,128)(2,1)}, bf16[2,96,512]{2,1,0:T(8,128)(2,1)S(1)}, u32[]{:S(2)}, u32[]{:S(2)}) collective-permute-start(bf16[2,96,512]{2,1,0:T(8,128)(2,1)} %get-tuple-element.38.refs_5_), channel_id=1, source_target_pairs={{0,2},{2,0},{4,6},{6,4},{1,3},{3,1},{5,7},{7,5},{8,10},{10,8},{12,... | collective-permute-start | bytes 589832 | tf_op jit(solution)/shard_map/ppermute | solution.py:329
  13.7 12.8 %collective-permute-start.11 = (bf16[2,96,512]{2,1,0:T(8,128)(2,1)}, bf16[2,96,512]{2,1,0:T(8,128)(2,1)S(1)}, u32[]{:S(2)}, u32[]{:S(2)}) collective-permute-start(bf16[2,96,512]{2,1,0:T(8,128)(2,1)} %get-tuple-element.42), channel_id=1, source_target_pairs={{0,6},{2,4},{4,2},{6,0},{1,7},{3,5},{5,3},{7,1},{8,14},{10,12},{12... | collective-permute-start | bytes 589832 | tf_op jit(solution)/shard_map/ppermute | solution.py:329
  16.2 17.0 %collective-permute-start.17 = (bf16[2,96,512]{2,1,0:T(8,128)(2,1)}, bf16[2,96,512]{2,1,0:T(8,128)(2,1)S(1)}, u32[]{:S(2)}, u32[]{:S(2)}) collective-permute-start(bf16[2,96,512]{2,1,0:T(8,128)(2,1)} %get-tuple-element.43), channel_id=1, source_target_pairs={{0,4},{2,6},{4,0},{6,2},{1,5},{3,7},{5,1},{7,3},{8,12},{10,14},{12... | collective-permute-start | bytes 589832 | tf_op jit(solution)/shard_map/ppermute | solution.py:329
  25.5 8.2 %collective-permute-start.7 = (bf16[2,96,512]{2,1,0:T(8,128)(2,1)}, bf16[2,96,512]{2,1,0:T(8,128)(2,1)S(1)}, u32[]{:S(2)}, u32[]{:S(2)}) collective-permute-start(bf16[2,96,512]{2,1,0:T(8,128)(2,1)} %follow.1.refs_6_), channel_id=1, source_target_pairs={{0,16},{16,0},{1,17},{17,1},{2,18},{18,2},{3,19},{19,3},{4,20},{20... | collective-permute-start | bytes 589832 | tf_op jit(solution)/shard_map/ppermute | solution.py:329
  26.0 8.3 %collective-permute-start.6 = (bf16[2,96,512]{2,1,0:T(8,128)(2,1)}, bf16[2,96,512]{2,1,0:T(8,128)(2,1)S(1)}, u32[]{:S(2)}, u32[]{:S(2)}) collective-permute-start(bf16[2,96,512]{2,1,0:T(8,128)(2,1)} %follow.1.refs_6_), channel_id=1, source_target_pairs={{0,1},{1,0},{2,3},{3,2},{4,5},{5,4},{6,7},{7,6},{8,9},{9,8},{10,11... | collective-permute-start | bytes 589832 | tf_op jit(solution)/shard_map/ppermute | solution.py:329
  26.6 10.4 %collective-permute-start.13 = (bf16[2,96,512]{2,1,0:T(8,128)(2,1)S(1)}, bf16[2,96,512]{2,1,0:T(8,128)(2,1)S(1)}, u32[]{:S(2)}, u32[]{:S(2)}) collective-permute-start(bf16[2,96,512]{2,1,0:T(8,128)(2,1)S(1)} %collective-permute-done.11.refs_12_), channel_id=1, source_target_pairs={{0,16},{16,0},{1,17},{17,1},{2,18},{18,2},{3,19},{19,3},{4,20},{20... | collective-permute-start | bytes 589832 | tf_op jit(solution)/shard_map/ppermute | solution.py:329
  28.1 9.1 %collective-permute-start.12 = (bf16[2,96,512]{2,1,0:T(8,128)(2,1)S(1)}, bf16[2,96,512]{2,1,0:T(8,128)(2,1)S(1)}, u32[]{:S(2)}, u32[]{:S(2)}) collective-permute-start(bf16[2,96,512]{2,1,0:T(8,128)(2,1)S(1)} %collective-permute-done.11.refs_12_), channel_id=1, source_target_pairs={{0,1},{1,0},{2,3},{3,2},{4,5},{5,4},{6,7},{7,6},{8,9},{9,8},{10,11... | collective-permute-start | bytes 589832 | tf_op jit(solution)/shard_map/ppermute | solution.py:329
  33.2 8.4 %collective-permute-start.18 = (bf16[2,96,512]{2,1,0:T(8,128)(2,1)S(1)}, bf16[2,96,512]{2,1,0:T(8,128)(2,1)S(1)}, u32[]{:S(2)}, u32[]{:S(2)}) collective-permute-start(bf16[2,96,512]{2,1,0:T(8,128)(2,1)S(1)} %collective-permute-done.17.refs_18_), channel_id=1, source_target_pairs={{0,1},{1,0},{2,3},{3,2},{4,5},{5,4},{6,7},{7,6},{8,9},{9,8},{10,11... | collective-permute-start | bytes 589832 | tf_op jit(solution)/shard_map/ppermute | solution.py:329
  34.4 9.5 %collective-permute-start.19 = (bf16[2,96,512]{2,1,0:T(8,128)(2,1)S(1)}, bf16[2,96,512]{2,1,0:T(8,128)(2,1)S(1)}, u32[]{:S(2)}, u32[]{:S(2)}) collective-permute-start(bf16[2,96,512]{2,1,0:T(8,128)(2,1)S(1)} %collective-permute-done.17.refs_18_), channel_id=1, source_target_pairs={{0,16},{16,0},{1,17},{17,1},{2,18},{18,2},{3,19},{19,3},{4,20},{20... | collective-permute-start | bytes 589832 | tf_op jit(solution)/shard_map/ppermute | solution.py:329
  37.0 12.5 %collective-permute-start.3 = (bf16[3,2,96,512]{3,2,1,0:T(8,128)(2,1)S(1)}, bf16[3,2,96,512]{3,2,1,0:T(8,128)(2,1)S(1)}, u32[]{:S(2)}, u32[]{:S(2)}) collective-permute-start(bf16[3,2,96,512]{3,2,1,0:T(8,128)(2,1)S(1)} %pad_maximum_fusion), channel_id=1, source_target_pairs={{0,8},{8,0},{1,9},{9,1},{2,10},{10,2},{3,11},{11,3},{4,12},{12,4},... | collective-permute-start | bytes 1769480 | tf_op jit(solution)/shard_map/ppermute | solution.py:329
  51.5 24.0 %collective-permute-start.40 = (f32[32,8,128]{2,1,0:T(8,128)S(1)}, f32[32,8,128]{2,1,0:T(8,128)}, u32[]{:S(2)}, u32[]{:S(2)}) collective-permute-start(f32[32,8,128]{2,1,0:T(8,128)S(1)} %copy-done.3), channel_id=1, source_target_pairs={{0,8},{8,0},{1,9},{9,1},{2,10},{10,2},{3,11},{11,3},{4,12},{12,4},... | collective-permute-start | bytes 393224 | tf_op jit(solution)/shard_map/ppermute | solution.py:329
  78.7 9.4 %collective-permute-start.34 = (f32[2,96]{1,0:T(2,128)S(1)}, f32[2,96]{1,0:T(2,128)S(1)}, u32[]{:S(2)}, u32[]{:S(2)}) collective-permute-start(f32[2,96]{1,0:T(2,128)S(1)} %slice.112), channel_id=1, source_target_pairs={{0,8},{8,0},{1,9},{9,1},{2,10},{10,2},{3,11},{11,3},{4,12},{12,4},... | collective-permute-start | bytes 2312 | tf_op jit(solution)/shard_map/ppermute | solution.py:329
  87.9 13.6 %collective-permute-start.24 = (bf16[2,2,2,96,512]{4,3,2,1,0:T(8,128)(2,1)S(1)}, bf16[2,2,2,96,512]{4,3,2,1,0:T(8,128)(2,1)S(1)}, u32[]{:S(2)}, u32[]{:S(2)}) collective-permute-start(bf16[2,2,2,96,512]{4,3,2,1,0:T(8,128)(2,1)S(1)} %get-tuple-element.50), channel_id=1, source_target_pairs={{0,8},{8,0},{1,9},{9,1},{2,10},{10,2},{3,11},{11,3},{4,12},{12,4},... | collective-permute-start | bytes 2359304 | tf_op jit(solution)/shard_map/ppermute | solution.py:329
  89.4 10.6 %collective-permute-start.30 = (bf16[2,96,512]{2,1,0:T(8,128)(2,1)S(1)}, bf16[2,96,512]{2,1,0:T(8,128)(2,1)S(1)}, u32[]{:S(2)}, u32[]{:S(2)}) collective-permute-start(bf16[2,96,512]{2,1,0:T(8,128)(2,1)S(1)} %get-tuple-element.85), channel_id=1, source_target_pairs={{0,17},{1,16},{16,1},{17,0},{2,19},{3,18},{18,3},{19,2},{4,21},{5,... | collective-permute-start | bytes 589832 | tf_op jit(solution)/shard_map/ppermute | solution.py:596
  90.6 10.8 %collective-permute-start.31 = (bf16[2,96,512]{2,1,0:T(8,128)(2,1)S(1)}, bf16[2,96,512]{2,1,0:T(8,128)(2,1)S(1)}, u32[]{:S(2)}, u32[]{:S(2)}) collective-permute-start(bf16[2,96,512]{2,1,0:T(8,128)(2,1)S(1)} %get-tuple-element.84), channel_id=1, source_target_pairs={{0,16},{16,0},{1,17},{17,1},{2,18},{18,2},{3,19},{19,3},{4,20},{20... | collective-permute-start | bytes 589832 | tf_op jit(solution)/shard_map/ppermute | solution.py:329
  91.7 25.0 %collective-permute-start.35 = (f32[96]{0:T(128)S(1)}, f32[96]{0:T(128)S(1)}, u32[]{:S(2)}, u32[]{:S(2)}) collective-permute-start(f32[96]{0:T(128)S(1)} %slice_bitcast_fusion.12), channel_id=1, source_target_pairs={{0,16},{16,0},{1,17},{17,1},{2,18},{18,2},{3,19},{19,3},{4,20},{20... | collective-permute-start | bytes 1160 | tf_op jit(solution)/shard_map/ppermute | solution.py:329
  102.8 9.8 %collective-permute-start.26 = (bf16[2,96,512]{2,1,0:T(8,128)(2,1)S(1)}, bf16[2,96,512]{2,1,0:T(8,128)(2,1)S(1)}, u32[]{:S(2)}, u32[]{:S(2)}) collective-permute-start(bf16[2,96,512]{2,1,0:T(8,128)(2,1)S(1)} %get-tuple-element.88), channel_id=1, source_target_pairs={{0,17},{1,16},{16,1},{17,0},{2,19},{3,18},{18,3},{19,2},{4,21},{5,... | collective-permute-start | bytes 589832 | tf_op jit(solution)/shard_map/ppermute | solution.py:596
  104.6 9.4 %collective-permute-start.27 = (bf16[2,96,512]{2,1,0:T(8,128)(2,1)S(1)}, bf16[2,96,512]{2,1,0:T(8,128)(2,1)S(1)}, u32[]{:S(2)}, u32[]{:S(2)}) collective-permute-start(bf16[2,96,512]{2,1,0:T(8,128)(2,1)S(1)} %get-tuple-element.87), channel_id=1, source_target_pairs={{0,16},{16,0},{1,17},{17,1},{2,18},{18,2},{3,19},{19,3},{4,20},{20... | collective-permute-start | bytes 589832 | tf_op jit(solution)/shard_map/ppermute | solution.py:329
  105.5 12.0 %collective-permute-start.32 = (bf16[96,512]{1,0:T(8,128)(2,1)S(1)}, bf16[96,512]{1,0:T(8,128)(2,1)S(1)}, u32[]{:S(2)}, u32[]{:S(2)}) collective-permute-start(bf16[96,512]{1,0:T(8,128)(2,1)S(1)} %get-tuple-element.98), channel_id=1, source_target_pairs={{0,4},{2,6},{4,0},{6,2},{1,5},{3,7},{5,1},{7,3},{8,12},{10,14},{12... | collective-permute-start | bytes 294920 | tf_op jit(solution)/shard_map/ppermute | solution.py:329
  116.7 31.6 %collective-permute-start.36 = (f32[96]{0:T(128)S(1)}, f32[96]{0:T(128)S(1)}, u32[]{:S(2)}, u32[]{:S(2)}) collective-permute-start(f32[96]{0:T(128)S(1)} %bitcast_add_fusion), channel_id=1, source_target_pairs={{0,1},{1,0},{2,3},{3,2},{4,5},{5,4},{6,7},{7,6},{8,9},{9,8},{10,11... | collective-permute-start | bytes 1160 | tf_op jit(solution)/shard_map/ppermute | solution.py:329
  127.7 9.3 %collective-permute-start.47 = (bf16[1024,128]{1,0:T(8,128)(2,1)S(1)}, bf16[1024,128]{1,0:T(8,128)(2,1)S(1)}, u32[]{:S(2)}, u32[]{:S(2)}) collective-permute-start(bf16[1024,128]{1,0:T(8,128)(2,1)S(1)} %get-tuple-element.56.after_ref), channel_id=1, source_target_pairs={{0,1},{1,0},{2,3},{3,2},{4,5},{5,4},{6,7},{7,6},{8,9},{9,8},{10,11... | collective-permute-start | bytes 786440 | tf_op jit(solution)/shard_map/ppermute | solution.py:329
  130.2 12.4 %collective-permute-start.45 = (bf16[1024,128]{1,0:T(8,128)(2,1)S(1)}, bf16[1024,128]{1,0:T(8,128)(2,1)S(1)}, u32[]{:S(2)}, u32[]{:S(2)}) collective-permute-start(bf16[1024,128]{1,0:T(8,128)(2,1)S(1)} %get-tuple-element.57.after_ref), channel_id=1, source_target_pairs={{0,1},{1,0},{2,3},{3,2},{4,5},{5,4},{6,7},{7,6},{8,9},{9,8},{10,11... | collective-permute-start | bytes 786440 | tf_op jit(solution)/shard_map/ppermute | solution.py:329
  132.4 13.6 %collective-permute-start.43 = (bf16[1024,128]{1,0:T(8,128)(2,1)S(1)}, bf16[1024,128]{1,0:T(8,128)(2,1)S(1)}, u32[]{:S(2)}, u32[]{:S(2)}) collective-permute-start(bf16[1024,128]{1,0:T(8,128)(2,1)S(1)} %get-tuple-element.58.after_ref), channel_id=1, source_target_pairs={{0,1},{1,0},{2,3},{3,2},{4,5},{5,4},{6,7},{7,6},{8,9},{9,8},{10,11... | collective-permute-start | bytes 786440 | tf_op jit(solution)/shard_map/ppermute | solution.py:329
  134.9 13.9 %collective-permute-start.42 = (bf16[1024,128]{1,0:T(8,128)(2,1)S(1)}, bf16[1024,128]{1,0:T(8,128)(2,1)S(1)}, u32[]{:S(2)}, u32[]{:S(2)}) collective-permute-start(bf16[1024,128]{1,0:T(8,128)(2,1)S(1)} %get-tuple-element.60), channel_id=1, source_target_pairs={{0,1},{1,0},{2,3},{3,2},{4,5},{5,4},{6,7},{7,6},{8,9},{9,8},{10,11... | collective-permute-start | bytes 786440 | tf_op jit(solution)/shard_map/ppermute | solution.py:329
  137.1 17.0 %collective-permute-start.48 = (bf16[1024,128]{1,0:T(8,128)(2,1)S(1)}, bf16[1024,128]{1,0:T(8,128)(2,1)S(1)}, u32[]{:S(2)}, u32[]{:S(2)}) collective-permute-start(bf16[1024,128]{1,0:T(8,128)(2,1)S(1)} %add_convert_fusion), channel_id=1, source_target_pairs={{0,6},{2,4},{4,2},{6,0},{1,7},{3,5},{5,3},{7,1},{8,14},{10,12},{12... | collective-permute-start | bytes 786440 | tf_op jit(solution)/shard_map/ppermute | solution.py:329
  142.8 14.8 %collective-permute-start.46 = (bf16[1024,128]{1,0:T(8,128)(2,1)S(1)}, bf16[1024,128]{1,0:T(8,128)(2,1)S(1)}, u32[]{:S(2)}, u32[]{:S(2)}) collective-permute-start(bf16[1024,128]{1,0:T(8,128)(2,1)S(1)} %add_convert_fusion.1), channel_id=1, source_target_pairs={{0,4},{2,6},{4,0},{6,2},{1,5},{3,7},{5,1},{7,3},{8,12},{10,14},{12... | collective-permute-start | bytes 786440 | tf_op jit(solution)/shard_map/ppermute | solution.py:329
  146.1 11.5 %collective-permute-start.44 = (bf16[1024,128]{1,0:T(8,128)(2,1)S(1)}, bf16[1024,128]{1,0:T(8,128)(2,1)S(1)}, u32[]{:S(2)}, u32[]{:S(2)}) collective-permute-start(bf16[1024,128]{1,0:T(8,128)(2,1)S(1)} %add_convert_fusion.2), channel_id=1, source_target_pairs={{0,2},{2,0},{4,6},{6,4},{1,3},{3,1},{5,7},{7,5},{8,10},{10,8},{12,... | collective-permute-start | bytes 786440 | tf_op jit(solution)/shard_map/ppermute | solution.py:329
  148.8 15.6 %collective-permute-start.37 = (f32[96]{0:T(128)S(1)}, f32[96]{0:T(128)S(1)}, u32[]{:S(2)}, u32[]{:S(2)}) collective-permute-start(f32[96]{0:T(128)S(1)} %add.98), channel_id=1, source_target_pairs={{0,2},{2,0},{4,6},{6,4},{1,3},{3,1},{5,7},{7,5},{8,10},{10,8},{12,... | collective-permute-start | bytes 1160 | tf_op jit(solution)/shard_map/ppermute | solution.py:329
  153.4 11.0 %collective-permute-start.38 = (f32[96]{0:T(128)S(1)}, f32[96]{0:T(128)S(1)}, u32[]{:S(2)}, u32[]{:S(2)}) collective-permute-start(f32[96]{0:T(128)S(1)} %add.98), channel_id=1, source_target_pairs={{0,4},{2,6},{4,0},{6,2},{1,5},{3,7},{5,1},{7,3},{8,12},{10,14},{12... | collective-permute-start | bytes 1160 | tf_op jit(solution)/shard_map/ppermute | solution.py:329
  154.1 10.3 %collective-permute-start.39 = (f32[96]{0:T(128)S(1)}, f32[96]{0:T(128)S(1)}, u32[]{:S(2)}, u32[]{:S(2)}) collective-permute-start(f32[96]{0:T(128)S(1)} %add.98), channel_id=1, source_target_pairs={{0,6},{2,4},{4,2},{6,0},{1,7},{3,5},{5,3},{7,1},{8,14},{10,12},{12... | collective-permute-start | bytes 1160 | tf_op jit(solution)/shard_map/ppermute | solution.py:329
  (57 other events, 400.7 us)

commit v3 on v2

--- a/solution.py
+++ b/solution.py
@@ -119,7 +119,7 @@
     copies = []
     for chunk in range(CHUNKS):
         low = chunk * span
-        carry = lax.fori_loop(low, low + span, advance, carry, unroll=4)
+        carry = lax.fori_loop(low, low + span, advance, carry, unroll=8)
         part = pl.ds(low, span)
         copies.append(
             pltpu.make_async_copy(kept_rows.at[part], kept_ref.at[part], copied.at[chunk])
@@ -215,7 +215,7 @@
     carry = ((zero,) * count, (zero,) * count, zero)
     for turn, copy in enumerate(copies):
         copy.wait()
-        carry = lax.fori_loop(turn * span, (turn + 1) * span, advance, carry, unroll=4)
+        carry = lax.fori_loop(turn * span, (turn + 1) * span, advance, carry, unroll=8)
     terms, moments, skips = carry
     for n in range(count):
         sums_ref[n] = terms[n]
@@ -291,7 +291,7 @@
     later = tuple(incoming_ref[n] for n in range(count))
     for turn, copy in enumerate(copies):
         copy.wait()
-        later = lax.fori_loop(turn * span, (turn + 1) * span, advance, later, unroll=4)
+        later = lax.fori_loop(turn * span, (turn + 1) * span, advance, later, unroll=8)
     for g in range(groups):
         part = slice(g * LANES, (g + 1) * LANES)
         input_out[part, :] = in_rows[pl.ds(g, tokens, stride=groups), :].T.astype(input_out.dtype)
@@ -631,7 +631,7 @@
         [],
         2,
         "resid_rows",
-        63,
+        44,
     )[0]
 
 

time: 182 us -> 176 us (0.967)
  local copies, waits for them, and re-layouts: 10.2 us -> 5.71 us
    unnamed x77 -> x71, local copies, waits for them, and re-layouts: 8.17 us -> 4.38 us
  transfers between devices with their start and end apart: 51 -> 51, of which waited for: 23 -> 25; matrix products, arithmetic and copies ran while one was open for 4% -> 3% of each run, Pallas kernels for 29% -> 30%
where the time goes in v3:
time: 176 us; the launch traced here: 175 us
  Pallas kernels  64.9 us (37%)
  starting transfers between devices  54.2 us (31%)
  waiting for transfers between devices  41.5 us (24%)
  other arithmetic  7.36 us (4%)
  local copies, waits for them, and re-layouts  5.71 us (3%)
    ppermute x49, starting transfers between devices, swap(): lax.ppermute(value, axis, [(place, place ^ distance) for place in range(c...  51.5 us
    ppermute x49, waiting for transfers between devices, swap(): lax.ppermute(value, axis, [(place, place ^ distance) for place in range(c...  37.3 us
    pallas_call x8, Pallas kernels, staged_call(): pl.pallas_call(body, grid=(1,), out_shape=tuple((out for out, kind in out...  30.4 us
    pallas_call x1, Pallas kernels, gather_call(): pl.pallas_call(functools.partial(gather_kernel, groups, blocks, first, la...  15.6 us
    pallas_call x2, Pallas kernels, return_call(): pl.pallas_call(functools.partial(return_kernel, row_count), out_shape=(ja...  14 us
    pallas_call x4, Pallas kernels, project_call(): pl.pallas_call(project_kernel, out_shape=(jax.ShapeDtypeStruct(shape, jnp...  4.95 us
    unnamed x71, local copies, waits for them, and re-layouts  4.38 us
    ppermute x2, waiting for transfers between devices, corner_swap(): return lax.ppermute(value, ('row', 'half'), pairs)  4.18 us
  transfers between devices with their start and end apart: 51, of which 25 were waited for; matrix products, arithmetic and copies ran while one was open for 3% of the time, Pallas kernels for 30%

profile of v3, /device:TPU:0, one launch (start us, length us, event | category | flops | bytes accessed | tf_op | source)
XLA Modules:
  0.0 175.0 jit_solution(18329309375384441745)
XLA Ops:
  1.8 2.8 %route_rows.1 = (bf16[2,96,512]{2,1,0:T(8,128)(2,1)}, bf16[2,96,512]{2,1,0:T(8,128)(2,1)}, bf16[2,96,512]{2,1,0:T(8,128)(2,1)}) custom-call(s32[14]{0:T(128)} %dynamic-slice_bitcast_fusion.refs_0_.places_ref, s32[2,128]{1,0:T(2,128)} %bitcast.85, f32[2,128]{1,0:T(2,128)} %bitcast.87, bf16[128,512]{1,0:T(8,128)(2,1)} %refs_3_.4, bf16[128,512]{1,0:T(8,128)(2,1)} %refs_1_.3), custom_call_target="tpu_custom_call" | custom-call | flops 3300000000 | tf_op jit(solution)/shard_map/route_rows/pallas_call | solution.py:55
  4.8 2.8 %route_own.1 = (bf16[2,96,512]{2,1,0:T(8,128)(2,1)}, f32[128,16]{1,0:T(8,128)}) custom-call(s32[14]{0:T(128)} %dynamic-slice_bitcast_fusion.refs_0_.places_ref, s32[2,128]{1,0:T(2,128)} %bitcast.86, f32[2,128]{1,0:T(2,128)} %bitcast.88, bf16[128,512]{1,0:T(8,128)(2,1)} %refs_3_.4, bf16[128,512]{1,0:T(8,128)(2,1)} %refs_1_.3, ...), custom_call_target="tpu_custom_call" | custom-call | flops 3300000000 | tf_op jit(solution)/shard_map/route_own/pallas_call | solution.py:55
  7.6 3.0 %collective-permute-start = (bf16[2,96,512]{2,1,0:T(8,128)(2,1)}, bf16[2,96,512]{2,1,0:T(8,128)(2,1)S(1)}, u32[]{:S(2)}, u32[]{:S(2)}) collective-permute-start(bf16[2,96,512]{2,1,0:T(8,128)(2,1)} %get-tuple-element.41.refs_0_), channel_id=1, source_target_pairs={{0,1},{1,0},{2,3},{3,2},{4,5},{5,4},{6,7},{7,6},{8,9},{9,8},{10,11... | collective-permute-start | bytes 589832 | tf_op jit(solution)/shard_map/ppermute | solution.py:329
  12.1 1.6 collective-permute-start.5
  13.7 2.5 %collective-permute-start.11 = (bf16[2,96,512]{2,1,0:T(8,128)(2,1)}, bf16[2,96,512]{2,1,0:T(8,128)(2,1)S(1)}, u32[]{:S(2)}, u32[]{:S(2)}) collective-permute-start(bf16[2,96,512]{2,1,0:T(8,128)(2,1)} %get-tuple-element.42), channel_id=1, source_target_pairs={{0,6},{2,4},{4,2},{6,0},{1,7},{3,5},{5,3},{7,1},{8,14},{10,12},{12... | collective-permute-start | bytes 589832 | tf_op jit(solution)/shard_map/ppermute | solution.py:329
  16.4 7.6 %scan_forward.1 = (f32[128,16,8,128]{3,2,1,0:T(8,128)}, f32[1024,128]{1,0:T(8,128)}, f32[1024,128]{1,0:T(8,128)}, f32[1024,128]{1,0:T(8,128)}, f32[1024,128]{1,0:T(8,128)}, /*index=5*/f32[32,8,128]{2,1,0:T(8,128)S(1)}) custom-call(bf16[1024,128]{1,0:T(8,128)(2,1)S(1)} %copy-done.6, bf16[1024,128]{1,0:T(8,128)(2,1)S(1)} %copy-done.8, ...), custom_call_target="tpu_custom_call" | custom-call | flops 23100000256 | tf_op jit(solution)/shard_map/scan_forward/pallas_call | solution.py:55
  29.4 3.9 %collective-permute-done.17.refs_18_ = bf16[2,96,512]{2,1,0:T(8,128)(2,1)S(1)} collective-permute-done((bf16[2,96,512]{2,1,0:T(8,128)(2,1)}, bf16[2,96,512]{2,1,0:T(8,128)(2,1)S(1)}, u32[]{:S(2)}, u32[]{:S(2)}) %collective-permute-start.17) | collective-permute-done | bytes 196640 | tf_op jit(solution)/shard_map/ppermute | solution.py:329
  34.4 1.6 collective-permute-start.19
  37.1 1.6 collective-permute-start.8
  38.7 2.9 %collective-permute-done.2.refs_3_ = bf16[2,96,512]{2,1,0:T(8,128)(2,1)S(1)} collective-permute-done((bf16[2,96,512]{2,1,0:T(8,128)(2,1)S(1)}, bf16[2,96,512]{2,1,0:T(8,128)(2,1)S(1)}, u32[]{:S(2)}, u32[]{:S(2)}) %collective-permute-start.2) | collective-permute-done | bytes 196640 | tf_op jit(solution)/shard_map/ppermute | solution.py:329
  44.8 4.0 %collective-permute-done.14.refs_15_ = bf16[2,96,512]{2,1,0:T(8,128)(2,1)S(1)} collective-permute-done((bf16[2,96,512]{2,1,0:T(8,128)(2,1)S(1)}, bf16[2,96,512]{2,1,0:T(8,128)(2,1)S(1)}, u32[]{:S(2)}, u32[]{:S(2)}) %collective-permute-start.14) | collective-permute-done | bytes 196640 | tf_op jit(solution)/shard_map/ppermute | solution.py:329
  52.6 15.6 %hidden_rows.1 = (bf16[384,1024]{1,0:T(8,128)(2,1)S(1)}, bf16[384,1024]{1,0:T(8,128)(2,1)S(1)}, f32[384,128]{1,0:T(8,128)S(1)}) custom-call(s32[14]{0:T(128)S(1)} %copy-done.16, f32[32,8,128]{2,1,0:T(8,128)S(1)} %copy-done.3, bf16[2,96,512]{2,1,0:T(8,128)(2,1)S(1)} %copy-done.4, bf16[2,96,512]{2,1,0:T(8,128)(2,1)S(1)} %collective-permute-done.refs_1_, ...), custom_call_target="tpu_custom_call" | custom-call | flops 52800000000 | tf_op jit(solution)/shard_map/hidden_rows/pallas_call | solution.py:532
  68.2 7.0 %route_grads.2 = (f32[2,2,2,96,512]{4,3,2,1,0:T(8,128)S(1)}, bf16[2,2,2,96,512]{4,3,2,1,0:T(8,128)(2,1)S(1)}) custom-call(s32[14]{0:T(128)S(1)} %copy-done.16, bf16[384,1024]{1,0:T(8,128)(2,1)S(1)} %get-tuple-element.44.gate_ref, bf16[384,1024]{1,0:T(8,128)(2,1)S(1)} %get-tuple-element.45.up_ref.refs_1_, bf16[1,4096,1024]{2,1,0:T(8,128)(2,1)} %gate_weight.3, ...), custom_call_target="tpu_custom_call" | custom-call | flops 26400000000 | tf_op jit(solution)/shard_map/route_grads/pallas_call | solution.py:571
  77.8 1.5 fusion.14
  79.4 7.0 %route_grads.3 = (f32[2,2,2,96,512]{4,3,2,1,0:T(8,128)S(1)}, bf16[2,2,2,96,512]{4,3,2,1,0:T(8,128)(2,1)S(1)}) custom-call(s32[14]{0:T(128)S(1)} %copy-done.16, bf16[384,1024]{1,0:T(8,128)(2,1)S(1)} %copy-done.26, bf16[384,1024]{1,0:T(8,128)(2,1)S(1)} %copy-done.19, bf16[1,4096,1024]{2,1,0:T(8,128)(2,1)} %gate_weight.3, bf16[1,4096,1024]{2,1,0:T(8,128)(2,1)} %up_weight.3, ...), custom_call_target="tpu_custom_call" | custom-call | flops 26400000000 | tf_op jit(solution)/shard_map/route_grads/pallas_call | solution.py:571
  90.9 3.5 %collective-permute-done.29 = bf16[2,96,512]{2,1,0:T(8,128)(2,1)S(1)} collective-permute-done((bf16[2,96,512]{2,1,0:T(8,128)(2,1)S(1)}, bf16[2,96,512]{2,1,0:T(8,128)(2,1)S(1)}, u32[]{:S(2)}, u32[]{:S(2)}) %collective-permute-start.29) | collective-permute-done | bytes 196640 | tf_op jit(solution)/shard_map/ppermute | solution.py:329
  94.4 4.0 %collective-permute-done.30 = bf16[2,96,512]{2,1,0:T(8,128)(2,1)S(1)} collective-permute-done((bf16[2,96,512]{2,1,0:T(8,128)(2,1)S(1)}, bf16[2,96,512]{2,1,0:T(8,128)(2,1)S(1)}, u32[]{:S(2)}, u32[]{:S(2)}) %collective-permute-start.30) | collective-permute-done | bytes 196640 | tf_op jit(solution)/shard_map/ppermute | solution.py:596
  101.3 1.8 %collective-permute-start.26 = (bf16[2,96,512]{2,1,0:T(8,128)(2,1)S(1)}, bf16[2,96,512]{2,1,0:T(8,128)(2,1)S(1)}, u32[]{:S(2)}, u32[]{:S(2)}) collective-permute-start(bf16[2,96,512]{2,1,0:T(8,128)(2,1)S(1)} %get-tuple-element.88), channel_id=1, source_target_pairs={{0,17},{1,16},{16,1},{17,0},{2,19},{3,18},{18,3},{19,2},{4,21},{5,... | collective-permute-start | bytes 589832 | tf_op jit(solution)/shard_map/ppermute | solution.py:596
  103.9 2.8 %collective-permute-start.32 = (bf16[96,512]{1,0:T(8,128)(2,1)S(1)}, bf16[96,512]{1,0:T(8,128)(2,1)S(1)}, u32[]{:S(2)}, u32[]{:S(2)}) collective-permute-start(bf16[96,512]{1,0:T(8,128)(2,1)S(1)} %get-tuple-element.98), channel_id=1, source_target_pairs={{0,4},{2,6},{4,0},{6,2},{1,5},{3,7},{5,1},{7,3},{8,12},{10,14},{12... | collective-permute-start | bytes 294920 | tf_op jit(solution)/shard_map/ppermute | solution.py:329
  108.2 2.6 %collective-permute-start.33 = (bf16[96,512]{1,0:T(8,128)(2,1)S(1)}, bf16[96,512]{1,0:T(8,128)(2,1)S(1)}, u32[]{:S(2)}, u32[]{:S(2)}) collective-permute-start(bf16[96,512]{1,0:T(8,128)(2,1)S(1)} %get-tuple-element.97), channel_id=1, source_target_pairs={{0,6},{2,4},{4,2},{6,0},{1,7},{3,5},{5,3},{7,1},{8,14},{10,12},{12... | collective-permute-start | bytes 294920 | tf_op jit(solution)/shard_map/ppermute | solution.py:329
  112.6 1.8 %collective-permute-start.28 = (bf16[96,512]{1,0:T(8,128)(2,1)S(1)}, bf16[96,512]{1,0:T(8,128)(2,1)S(1)}, u32[]{:S(2)}, u32[]{:S(2)}) collective-permute-start(bf16[96,512]{1,0:T(8,128)(2,1)S(1)} %get-tuple-element.99), channel_id=1, source_target_pairs={{0,2},{2,0},{4,6},{6,4},{1,3},{3,1},{5,7},{7,5},{8,10},{10,8},{12,... | collective-permute-start | bytes 294920 | tf_op jit(solution)/shard_map/ppermute | solution.py:329
  115.2 2.1 %collective-permute-done.28.refs_3_ = bf16[96,512]{1,0:T(8,128)(2,1)S(1)} collective-permute-done((bf16[96,512]{1,0:T(8,128)(2,1)S(1)}, bf16[96,512]{1,0:T(8,128)(2,1)S(1)}, u32[]{:S(2)}, u32[]{:S(2)}) %collective-permute-start.28) | collective-permute-done | bytes 98336 | tf_op jit(solution)/shard_map/ppermute | solution.py:329
  117.3 2.0 %resid_rows.1.resid_ref.after_ref = bf16[128,512]{1,0:T(8,128)(2,1)} custom-call(f32[128,16]{1,0:T(8,128)S(1)} %copy-done.20, bf16[128,512]{1,0:T(8,128)(2,1)S(1)} %copy-done.9, bf16[96,512]{1,0:T(8,128)(2,1)S(1)} %get-tuple-element.100.refs_2_, bf16[96,512]{1,0:T(8,128)(2,1)S(1)} %collective-permute-done.28.refs_3_, ...), custom_call_target="tpu_custom_call" | custom-call | flops 6600000000 | tf_op jit(solution)/shard_map/resid_rows/pallas_call | solution.py:55
  131.0 2.7 %collective-permute-start.48 = (bf16[1024,128]{1,0:T(8,128)(2,1)S(1)}, bf16[1024,128]{1,0:T(8,128)(2,1)S(1)}, u32[]{:S(2)}, u32[]{:S(2)}) collective-permute-start(bf16[1024,128]{1,0:T(8,128)(2,1)S(1)} %add_convert_fusion), channel_id=1, source_target_pairs={{0,6},{2,4},{4,2},{6,0},{1,7},{3,5},{5,3},{7,1},{8,14},{10,12},{12... | collective-permute-start | bytes 786440 | tf_op jit(solution)/shard_map/ppermute | solution.py:329
  133.7 2.9 %collective-permute-done.45 = bf16[1024,128]{1,0:T(8,128)(2,1)S(1)} collective-permute-done((bf16[1024,128]{1,0:T(8,128)(2,1)S(1)}, bf16[1024,128]{1,0:T(8,128)(2,1)S(1)}, u32[]{:S(2)}, u32[]{:S(2)}) %collective-permute-start.45) | collective-permute-done | bytes 262176 | tf_op jit(solution)/shard_map/ppermute | solution.py:329
  136.7 3.1 %collective-permute-start.46 = (bf16[1024,128]{1,0:T(8,128)(2,1)S(1)}, bf16[1024,128]{1,0:T(8,128)(2,1)S(1)}, u32[]{:S(2)}, u32[]{:S(2)}) collective-permute-start(bf16[1024,128]{1,0:T(8,128)(2,1)S(1)} %add_convert_fusion.1), channel_id=1, source_target_pairs={{0,4},{2,6},{4,0},{6,2},{1,5},{3,7},{5,1},{7,3},{8,12},{10,14},{12... | collective-permute-start | bytes 786440 | tf_op jit(solution)/shard_map/ppermute | solution.py:329
  139.8 1.9 %collective-permute-start.44 = (bf16[1024,128]{1,0:T(8,128)(2,1)S(1)}, bf16[1024,128]{1,0:T(8,128)(2,1)S(1)}, u32[]{:S(2)}, u32[]{:S(2)}) collective-permute-start(bf16[1024,128]{1,0:T(8,128)(2,1)S(1)} %add_convert_fusion.2), channel_id=1, source_target_pairs={{0,2},{2,0},{4,6},{6,4},{1,3},{3,1},{5,7},{7,5},{8,10},{10,8},{12,... | collective-permute-start | bytes 786440 | tf_op jit(solution)/shard_map/ppermute | solution.py:329
  142.3 2.1 %collective-permute-start.37 = (f32[96]{0:T(128)S(1)}, f32[96]{0:T(128)S(1)}, u32[]{:S(2)}, u32[]{:S(2)}) collective-permute-start(f32[96]{0:T(128)S(1)} %add.98), channel_id=1, source_target_pairs={{0,2},{2,0},{4,6},{6,4},{1,3},{3,1},{5,7},{7,5},{8,10},{10,8},{12,... | collective-permute-start | bytes 1160 | tf_op jit(solution)/shard_map/ppermute | solution.py:329
  145.3 1.5 collective-permute-done.41.refs_8_
  151.1 6.5 %scan_local.1 = (bf16[1024,128]{1,0:T(8,128)(2,1)}, f32[1024,128]{1,0:T(8,128)S(1)}, f32[33,8,128]{2,1,0:T(8,128)S(1)}) custom-call(f32[1024,128]{1,0:T(8,128)S(1)} %copy-done.23, f32[1024,128]{1,0:T(8,128)S(1)} %copy-done.24, f32[1024,128]{1,0:T(8,128)S(1)} %copy-done.21, f32[1024,128]{1,0:T(8,128)S(1)} %copy-done.22, ...), custom_call_target="tpu_custom_call" | custom-call | flops 19800000512 | tf_op jit(solution)/shard_map/scan_local/pallas_call | solution.py:55
  162.6 3.2 %collective-permute-done.50 = f32[33,8,128]{2,1,0:T(8,128)S(1)} collective-permute-done((f32[33,8,128]{2,1,0:T(8,128)}, f32[33,8,128]{2,1,0:T(8,128)S(1)}, u32[]{:S(2)}, u32[]{:S(2)}) %collective-permute-start.50) | collective-permute-done | bytes 135200 | tf_op jit(solution)/shard_map/ppermute | solution.py:329
  167.3 7.1 %scan_adjoint.1 = (bf16[1024,128]{1,0:T(8,128)(2,1)}, bf16[1024,128]{1,0:T(8,128)(2,1)}) custom-call(f32[16,8,128]{2,1,0:T(8,128)S(1)} %get-tuple-element.90.refs_0_, f32[1024,128]{1,0:T(8,128)S(1)} %get-tuple-element.65.refs_1_, f32[1024,128]{1,0:T(8,128)S(1)} %copy-done.21, f32[1024,128]{1,0:T(8,128)S(1)} %copy-done.22, ...), custom_call_target="tpu_custom_call" | custom-call | flops 23100000256 | tf_op jit(solution)/shard_map/scan_adjoint/pallas_call | solution.py:55
  (193 shorter events, 56.7 us)
Async XLA Ops:
  7.6 18.2 %collective-permute-start = (bf16[2,96,512]{2,1,0:T(8,128)(2,1)}, bf16[2,96,512]{2,1,0:T(8,128)(2,1)S(1)}, u32[]{:S(2)}, u32[]{:S(2)}) collective-permute-start(bf16[2,96,512]{2,1,0:T(8,128)(2,1)} %get-tuple-element.41.refs_0_), channel_id=1, source_target_pairs={{0,1},{1,0},{2,3},{3,2},{4,5},{5,4},{6,7},{7,6},{8,9},{9,8},{10,11... | collective-permute-start | bytes 589832 | tf_op jit(solution)/shard_map/ppermute | solution.py:329
  10.6 17.2 %collective-permute-start.1 = (bf16[2,96,512]{2,1,0:T(8,128)(2,1)}, bf16[2,96,512]{2,1,0:T(8,128)(2,1)S(1)}, u32[]{:S(2)}, u32[]{:S(2)}) collective-permute-start(bf16[2,96,512]{2,1,0:T(8,128)(2,1)} %get-tuple-element.41.refs_0_), channel_id=1, source_target_pairs={{0,16},{16,0},{1,17},{17,1},{2,18},{18,2},{3,19},{19,3},{4,20},{20... | collective-permute-start | bytes 589832 | tf_op jit(solution)/shard_map/ppermute | solution.py:329
  12.1 12.5 %collective-permute-start.5 = (bf16[2,96,512]{2,1,0:T(8,128)(2,1)}, bf16[2,96,512]{2,1,0:T(8,128)(2,1)S(1)}, u32[]{:S(2)}, u32[]{:S(2)}) collective-permute-start(bf16[2,96,512]{2,1,0:T(8,128)(2,1)} %get-tuple-element.38.refs_5_), channel_id=1, source_target_pairs={{0,2},{2,0},{4,6},{6,4},{1,3},{3,1},{5,7},{7,5},{8,10},{10,8},{12,... | collective-permute-start | bytes 589832 | tf_op jit(solution)/shard_map/ppermute | solution.py:329
  13.7 12.8 %collective-permute-start.11 = (bf16[2,96,512]{2,1,0:T(8,128)(2,1)}, bf16[2,96,512]{2,1,0:T(8,128)(2,1)S(1)}, u32[]{:S(2)}, u32[]{:S(2)}) collective-permute-start(bf16[2,96,512]{2,1,0:T(8,128)(2,1)} %get-tuple-element.42), channel_id=1, source_target_pairs={{0,6},{2,4},{4,2},{6,0},{1,7},{3,5},{5,3},{7,1},{8,14},{10,12},{12... | collective-permute-start | bytes 589832 | tf_op jit(solution)/shard_map/ppermute | solution.py:329
  16.2 17.0 %collective-permute-start.17 = (bf16[2,96,512]{2,1,0:T(8,128)(2,1)}, bf16[2,96,512]{2,1,0:T(8,128)(2,1)S(1)}, u32[]{:S(2)}, u32[]{:S(2)}) collective-permute-start(bf16[2,96,512]{2,1,0:T(8,128)(2,1)} %get-tuple-element.43), channel_id=1, source_target_pairs={{0,4},{2,6},{4,0},{6,2},{1,5},{3,7},{5,1},{7,3},{8,12},{10,14},{12... | collective-permute-start | bytes 589832 | tf_op jit(solution)/shard_map/ppermute | solution.py:329
  25.3 8.5 %collective-permute-start.7 = (bf16[2,96,512]{2,1,0:T(8,128)(2,1)}, bf16[2,96,512]{2,1,0:T(8,128)(2,1)S(1)}, u32[]{:S(2)}, u32[]{:S(2)}) collective-permute-start(bf16[2,96,512]{2,1,0:T(8,128)(2,1)} %follow.1.refs_6_), channel_id=1, source_target_pairs={{0,16},{16,0},{1,17},{17,1},{2,18},{18,2},{3,19},{19,3},{4,20},{20... | collective-permute-start | bytes 589832 | tf_op jit(solution)/shard_map/ppermute | solution.py:329
  25.8 8.5 %collective-permute-start.6 = (bf16[2,96,512]{2,1,0:T(8,128)(2,1)}, bf16[2,96,512]{2,1,0:T(8,128)(2,1)S(1)}, u32[]{:S(2)}, u32[]{:S(2)}) collective-permute-start(bf16[2,96,512]{2,1,0:T(8,128)(2,1)} %follow.1.refs_6_), channel_id=1, source_target_pairs={{0,1},{1,0},{2,3},{3,2},{4,5},{5,4},{6,7},{7,6},{8,9},{9,8},{10,11... | collective-permute-start | bytes 589832 | tf_op jit(solution)/shard_map/ppermute | solution.py:329
  26.5 10.5 %collective-permute-start.13 = (bf16[2,96,512]{2,1,0:T(8,128)(2,1)S(1)}, bf16[2,96,512]{2,1,0:T(8,128)(2,1)S(1)}, u32[]{:S(2)}, u32[]{:S(2)}) collective-permute-start(bf16[2,96,512]{2,1,0:T(8,128)(2,1)S(1)} %collective-permute-done.11.refs_12_), channel_id=1, source_target_pairs={{0,16},{16,0},{1,17},{17,1},{2,18},{18,2},{3,19},{19,3},{4,20},{20... | collective-permute-start | bytes 589832 | tf_op jit(solution)/shard_map/ppermute | solution.py:329
  27.9 9.2 %collective-permute-start.12 = (bf16[2,96,512]{2,1,0:T(8,128)(2,1)S(1)}, bf16[2,96,512]{2,1,0:T(8,128)(2,1)S(1)}, u32[]{:S(2)}, u32[]{:S(2)}) collective-permute-start(bf16[2,96,512]{2,1,0:T(8,128)(2,1)S(1)} %collective-permute-done.11.refs_12_), channel_id=1, source_target_pairs={{0,1},{1,0},{2,3},{3,2},{4,5},{5,4},{6,7},{7,6},{8,9},{9,8},{10,11... | collective-permute-start | bytes 589832 | tf_op jit(solution)/shard_map/ppermute | solution.py:329
  34.4 9.3 %collective-permute-start.19 = (bf16[2,96,512]{2,1,0:T(8,128)(2,1)S(1)}, bf16[2,96,512]{2,1,0:T(8,128)(2,1)S(1)}, u32[]{:S(2)}, u32[]{:S(2)}) collective-permute-start(bf16[2,96,512]{2,1,0:T(8,128)(2,1)S(1)} %collective-permute-done.17.refs_18_), channel_id=1, source_target_pairs={{0,16},{16,0},{1,17},{17,1},{2,18},{18,2},{3,19},{19,3},{4,20},{20... | collective-permute-start | bytes 589832 | tf_op jit(solution)/shard_map/ppermute | solution.py:329
  37.0 12.4 %collective-permute-start.3 = (bf16[3,2,96,512]{3,2,1,0:T(8,128)(2,1)S(1)}, bf16[3,2,96,512]{3,2,1,0:T(8,128)(2,1)S(1)}, u32[]{:S(2)}, u32[]{:S(2)}) collective-permute-start(bf16[3,2,96,512]{3,2,1,0:T(8,128)(2,1)S(1)} %pad_maximum_fusion), channel_id=1, source_target_pairs={{0,8},{8,0},{1,9},{9,1},{2,10},{10,2},{3,11},{11,3},{4,12},{12,4},... | collective-permute-start | bytes 1769480 | tf_op jit(solution)/shard_map/ppermute | solution.py:329
  44.3 8.4 %collective-permute-start.9 = (bf16[3,2,96,512]{3,2,1,0:T(8,128)(2,1)S(1)}, bf16[3,2,96,512]{3,2,1,0:T(8,128)(2,1)S(1)}, u32[]{:S(2)}, u32[]{:S(2)}) collective-permute-start(bf16[3,2,96,512]{3,2,1,0:T(8,128)(2,1)S(1)} %pad_maximum_fusion.1), channel_id=1, source_target_pairs={{0,8},{8,0},{1,9},{9,1},{2,10},{10,2},{3,11},{11,3},{4,12},{12,4},... | collective-permute-start | bytes 1769480 | tf_op jit(solution)/shard_map/ppermute | solution.py:329
  51.5 24.0 %collective-permute-start.40 = (f32[32,8,128]{2,1,0:T(8,128)S(1)}, f32[32,8,128]{2,1,0:T(8,128)S(1)}, u32[]{:S(2)}, u32[]{:S(2)}) collective-permute-start(f32[32,8,128]{2,1,0:T(8,128)S(1)} %copy-done.3), channel_id=1, source_target_pairs={{0,8},{8,0},{1,9},{9,1},{2,10},{10,2},{3,11},{11,3},{4,12},{12,4},... | collective-permute-start | bytes 393224 | tf_op jit(solution)/shard_map/ppermute | solution.py:329
  77.1 9.4 %collective-permute-start.34 = (f32[2,96]{1,0:T(2,128)S(1)}, f32[2,96]{1,0:T(2,128)S(1)}, u32[]{:S(2)}, u32[]{:S(2)}) collective-permute-start(f32[2,96]{1,0:T(2,128)S(1)} %slice.112), channel_id=1, source_target_pairs={{0,8},{8,0},{1,9},{9,1},{2,10},{10,2},{3,11},{11,3},{4,12},{12,4},... | collective-permute-start | bytes 2312 | tf_op jit(solution)/shard_map/ppermute | solution.py:329
  86.4 13.5 %collective-permute-start.24 = (bf16[2,2,2,96,512]{4,3,2,1,0:T(8,128)(2,1)S(1)}, bf16[2,2,2,96,512]{4,3,2,1,0:T(8,128)(2,1)S(1)}, u32[]{:S(2)}, u32[]{:S(2)}) collective-permute-start(bf16[2,2,2,96,512]{4,3,2,1,0:T(8,128)(2,1)S(1)} %get-tuple-element.50), channel_id=1, source_target_pairs={{0,8},{8,0},{1,9},{9,1},{2,10},{10,2},{3,11},{11,3},{4,12},{12,4},... | collective-permute-start | bytes 2359304 | tf_op jit(solution)/shard_map/ppermute | solution.py:329
  87.9 10.4 %collective-permute-start.30 = (bf16[2,96,512]{2,1,0:T(8,128)(2,1)S(1)}, bf16[2,96,512]{2,1,0:T(8,128)(2,1)S(1)}, u32[]{:S(2)}, u32[]{:S(2)}) collective-permute-start(bf16[2,96,512]{2,1,0:T(8,128)(2,1)S(1)} %get-tuple-element.85), channel_id=1, source_target_pairs={{0,17},{1,16},{16,1},{17,0},{2,19},{3,18},{18,3},{19,2},{4,21},{5,... | collective-permute-start | bytes 589832 | tf_op jit(solution)/shard_map/ppermute | solution.py:596
  88.9 10.8 %collective-permute-start.31 = (bf16[2,96,512]{2,1,0:T(8,128)(2,1)S(1)}, bf16[2,96,512]{2,1,0:T(8,128)(2,1)S(1)}, u32[]{:S(2)}, u32[]{:S(2)}) collective-permute-start(bf16[2,96,512]{2,1,0:T(8,128)(2,1)S(1)} %get-tuple-element.84), channel_id=1, source_target_pairs={{0,16},{16,0},{1,17},{17,1},{2,18},{18,2},{3,19},{19,3},{4,20},{20... | collective-permute-start | bytes 589832 | tf_op jit(solution)/shard_map/ppermute | solution.py:329
  90.2 24.2 %collective-permute-start.35 = (f32[96]{0:T(128)S(1)}, f32[96]{0:T(128)S(1)}, u32[]{:S(2)}, u32[]{:S(2)}) collective-permute-start(f32[96]{0:T(128)S(1)} %slice_bitcast_fusion.12), channel_id=1, source_target_pairs={{0,16},{16,0},{1,17},{17,1},{2,18},{18,2},{3,19},{19,3},{4,20},{20... | collective-permute-start | bytes 1160 | tf_op jit(solution)/shard_map/ppermute | solution.py:329
  101.3 9.7 %collective-permute-start.26 = (bf16[2,96,512]{2,1,0:T(8,128)(2,1)S(1)}, bf16[2,96,512]{2,1,0:T(8,128)(2,1)S(1)}, u32[]{:S(2)}, u32[]{:S(2)}) collective-permute-start(bf16[2,96,512]{2,1,0:T(8,128)(2,1)S(1)} %get-tuple-element.88), channel_id=1, source_target_pairs={{0,17},{1,16},{16,1},{17,0},{2,19},{3,18},{18,3},{19,2},{4,21},{5,... | collective-permute-start | bytes 589832 | tf_op jit(solution)/shard_map/ppermute | solution.py:596
  103.1 9.4 %collective-permute-start.27 = (bf16[2,96,512]{2,1,0:T(8,128)(2,1)S(1)}, bf16[2,96,512]{2,1,0:T(8,128)(2,1)S(1)}, u32[]{:S(2)}, u32[]{:S(2)}) collective-permute-start(bf16[2,96,512]{2,1,0:T(8,128)(2,1)S(1)} %get-tuple-element.87), channel_id=1, source_target_pairs={{0,16},{16,0},{1,17},{17,1},{2,18},{18,2},{3,19},{19,3},{4,20},{20... | collective-permute-start | bytes 589832 | tf_op jit(solution)/shard_map/ppermute | solution.py:329
  103.9 11.4 %collective-permute-start.32 = (bf16[96,512]{1,0:T(8,128)(2,1)S(1)}, bf16[96,512]{1,0:T(8,128)(2,1)S(1)}, u32[]{:S(2)}, u32[]{:S(2)}) collective-permute-start(bf16[96,512]{1,0:T(8,128)(2,1)S(1)} %get-tuple-element.98), channel_id=1, source_target_pairs={{0,4},{2,6},{4,0},{6,2},{1,5},{3,7},{5,1},{7,3},{8,12},{10,14},{12... | collective-permute-start | bytes 294920 | tf_op jit(solution)/shard_map/ppermute | solution.py:329
  114.4 27.3 %collective-permute-start.36 = (f32[96]{0:T(128)S(1)}, f32[96]{0:T(128)S(1)}, u32[]{:S(2)}, u32[]{:S(2)}) collective-permute-start(f32[96]{0:T(128)S(1)} %bitcast_add_fusion), channel_id=1, source_target_pairs={{0,1},{1,0},{2,3},{3,2},{4,5},{5,4},{6,7},{7,6},{8,9},{9,8},{10,11... | collective-permute-start | bytes 1160 | tf_op jit(solution)/shard_map/ppermute | solution.py:329
  121.6 9.3 %collective-permute-start.47 = (bf16[1024,128]{1,0:T(8,128)(2,1)S(1)}, bf16[1024,128]{1,0:T(8,128)(2,1)S(1)}, u32[]{:S(2)}, u32[]{:S(2)}) collective-permute-start(bf16[1024,128]{1,0:T(8,128)(2,1)S(1)} %get-tuple-element.56.after_ref), channel_id=1, source_target_pairs={{0,1},{1,0},{2,3},{3,2},{4,5},{5,4},{6,7},{7,6},{8,9},{9,8},{10,11... | collective-permute-start | bytes 786440 | tf_op jit(solution)/shard_map/ppermute | solution.py:329
  124.2 12.4 %collective-permute-start.45 = (bf16[1024,128]{1,0:T(8,128)(2,1)S(1)}, bf16[1024,128]{1,0:T(8,128)(2,1)S(1)}, u32[]{:S(2)}, u32[]{:S(2)}) collective-permute-start(bf16[1024,128]{1,0:T(8,128)(2,1)S(1)} %get-tuple-element.57.after_ref), channel_id=1, source_target_pairs={{0,1},{1,0},{2,3},{3,2},{4,5},{5,4},{6,7},{7,6},{8,9},{9,8},{10,11... | collective-permute-start | bytes 786440 | tf_op jit(solution)/shard_map/ppermute | solution.py:329
  126.3 13.5 %collective-permute-start.43 = (bf16[1024,128]{1,0:T(8,128)(2,1)S(1)}, bf16[1024,128]{1,0:T(8,128)(2,1)S(1)}, u32[]{:S(2)}, u32[]{:S(2)}) collective-permute-start(bf16[1024,128]{1,0:T(8,128)(2,1)S(1)} %get-tuple-element.58.after_ref), channel_id=1, source_target_pairs={{0,1},{1,0},{2,3},{3,2},{4,5},{5,4},{6,7},{7,6},{8,9},{9,8},{10,11... | collective-permute-start | bytes 786440 | tf_op jit(solution)/shard_map/ppermute | solution.py:329
  128.8 13.5 %collective-permute-start.42 = (bf16[1024,128]{1,0:T(8,128)(2,1)S(1)}, bf16[1024,128]{1,0:T(8,128)(2,1)S(1)}, u32[]{:S(2)}, u32[]{:S(2)}) collective-permute-start(bf16[1024,128]{1,0:T(8,128)(2,1)S(1)} %get-tuple-element.60), channel_id=1, source_target_pairs={{0,1},{1,0},{2,3},{3,2},{4,5},{5,4},{6,7},{7,6},{8,9},{9,8},{10,11... | collective-permute-start | bytes 786440 | tf_op jit(solution)/shard_map/ppermute | solution.py:329
  131.0 17.2 %collective-permute-start.48 = (bf16[1024,128]{1,0:T(8,128)(2,1)S(1)}, bf16[1024,128]{1,0:T(8,128)(2,1)S(1)}, u32[]{:S(2)}, u32[]{:S(2)}) collective-permute-start(bf16[1024,128]{1,0:T(8,128)(2,1)S(1)} %add_convert_fusion), channel_id=1, source_target_pairs={{0,6},{2,4},{4,2},{6,0},{1,7},{3,5},{5,3},{7,1},{8,14},{10,12},{12... | collective-permute-start | bytes 786440 | tf_op jit(solution)/shard_map/ppermute | solution.py:329
  136.7 14.4 %collective-permute-start.46 = (bf16[1024,128]{1,0:T(8,128)(2,1)S(1)}, bf16[1024,128]{1,0:T(8,128)(2,1)S(1)}, u32[]{:S(2)}, u32[]{:S(2)}) collective-permute-start(bf16[1024,128]{1,0:T(8,128)(2,1)S(1)} %add_convert_fusion.1), channel_id=1, source_target_pairs={{0,4},{2,6},{4,0},{6,2},{1,5},{3,7},{5,1},{7,3},{8,12},{10,14},{12... | collective-permute-start | bytes 786440 | tf_op jit(solution)/shard_map/ppermute | solution.py:329
  139.8 11.3 %collective-permute-start.44 = (bf16[1024,128]{1,0:T(8,128)(2,1)S(1)}, bf16[1024,128]{1,0:T(8,128)(2,1)S(1)}, u32[]{:S(2)}, u32[]{:S(2)}) collective-permute-start(bf16[1024,128]{1,0:T(8,128)(2,1)S(1)} %add_convert_fusion.2), channel_id=1, source_target_pairs={{0,2},{2,0},{4,6},{6,4},{1,3},{3,1},{5,7},{7,5},{8,10},{10,8},{12,... | collective-permute-start | bytes 786440 | tf_op jit(solution)/shard_map/ppermute | solution.py:329
  142.3 15.5 %collective-permute-start.37 = (f32[96]{0:T(128)S(1)}, f32[96]{0:T(128)S(1)}, u32[]{:S(2)}, u32[]{:S(2)}) collective-permute-start(f32[96]{0:T(128)S(1)} %add.98), channel_id=1, source_target_pairs={{0,2},{2,0},{4,6},{6,4},{1,3},{3,1},{5,7},{7,5},{8,10},{10,8},{12,... | collective-permute-start | bytes 1160 | tf_op jit(solution)/shard_map/ppermute | solution.py:329
  146.8 11.0 %collective-permute-start.38 = (f32[96]{0:T(128)S(1)}, f32[96]{0:T(128)S(1)}, u32[]{:S(2)}, u32[]{:S(2)}) collective-permute-start(f32[96]{0:T(128)S(1)} %add.98), channel_id=1, source_target_pairs={{0,4},{2,6},{4,0},{6,2},{1,5},{3,7},{5,1},{7,3},{8,12},{10,14},{12... | collective-permute-start | bytes 1160 | tf_op jit(solution)/shard_map/ppermute | solution.py:329
  148.2 9.6 %collective-permute-start.39 = (f32[96]{0:T(128)S(1)}, f32[96]{0:T(128)S(1)}, u32[]{:S(2)}, u32[]{:S(2)}) collective-permute-start(f32[96]{0:T(128)S(1)} %add.98), channel_id=1, source_target_pairs={{0,6},{2,4},{4,2},{6,0},{1,7},{3,5},{5,3},{7,1},{8,14},{10,12},{12... | collective-permute-start | bytes 1160 | tf_op jit(solution)/shard_map/ppermute | solution.py:329
  (54 other events, 576.5 us)

commit v4 on v3

--- a/solution.py
+++ b/solution.py
@@ -32,7 +32,7 @@
     )
 
 
-def staged_call(kernel, operands, kinds, outs, scratch, cost, name, room):
+def staged_call(kernel, operands, kinds, outs, scratch, cost, name, room, early=None):
     fetched = [place for place, kind in enumerate(kinds) if kind == "in"]
     given, total = len(operands), len(outs)
     held = {"in": pltpu.HBM, "hbm": pltpu.HBM, "smem": pltpu.SMEM}
@@ -48,6 +48,8 @@
             )
             copies[-1].start()
             ins[place] = buffers[index]
+        if early is not None:
+            first_back(ins[early], rest[-2], rest[-1]).start()
         for copy in copies:
             copy.wait()
         kernel(*ins, *made, *rest[len(fetched) + 1 :])
@@ -167,6 +169,12 @@
     )
 
 
+def first_back(kept_ref, kept_rows, copied):
+    span = kept_rows.shape[0] // CHUNKS
+    part = pl.ds((CHUNKS - 1) * span, span)
+    return pltpu.make_async_copy(kept_ref.at[part], kept_rows.at[part], copied.at[CHUNKS - 1])
+
+
 def fetch_back(kept_ref, kept_rows, copied, span):
     copies = []
     for chunk in reversed(range(CHUNKS)):
@@ -174,7 +182,8 @@
         copies.append(
             pltpu.make_async_copy(kept_ref.at[part], kept_rows.at[part], copied.at[chunk])
         )
-        copies[-1].start()
+        if len(copies) > 1:
+            copies[-1].start()
     return copies
 
 
@@ -248,6 +257,7 @@
         6,
         "scan_local",
         50,
+        early=4,
     )
 
 
@@ -321,6 +331,7 @@
         7,
         "scan_adjoint",
         50,
+        early=4,
     )
 
 

time: 176 us -> 175 us (level)
  no operation moved by 1% of the time
where the time goes in v4:
time: 175 us
  Pallas kernels  64.6 us (37%)
  starting transfers between devices  54.2 us (31%)
  waiting for transfers between devices  41.5 us (24%)
  other arithmetic  7.36 us (4%)
  local copies, waits for them, and re-layouts  5.71 us (3%)
    ppermute x49, starting transfers between devices, swap(): lax.ppermute(value, axis, [(place, place ^ distance) for place in range(c...  51.5 us
    ppermute x49, waiting for transfers between devices, swap(): lax.ppermute(value, axis, [(place, place ^ distance) for place in range(c...  37.3 us
    pallas_call x8, Pallas kernels, staged_call(): pl.pallas_call(body, grid=(1,), out_shape=tuple((out for out, kind in out...  30.1 us
    pallas_call x1, Pallas kernels, gather_call(): pl.pallas_call(functools.partial(gather_kernel, groups, blocks, first, la...  15.6 us
    pallas_call x2, Pallas kernels, return_call(): pl.pallas_call(functools.partial(return_kernel, row_count), out_shape=(ja...  14 us
    pallas_call x4, Pallas kernels, project_call(): pl.pallas_call(project_kernel, out_shape=(jax.ShapeDtypeStruct(shape, jnp...  4.95 us
    unnamed x71, local copies, waits for them, and re-layouts  4.38 us
    ppermute x2, waiting for transfers between devices, corner_swap(): return lax.ppermute(value, ('row', 'half'), pairs)  4.18 us
  transfers between devices with their start and end apart: 51, of which 25 were waited for; matrix products, arithmetic and copies ran while one was open for 3% of the time, Pallas kernels for 30%

profile of v4, /device:TPU:0, one launch (start us, length us, event | category | flops | bytes accessed | tf_op | source)
XLA Modules:
  0.0 174.7 jit_solution(12886708425082083837)
XLA Ops:
  1.8 2.8 %route_rows.1 = (bf16[2,96,512]{2,1,0:T(8,128)(2,1)}, bf16[2,96,512]{2,1,0:T(8,128)(2,1)}, bf16[2,96,512]{2,1,0:T(8,128)(2,1)}) custom-call(s32[14]{0:T(128)} %dynamic-slice_bitcast_fusion.refs_0_.places_ref, s32[2,128]{1,0:T(2,128)} %bitcast.85, f32[2,128]{1,0:T(2,128)} %bitcast.87, bf16[128,512]{1,0:T(8,128)(2,1)} %refs_3_.4, bf16[128,512]{1,0:T(8,128)(2,1)} %refs_1_.3), custom_call_target="tpu_custom_call" | custom-call | flops 3300000000 | tf_op jit(solution)/shard_map/route_rows/pallas_call | solution.py:57
  4.8 2.8 %route_own.1 = (bf16[2,96,512]{2,1,0:T(8,128)(2,1)}, f32[128,16]{1,0:T(8,128)}) custom-call(s32[14]{0:T(128)} %dynamic-slice_bitcast_fusion.refs_0_.places_ref, s32[2,128]{1,0:T(2,128)} %bitcast.86, f32[2,128]{1,0:T(2,128)} %bitcast.88, bf16[128,512]{1,0:T(8,128)(2,1)} %refs_3_.4, bf16[128,512]{1,0:T(8,128)(2,1)} %refs_1_.3, ...), custom_call_target="tpu_custom_call" | custom-call | flops 3300000000 | tf_op jit(solution)/shard_map/route_own/pallas_call | solution.py:57
  7.6 3.0 %collective-permute-start = (bf16[2,96,512]{2,1,0:T(8,128)(2,1)}, bf16[2,96,512]{2,1,0:T(8,128)(2,1)S(1)}, u32[]{:S(2)}, u32[]{:S(2)}) collective-permute-start(bf16[2,96,512]{2,1,0:T(8,128)(2,1)} %get-tuple-element.41.refs_0_), channel_id=1, source_target_pairs={{0,1},{1,0},{2,3},{3,2},{4,5},{5,4},{6,7},{7,6},{8,9},{9,8},{10,11... | collective-permute-start | bytes 589832 | tf_op jit(solution)/shard_map/ppermute | solution.py:340
  12.1 1.6 collective-permute-start.5
  13.7 2.5 %collective-permute-start.11 = (bf16[2,96,512]{2,1,0:T(8,128)(2,1)}, bf16[2,96,512]{2,1,0:T(8,128)(2,1)S(1)}, u32[]{:S(2)}, u32[]{:S(2)}) collective-permute-start(bf16[2,96,512]{2,1,0:T(8,128)(2,1)} %get-tuple-element.42), channel_id=1, source_target_pairs={{0,6},{2,4},{4,2},{6,0},{1,7},{3,5},{5,3},{7,1},{8,14},{10,12},{12... | collective-permute-start | bytes 589832 | tf_op jit(solution)/shard_map/ppermute | solution.py:340
  16.4 7.6 %scan_forward.1 = (f32[128,16,8,128]{3,2,1,0:T(8,128)}, f32[1024,128]{1,0:T(8,128)}, f32[1024,128]{1,0:T(8,128)}, f32[1024,128]{1,0:T(8,128)}, f32[1024,128]{1,0:T(8,128)}, /*index=5*/f32[32,8,128]{2,1,0:T(8,128)S(1)}) custom-call(bf16[1024,128]{1,0:T(8,128)(2,1)S(1)} %copy-done.6, bf16[1024,128]{1,0:T(8,128)(2,1)S(1)} %copy-done.8, ...), custom_call_target="tpu_custom_call" | custom-call | flops 23100000256 | tf_op jit(solution)/shard_map/scan_forward/pallas_call | solution.py:57
  29.4 3.9 %collective-permute-done.17.refs_18_ = bf16[2,96,512]{2,1,0:T(8,128)(2,1)S(1)} collective-permute-done((bf16[2,96,512]{2,1,0:T(8,128)(2,1)}, bf16[2,96,512]{2,1,0:T(8,128)(2,1)S(1)}, u32[]{:S(2)}, u32[]{:S(2)}) %collective-permute-start.17) | collective-permute-done | bytes 196640 | tf_op jit(solution)/shard_map/ppermute | solution.py:340
  34.4 1.6 collective-permute-start.19
  37.1 1.6 collective-permute-start.8
  38.7 2.9 %collective-permute-done.2.refs_3_ = bf16[2,96,512]{2,1,0:T(8,128)(2,1)S(1)} collective-permute-done((bf16[2,96,512]{2,1,0:T(8,128)(2,1)S(1)}, bf16[2,96,512]{2,1,0:T(8,128)(2,1)S(1)}, u32[]{:S(2)}, u32[]{:S(2)}) %collective-permute-start.2) | collective-permute-done | bytes 196640 | tf_op jit(solution)/shard_map/ppermute | solution.py:340
  44.8 4.0 %collective-permute-done.14.refs_15_ = bf16[2,96,512]{2,1,0:T(8,128)(2,1)S(1)} collective-permute-done((bf16[2,96,512]{2,1,0:T(8,128)(2,1)S(1)}, bf16[2,96,512]{2,1,0:T(8,128)(2,1)S(1)}, u32[]{:S(2)}, u32[]{:S(2)}) %collective-permute-start.14) | collective-permute-done | bytes 196640 | tf_op jit(solution)/shard_map/ppermute | solution.py:340
  52.6 15.6 %hidden_rows.1 = (bf16[384,1024]{1,0:T(8,128)(2,1)S(1)}, bf16[384,1024]{1,0:T(8,128)(2,1)S(1)}, f32[384,128]{1,0:T(8,128)S(1)}) custom-call(s32[14]{0:T(128)S(1)} %copy-done.16, f32[32,8,128]{2,1,0:T(8,128)S(1)} %copy-done.3, bf16[2,96,512]{2,1,0:T(8,128)(2,1)S(1)} %copy-done.4, bf16[2,96,512]{2,1,0:T(8,128)(2,1)S(1)} %collective-permute-done.refs_1_, ...), custom_call_target="tpu_custom_call" | custom-call | flops 52800000000 | tf_op jit(solution)/shard_map/hidden_rows/pallas_call | solution.py:543
  68.2 7.0 %route_grads.2 = (f32[2,2,2,96,512]{4,3,2,1,0:T(8,128)S(1)}, bf16[2,2,2,96,512]{4,3,2,1,0:T(8,128)(2,1)S(1)}) custom-call(s32[14]{0:T(128)S(1)} %copy-done.16, bf16[384,1024]{1,0:T(8,128)(2,1)S(1)} %get-tuple-element.44.gate_ref, bf16[384,1024]{1,0:T(8,128)(2,1)S(1)} %get-tuple-element.45.up_ref.refs_1_, bf16[1,4096,1024]{2,1,0:T(8,128)(2,1)} %gate_weight.3, ...), custom_call_target="tpu_custom_call" | custom-call | flops 26400000000 | tf_op jit(solution)/shard_map/route_grads/pallas_call | solution.py:582
  77.8 1.5 fusion.14
  79.4 7.0 %route_grads.3 = (f32[2,2,2,96,512]{4,3,2,1,0:T(8,128)S(1)}, bf16[2,2,2,96,512]{4,3,2,1,0:T(8,128)(2,1)S(1)}) custom-call(s32[14]{0:T(128)S(1)} %copy-done.16, bf16[384,1024]{1,0:T(8,128)(2,1)S(1)} %copy-done.26, bf16[384,1024]{1,0:T(8,128)(2,1)S(1)} %copy-done.19, bf16[1,4096,1024]{2,1,0:T(8,128)(2,1)} %gate_weight.3, bf16[1,4096,1024]{2,1,0:T(8,128)(2,1)} %up_weight.3, ...), custom_call_target="tpu_custom_call" | custom-call | flops 26400000000 | tf_op jit(solution)/shard_map/route_grads/pallas_call | solution.py:582
  90.9 3.5 %collective-permute-done.29 = bf16[2,96,512]{2,1,0:T(8,128)(2,1)S(1)} collective-permute-done((bf16[2,96,512]{2,1,0:T(8,128)(2,1)S(1)}, bf16[2,96,512]{2,1,0:T(8,128)(2,1)S(1)}, u32[]{:S(2)}, u32[]{:S(2)}) %collective-permute-start.29) | collective-permute-done | bytes 196640 | tf_op jit(solution)/shard_map/ppermute | solution.py:340
  94.4 4.0 %collective-permute-done.30 = bf16[2,96,512]{2,1,0:T(8,128)(2,1)S(1)} collective-permute-done((bf16[2,96,512]{2,1,0:T(8,128)(2,1)S(1)}, bf16[2,96,512]{2,1,0:T(8,128)(2,1)S(1)}, u32[]{:S(2)}, u32[]{:S(2)}) %collective-permute-start.30) | collective-permute-done | bytes 196640 | tf_op jit(solution)/shard_map/ppermute | solution.py:607
  101.3 1.8 %collective-permute-start.26 = (bf16[2,96,512]{2,1,0:T(8,128)(2,1)S(1)}, bf16[2,96,512]{2,1,0:T(8,128)(2,1)S(1)}, u32[]{:S(2)}, u32[]{:S(2)}) collective-permute-start(bf16[2,96,512]{2,1,0:T(8,128)(2,1)S(1)} %get-tuple-element.88), channel_id=1, source_target_pairs={{0,17},{1,16},{16,1},{17,0},{2,19},{3,18},{18,3},{19,2},{4,21},{5,... | collective-permute-start | bytes 589832 | tf_op jit(solution)/shard_map/ppermute | solution.py:607
  103.9 2.8 %collective-permute-start.32 = (bf16[96,512]{1,0:T(8,128)(2,1)S(1)}, bf16[96,512]{1,0:T(8,128)(2,1)S(1)}, u32[]{:S(2)}, u32[]{:S(2)}) collective-permute-start(bf16[96,512]{1,0:T(8,128)(2,1)S(1)} %get-tuple-element.98), channel_id=1, source_target_pairs={{0,4},{2,6},{4,0},{6,2},{1,5},{3,7},{5,1},{7,3},{8,12},{10,14},{12... | collective-permute-start | bytes 294920 | tf_op jit(solution)/shard_map/ppermute | solution.py:340
  108.2 2.6 %collective-permute-start.33 = (bf16[96,512]{1,0:T(8,128)(2,1)S(1)}, bf16[96,512]{1,0:T(8,128)(2,1)S(1)}, u32[]{:S(2)}, u32[]{:S(2)}) collective-permute-start(bf16[96,512]{1,0:T(8,128)(2,1)S(1)} %get-tuple-element.97), channel_id=1, source_target_pairs={{0,6},{2,4},{4,2},{6,0},{1,7},{3,5},{5,3},{7,1},{8,14},{10,12},{12... | collective-permute-start | bytes 294920 | tf_op jit(solution)/shard_map/ppermute | solution.py:340
  112.6 1.8 %collective-permute-start.28 = (bf16[96,512]{1,0:T(8,128)(2,1)S(1)}, bf16[96,512]{1,0:T(8,128)(2,1)S(1)}, u32[]{:S(2)}, u32[]{:S(2)}) collective-permute-start(bf16[96,512]{1,0:T(8,128)(2,1)S(1)} %get-tuple-element.99), channel_id=1, source_target_pairs={{0,2},{2,0},{4,6},{6,4},{1,3},{3,1},{5,7},{7,5},{8,10},{10,8},{12,... | collective-permute-start | bytes 294920 | tf_op jit(solution)/shard_map/ppermute | solution.py:340
  115.2 2.1 %collective-permute-done.28.refs_3_ = bf16[96,512]{1,0:T(8,128)(2,1)S(1)} collective-permute-done((bf16[96,512]{1,0:T(8,128)(2,1)S(1)}, bf16[96,512]{1,0:T(8,128)(2,1)S(1)}, u32[]{:S(2)}, u32[]{:S(2)}) %collective-permute-start.28) | collective-permute-done | bytes 98336 | tf_op jit(solution)/shard_map/ppermute | solution.py:340
  117.3 2.0 %resid_rows.1.resid_ref.after_ref = bf16[128,512]{1,0:T(8,128)(2,1)} custom-call(f32[128,16]{1,0:T(8,128)S(1)} %copy-done.20, bf16[128,512]{1,0:T(8,128)(2,1)S(1)} %copy-done.9, bf16[96,512]{1,0:T(8,128)(2,1)S(1)} %get-tuple-element.100.refs_2_, bf16[96,512]{1,0:T(8,128)(2,1)S(1)} %collective-permute-done.28.refs_3_, ...), custom_call_target="tpu_custom_call" | custom-call | flops 6600000000 | tf_op jit(solution)/shard_map/resid_rows/pallas_call | solution.py:57
  131.0 2.7 %collective-permute-start.48 = (bf16[1024,128]{1,0:T(8,128)(2,1)S(1)}, bf16[1024,128]{1,0:T(8,128)(2,1)S(1)}, u32[]{:S(2)}, u32[]{:S(2)}) collective-permute-start(bf16[1024,128]{1,0:T(8,128)(2,1)S(1)} %add_convert_fusion), channel_id=1, source_target_pairs={{0,6},{2,4},{4,2},{6,0},{1,7},{3,5},{5,3},{7,1},{8,14},{10,12},{12... | collective-permute-start | bytes 786440 | tf_op jit(solution)/shard_map/ppermute | solution.py:340
  133.7 2.9 %collective-permute-done.45 = bf16[1024,128]{1,0:T(8,128)(2,1)S(1)} collective-permute-done((bf16[1024,128]{1,0:T(8,128)(2,1)S(1)}, bf16[1024,128]{1,0:T(8,128)(2,1)S(1)}, u32[]{:S(2)}, u32[]{:S(2)}) %collective-permute-start.45) | collective-permute-done | bytes 262176 | tf_op jit(solution)/shard_map/ppermute | solution.py:340
  136.7 3.1 %collective-permute-start.46 = (bf16[1024,128]{1,0:T(8,128)(2,1)S(1)}, bf16[1024,128]{1,0:T(8,128)(2,1)S(1)}, u32[]{:S(2)}, u32[]{:S(2)}) collective-permute-start(bf16[1024,128]{1,0:T(8,128)(2,1)S(1)} %add_convert_fusion.1), channel_id=1, source_target_pairs={{0,4},{2,6},{4,0},{6,2},{1,5},{3,7},{5,1},{7,3},{8,12},{10,14},{12... | collective-permute-start | bytes 786440 | tf_op jit(solution)/shard_map/ppermute | solution.py:340
  139.8 1.9 %collective-permute-start.44 = (bf16[1024,128]{1,0:T(8,128)(2,1)S(1)}, bf16[1024,128]{1,0:T(8,128)(2,1)S(1)}, u32[]{:S(2)}, u32[]{:S(2)}) collective-permute-start(bf16[1024,128]{1,0:T(8,128)(2,1)S(1)} %add_convert_fusion.2), channel_id=1, source_target_pairs={{0,2},{2,0},{4,6},{6,4},{1,3},{3,1},{5,7},{7,5},{8,10},{10,8},{12,... | collective-permute-start | bytes 786440 | tf_op jit(solution)/shard_map/ppermute | solution.py:340
  142.3 2.1 %collective-permute-start.37 = (f32[96]{0:T(128)S(1)}, f32[96]{0:T(128)S(1)}, u32[]{:S(2)}, u32[]{:S(2)}) collective-permute-start(f32[96]{0:T(128)S(1)} %add.98), channel_id=1, source_target_pairs={{0,2},{2,0},{4,6},{6,4},{1,3},{3,1},{5,7},{7,5},{8,10},{10,8},{12,... | collective-permute-start | bytes 1160 | tf_op jit(solution)/shard_map/ppermute | solution.py:340
  145.3 1.5 collective-permute-done.41.refs_8_
  151.1 6.3 %scan_local.1 = (bf16[1024,128]{1,0:T(8,128)(2,1)}, f32[1024,128]{1,0:T(8,128)S(1)}, f32[33,8,128]{2,1,0:T(8,128)S(1)}) custom-call(f32[1024,128]{1,0:T(8,128)S(1)} %copy-done.23, f32[1024,128]{1,0:T(8,128)S(1)} %copy-done.24, f32[1024,128]{1,0:T(8,128)S(1)} %copy-done.21, f32[1024,128]{1,0:T(8,128)S(1)} %copy-done.22, ...), custom_call_target="tpu_custom_call" | custom-call | flops 19800000512 | tf_op jit(solution)/shard_map/scan_local/pallas_call | solution.py:57
  162.3 3.2 %collective-permute-done.50 = f32[33,8,128]{2,1,0:T(8,128)S(1)} collective-permute-done((f32[33,8,128]{2,1,0:T(8,128)}, f32[33,8,128]{2,1,0:T(8,128)S(1)}, u32[]{:S(2)}, u32[]{:S(2)}) %collective-permute-start.50) | collective-permute-done | bytes 135200 | tf_op jit(solution)/shard_map/ppermute | solution.py:340
  167.1 7.1 %scan_adjoint.1 = (bf16[1024,128]{1,0:T(8,128)(2,1)}, bf16[1024,128]{1,0:T(8,128)(2,1)}) custom-call(f32[16,8,128]{2,1,0:T(8,128)S(1)} %get-tuple-element.90.refs_0_, f32[1024,128]{1,0:T(8,128)S(1)} %get-tuple-element.65.refs_1_, f32[1024,128]{1,0:T(8,128)S(1)} %copy-done.21, f32[1024,128]{1,0:T(8,128)S(1)} %copy-done.22, ...), custom_call_target="tpu_custom_call" | custom-call | flops 23100000256 | tf_op jit(solution)/shard_map/scan_adjoint/pallas_call | solution.py:57
  (193 shorter events, 56.7 us)
Async XLA Ops:
  7.6 18.2 %collective-permute-start = (bf16[2,96,512]{2,1,0:T(8,128)(2,1)}, bf16[2,96,512]{2,1,0:T(8,128)(2,1)S(1)}, u32[]{:S(2)}, u32[]{:S(2)}) collective-permute-start(bf16[2,96,512]{2,1,0:T(8,128)(2,1)} %get-tuple-element.41.refs_0_), channel_id=1, source_target_pairs={{0,1},{1,0},{2,3},{3,2},{4,5},{5,4},{6,7},{7,6},{8,9},{9,8},{10,11... | collective-permute-start | bytes 589832 | tf_op jit(solution)/shard_map/ppermute | solution.py:340
  10.6 17.2 %collective-permute-start.1 = (bf16[2,96,512]{2,1,0:T(8,128)(2,1)}, bf16[2,96,512]{2,1,0:T(8,128)(2,1)S(1)}, u32[]{:S(2)}, u32[]{:S(2)}) collective-permute-start(bf16[2,96,512]{2,1,0:T(8,128)(2,1)} %get-tuple-element.41.refs_0_), channel_id=1, source_target_pairs={{0,16},{16,0},{1,17},{17,1},{2,18},{18,2},{3,19},{19,3},{4,20},{20... | collective-permute-start | bytes 589832 | tf_op jit(solution)/shard_map/ppermute | solution.py:340
  12.1 12.5 %collective-permute-start.5 = (bf16[2,96,512]{2,1,0:T(8,128)(2,1)}, bf16[2,96,512]{2,1,0:T(8,128)(2,1)S(1)}, u32[]{:S(2)}, u32[]{:S(2)}) collective-permute-start(bf16[2,96,512]{2,1,0:T(8,128)(2,1)} %get-tuple-element.38.refs_5_), channel_id=1, source_target_pairs={{0,2},{2,0},{4,6},{6,4},{1,3},{3,1},{5,7},{7,5},{8,10},{10,8},{12,... | collective-permute-start | bytes 589832 | tf_op jit(solution)/shard_map/ppermute | solution.py:340
  13.7 12.8 %collective-permute-start.11 = (bf16[2,96,512]{2,1,0:T(8,128)(2,1)}, bf16[2,96,512]{2,1,0:T(8,128)(2,1)S(1)}, u32[]{:S(2)}, u32[]{:S(2)}) collective-permute-start(bf16[2,96,512]{2,1,0:T(8,128)(2,1)} %get-tuple-element.42), channel_id=1, source_target_pairs={{0,6},{2,4},{4,2},{6,0},{1,7},{3,5},{5,3},{7,1},{8,14},{10,12},{12... | collective-permute-start | bytes 589832 | tf_op jit(solution)/shard_map/ppermute | solution.py:340
  16.2 17.0 %collective-permute-start.17 = (bf16[2,96,512]{2,1,0:T(8,128)(2,1)}, bf16[2,96,512]{2,1,0:T(8,128)(2,1)S(1)}, u32[]{:S(2)}, u32[]{:S(2)}) collective-permute-start(bf16[2,96,512]{2,1,0:T(8,128)(2,1)} %get-tuple-element.43), channel_id=1, source_target_pairs={{0,4},{2,6},{4,0},{6,2},{1,5},{3,7},{5,1},{7,3},{8,12},{10,14},{12... | collective-permute-start | bytes 589832 | tf_op jit(solution)/shard_map/ppermute | solution.py:340
  25.3 8.5 %collective-permute-start.7 = (bf16[2,96,512]{2,1,0:T(8,128)(2,1)}, bf16[2,96,512]{2,1,0:T(8,128)(2,1)S(1)}, u32[]{:S(2)}, u32[]{:S(2)}) collective-permute-start(bf16[2,96,512]{2,1,0:T(8,128)(2,1)} %follow.1.refs_6_), channel_id=1, source_target_pairs={{0,16},{16,0},{1,17},{17,1},{2,18},{18,2},{3,19},{19,3},{4,20},{20... | collective-permute-start | bytes 589832 | tf_op jit(solution)/shard_map/ppermute | solution.py:340
  25.8 8.5 %collective-permute-start.6 = (bf16[2,96,512]{2,1,0:T(8,128)(2,1)}, bf16[2,96,512]{2,1,0:T(8,128)(2,1)S(1)}, u32[]{:S(2)}, u32[]{:S(2)}) collective-permute-start(bf16[2,96,512]{2,1,0:T(8,128)(2,1)} %follow.1.refs_6_), channel_id=1, source_target_pairs={{0,1},{1,0},{2,3},{3,2},{4,5},{5,4},{6,7},{7,6},{8,9},{9,8},{10,11... | collective-permute-start | bytes 589832 | tf_op jit(solution)/shard_map/ppermute | solution.py:340
  26.5 10.5 %collective-permute-start.13 = (bf16[2,96,512]{2,1,0:T(8,128)(2,1)S(1)}, bf16[2,96,512]{2,1,0:T(8,128)(2,1)S(1)}, u32[]{:S(2)}, u32[]{:S(2)}) collective-permute-start(bf16[2,96,512]{2,1,0:T(8,128)(2,1)S(1)} %collective-permute-done.11.refs_12_), channel_id=1, source_target_pairs={{0,16},{16,0},{1,17},{17,1},{2,18},{18,2},{3,19},{19,3},{4,20},{20... | collective-permute-start | bytes 589832 | tf_op jit(solution)/shard_map/ppermute | solution.py:340
  27.9 9.2 %collective-permute-start.12 = (bf16[2,96,512]{2,1,0:T(8,128)(2,1)S(1)}, bf16[2,96,512]{2,1,0:T(8,128)(2,1)S(1)}, u32[]{:S(2)}, u32[]{:S(2)}) collective-permute-start(bf16[2,96,512]{2,1,0:T(8,128)(2,1)S(1)} %collective-permute-done.11.refs_12_), channel_id=1, source_target_pairs={{0,1},{1,0},{2,3},{3,2},{4,5},{5,4},{6,7},{7,6},{8,9},{9,8},{10,11... | collective-permute-start | bytes 589832 | tf_op jit(solution)/shard_map/ppermute | solution.py:340
  34.4 9.3 %collective-permute-start.19 = (bf16[2,96,512]{2,1,0:T(8,128)(2,1)S(1)}, bf16[2,96,512]{2,1,0:T(8,128)(2,1)S(1)}, u32[]{:S(2)}, u32[]{:S(2)}) collective-permute-start(bf16[2,96,512]{2,1,0:T(8,128)(2,1)S(1)} %collective-permute-done.17.refs_18_), channel_id=1, source_target_pairs={{0,16},{16,0},{1,17},{17,1},{2,18},{18,2},{3,19},{19,3},{4,20},{20... | collective-permute-start | bytes 589832 | tf_op jit(solution)/shard_map/ppermute | solution.py:340
  37.0 12.4 %collective-permute-start.3 = (bf16[3,2,96,512]{3,2,1,0:T(8,128)(2,1)S(1)}, bf16[3,2,96,512]{3,2,1,0:T(8,128)(2,1)S(1)}, u32[]{:S(2)}, u32[]{:S(2)}) collective-permute-start(bf16[3,2,96,512]{3,2,1,0:T(8,128)(2,1)S(1)} %pad_maximum_fusion), channel_id=1, source_target_pairs={{0,8},{8,0},{1,9},{9,1},{2,10},{10,2},{3,11},{11,3},{4,12},{12,4},... | collective-permute-start | bytes 1769480 | tf_op jit(solution)/shard_map/ppermute | solution.py:340
  44.3 8.4 %collective-permute-start.9 = (bf16[3,2,96,512]{3,2,1,0:T(8,128)(2,1)S(1)}, bf16[3,2,96,512]{3,2,1,0:T(8,128)(2,1)S(1)}, u32[]{:S(2)}, u32[]{:S(2)}) collective-permute-start(bf16[3,2,96,512]{3,2,1,0:T(8,128)(2,1)S(1)} %pad_maximum_fusion.1), channel_id=1, source_target_pairs={{0,8},{8,0},{1,9},{9,1},{2,10},{10,2},{3,11},{11,3},{4,12},{12,4},... | collective-permute-start | bytes 1769480 | tf_op jit(solution)/shard_map/ppermute | solution.py:340
  51.5 24.0 %collective-permute-start.40 = (f32[32,8,128]{2,1,0:T(8,128)S(1)}, f32[32,8,128]{2,1,0:T(8,128)S(1)}, u32[]{:S(2)}, u32[]{:S(2)}) collective-permute-start(f32[32,8,128]{2,1,0:T(8,128)S(1)} %copy-done.3), channel_id=1, source_target_pairs={{0,8},{8,0},{1,9},{9,1},{2,10},{10,2},{3,11},{11,3},{4,12},{12,4},... | collective-permute-start | bytes 393224 | tf_op jit(solution)/shard_map/ppermute | solution.py:340
  77.1 9.4 %collective-permute-start.34 = (f32[2,96]{1,0:T(2,128)S(1)}, f32[2,96]{1,0:T(2,128)S(1)}, u32[]{:S(2)}, u32[]{:S(2)}) collective-permute-start(f32[2,96]{1,0:T(2,128)S(1)} %slice.112), channel_id=1, source_target_pairs={{0,8},{8,0},{1,9},{9,1},{2,10},{10,2},{3,11},{11,3},{4,12},{12,4},... | collective-permute-start | bytes 2312 | tf_op jit(solution)/shard_map/ppermute | solution.py:340
  86.4 13.5 %collective-permute-start.24 = (bf16[2,2,2,96,512]{4,3,2,1,0:T(8,128)(2,1)S(1)}, bf16[2,2,2,96,512]{4,3,2,1,0:T(8,128)(2,1)S(1)}, u32[]{:S(2)}, u32[]{:S(2)}) collective-permute-start(bf16[2,2,2,96,512]{4,3,2,1,0:T(8,128)(2,1)S(1)} %get-tuple-element.50), channel_id=1, source_target_pairs={{0,8},{8,0},{1,9},{9,1},{2,10},{10,2},{3,11},{11,3},{4,12},{12,4},... | collective-permute-start | bytes 2359304 | tf_op jit(solution)/shard_map/ppermute | solution.py:340
  87.9 10.4 %collective-permute-start.30 = (bf16[2,96,512]{2,1,0:T(8,128)(2,1)S(1)}, bf16[2,96,512]{2,1,0:T(8,128)(2,1)S(1)}, u32[]{:S(2)}, u32[]{:S(2)}) collective-permute-start(bf16[2,96,512]{2,1,0:T(8,128)(2,1)S(1)} %get-tuple-element.85), channel_id=1, source_target_pairs={{0,17},{1,16},{16,1},{17,0},{2,19},{3,18},{18,3},{19,2},{4,21},{5,... | collective-permute-start | bytes 589832 | tf_op jit(solution)/shard_map/ppermute | solution.py:607
  88.9 10.8 %collective-permute-start.31 = (bf16[2,96,512]{2,1,0:T(8,128)(2,1)S(1)}, bf16[2,96,512]{2,1,0:T(8,128)(2,1)S(1)}, u32[]{:S(2)}, u32[]{:S(2)}) collective-permute-start(bf16[2,96,512]{2,1,0:T(8,128)(2,1)S(1)} %get-tuple-element.84), channel_id=1, source_target_pairs={{0,16},{16,0},{1,17},{17,1},{2,18},{18,2},{3,19},{19,3},{4,20},{20... | collective-permute-start | bytes 589832 | tf_op jit(solution)/shard_map/ppermute | solution.py:340
  90.2 24.2 %collective-permute-start.35 = (f32[96]{0:T(128)S(1)}, f32[96]{0:T(128)S(1)}, u32[]{:S(2)}, u32[]{:S(2)}) collective-permute-start(f32[96]{0:T(128)S(1)} %slice_bitcast_fusion.12), channel_id=1, source_target_pairs={{0,16},{16,0},{1,17},{17,1},{2,18},{18,2},{3,19},{19,3},{4,20},{20... | collective-permute-start | bytes 1160 | tf_op jit(solution)/shard_map/ppermute | solution.py:340
  101.3 9.7 %collective-permute-start.26 = (bf16[2,96,512]{2,1,0:T(8,128)(2,1)S(1)}, bf16[2,96,512]{2,1,0:T(8,128)(2,1)S(1)}, u32[]{:S(2)}, u32[]{:S(2)}) collective-permute-start(bf16[2,96,512]{2,1,0:T(8,128)(2,1)S(1)} %get-tuple-element.88), channel_id=1, source_target_pairs={{0,17},{1,16},{16,1},{17,0},{2,19},{3,18},{18,3},{19,2},{4,21},{5,... | collective-permute-start | bytes 589832 | tf_op jit(solution)/shard_map/ppermute | solution.py:607
  103.1 9.4 %collective-permute-start.27 = (bf16[2,96,512]{2,1,0:T(8,128)(2,1)S(1)}, bf16[2,96,512]{2,1,0:T(8,128)(2,1)S(1)}, u32[]{:S(2)}, u32[]{:S(2)}) collective-permute-start(bf16[2,96,512]{2,1,0:T(8,128)(2,1)S(1)} %get-tuple-element.87), channel_id=1, source_target_pairs={{0,16},{16,0},{1,17},{17,1},{2,18},{18,2},{3,19},{19,3},{4,20},{20... | collective-permute-start | bytes 589832 | tf_op jit(solution)/shard_map/ppermute | solution.py:340
  103.9 11.4 %collective-permute-start.32 = (bf16[96,512]{1,0:T(8,128)(2,1)S(1)}, bf16[96,512]{1,0:T(8,128)(2,1)S(1)}, u32[]{:S(2)}, u32[]{:S(2)}) collective-permute-start(bf16[96,512]{1,0:T(8,128)(2,1)S(1)} %get-tuple-element.98), channel_id=1, source_target_pairs={{0,4},{2,6},{4,0},{6,2},{1,5},{3,7},{5,1},{7,3},{8,12},{10,14},{12... | collective-permute-start | bytes 294920 | tf_op jit(solution)/shard_map/ppermute | solution.py:340
  114.4 27.3 %collective-permute-start.36 = (f32[96]{0:T(128)S(1)}, f32[96]{0:T(128)S(1)}, u32[]{:S(2)}, u32[]{:S(2)}) collective-permute-start(f32[96]{0:T(128)S(1)} %bitcast_add_fusion), channel_id=1, source_target_pairs={{0,1},{1,0},{2,3},{3,2},{4,5},{5,4},{6,7},{7,6},{8,9},{9,8},{10,11... | collective-permute-start | bytes 1160 | tf_op jit(solution)/shard_map/ppermute | solution.py:340
  121.6 9.3 %collective-permute-start.47 = (bf16[1024,128]{1,0:T(8,128)(2,1)S(1)}, bf16[1024,128]{1,0:T(8,128)(2,1)S(1)}, u32[]{:S(2)}, u32[]{:S(2)}) collective-permute-start(bf16[1024,128]{1,0:T(8,128)(2,1)S(1)} %get-tuple-element.56.after_ref), channel_id=1, source_target_pairs={{0,1},{1,0},{2,3},{3,2},{4,5},{5,4},{6,7},{7,6},{8,9},{9,8},{10,11... | collective-permute-start | bytes 786440 | tf_op jit(solution)/shard_map/ppermute | solution.py:340
  124.2 12.4 %collective-permute-start.45 = (bf16[1024,128]{1,0:T(8,128)(2,1)S(1)}, bf16[1024,128]{1,0:T(8,128)(2,1)S(1)}, u32[]{:S(2)}, u32[]{:S(2)}) collective-permute-start(bf16[1024,128]{1,0:T(8,128)(2,1)S(1)} %get-tuple-element.57.after_ref), channel_id=1, source_target_pairs={{0,1},{1,0},{2,3},{3,2},{4,5},{5,4},{6,7},{7,6},{8,9},{9,8},{10,11... | collective-permute-start | bytes 786440 | tf_op jit(solution)/shard_map/ppermute | solution.py:340
  126.3 13.5 %collective-permute-start.43 = (bf16[1024,128]{1,0:T(8,128)(2,1)S(1)}, bf16[1024,128]{1,0:T(8,128)(2,1)S(1)}, u32[]{:S(2)}, u32[]{:S(2)}) collective-permute-start(bf16[1024,128]{1,0:T(8,128)(2,1)S(1)} %get-tuple-element.58.after_ref), channel_id=1, source_target_pairs={{0,1},{1,0},{2,3},{3,2},{4,5},{5,4},{6,7},{7,6},{8,9},{9,8},{10,11... | collective-permute-start | bytes 786440 | tf_op jit(solution)/shard_map/ppermute | solution.py:340
  128.8 13.5 %collective-permute-start.42 = (bf16[1024,128]{1,0:T(8,128)(2,1)S(1)}, bf16[1024,128]{1,0:T(8,128)(2,1)S(1)}, u32[]{:S(2)}, u32[]{:S(2)}) collective-permute-start(bf16[1024,128]{1,0:T(8,128)(2,1)S(1)} %get-tuple-element.60), channel_id=1, source_target_pairs={{0,1},{1,0},{2,3},{3,2},{4,5},{5,4},{6,7},{7,6},{8,9},{9,8},{10,11... | collective-permute-start | bytes 786440 | tf_op jit(solution)/shard_map/ppermute | solution.py:340
  131.0 17.2 %collective-permute-start.48 = (bf16[1024,128]{1,0:T(8,128)(2,1)S(1)}, bf16[1024,128]{1,0:T(8,128)(2,1)S(1)}, u32[]{:S(2)}, u32[]{:S(2)}) collective-permute-start(bf16[1024,128]{1,0:T(8,128)(2,1)S(1)} %add_convert_fusion), channel_id=1, source_target_pairs={{0,6},{2,4},{4,2},{6,0},{1,7},{3,5},{5,3},{7,1},{8,14},{10,12},{12... | collective-permute-start | bytes 786440 | tf_op jit(solution)/shard_map/ppermute | solution.py:340
  136.7 14.4 %collective-permute-start.46 = (bf16[1024,128]{1,0:T(8,128)(2,1)S(1)}, bf16[1024,128]{1,0:T(8,128)(2,1)S(1)}, u32[]{:S(2)}, u32[]{:S(2)}) collective-permute-start(bf16[1024,128]{1,0:T(8,128)(2,1)S(1)} %add_convert_fusion.1), channel_id=1, source_target_pairs={{0,4},{2,6},{4,0},{6,2},{1,5},{3,7},{5,1},{7,3},{8,12},{10,14},{12... | collective-permute-start | bytes 786440 | tf_op jit(solution)/shard_map/ppermute | solution.py:340
  139.8 11.3 %collective-permute-start.44 = (bf16[1024,128]{1,0:T(8,128)(2,1)S(1)}, bf16[1024,128]{1,0:T(8,128)(2,1)S(1)}, u32[]{:S(2)}, u32[]{:S(2)}) collective-permute-start(bf16[1024,128]{1,0:T(8,128)(2,1)S(1)} %add_convert_fusion.2), channel_id=1, source_target_pairs={{0,2},{2,0},{4,6},{6,4},{1,3},{3,1},{5,7},{7,5},{8,10},{10,8},{12,... | collective-permute-start | bytes 786440 | tf_op jit(solution)/shard_map/ppermute | solution.py:340
  142.3 15.3 %collective-permute-start.37 = (f32[96]{0:T(128)S(1)}, f32[96]{0:T(128)S(1)}, u32[]{:S(2)}, u32[]{:S(2)}) collective-permute-start(f32[96]{0:T(128)S(1)} %add.98), channel_id=1, source_target_pairs={{0,2},{2,0},{4,6},{6,4},{1,3},{3,1},{5,7},{7,5},{8,10},{10,8},{12,... | collective-permute-start | bytes 1160 | tf_op jit(solution)/shard_map/ppermute | solution.py:340
  146.8 10.8 %collective-permute-start.38 = (f32[96]{0:T(128)S(1)}, f32[96]{0:T(128)S(1)}, u32[]{:S(2)}, u32[]{:S(2)}) collective-permute-start(f32[96]{0:T(128)S(1)} %add.98), channel_id=1, source_target_pairs={{0,4},{2,6},{4,0},{6,2},{1,5},{3,7},{5,1},{7,3},{8,12},{10,14},{12... | collective-permute-start | bytes 1160 | tf_op jit(solution)/shard_map/ppermute | solution.py:340
  148.2 9.4 %collective-permute-start.39 = (f32[96]{0:T(128)S(1)}, f32[96]{0:T(128)S(1)}, u32[]{:S(2)}, u32[]{:S(2)}) collective-permute-start(f32[96]{0:T(128)S(1)} %add.98), channel_id=1, source_target_pairs={{0,6},{2,4},{4,2},{6,0},{1,7},{3,5},{5,3},{7,1},{8,14},{10,12},{12... | collective-permute-start | bytes 1160 | tf_op jit(solution)/shard_map/ppermute | solution.py:340
  (54 other events, 576.0 us)
